TPU v7x, 256 devices: a whole 4x4x8 slice. The times are simulated.
256 devices in a mesh: gx: 8 (over z), gy: 32 (over y, x, core).
Axes of the slice: x: 4, y: 4, z: 8, core: 2. Of those that a mesh axis runs over, the one named last changes fastest.
Arguments:
- tokens: bfloat16 [768, 16384], P(None, ('gx', 'gy')), may hold values from -24 to 24
- norm_attn: bfloat16 [16384], P(('gx', 'gy')), may hold values from 0.099609375 to 1.8984375
- w_query: bfloat16 [16384, 8192], P('gx', 'gy')
- w_key: bfloat16 [16384, 512], P('gx', 'gy')
- w_value: bfloat16 [16384, 512], P('gx', 'gy'), may hold values from -0.046875 to 0.046875
- w_out: bfloat16 [8192, 16384], P('gy', 'gx'), may hold values from -0.0625 to 0.0625
- norm_ffn: bfloat16 [16384], P(('gx', 'gy')), may hold values from 0.099609375 to 1.8984375
- w_gate: bfloat16 [16384, 26624], P('gx', 'gy'), may hold values from -0.046875 to 0.046875
- w_up: bfloat16 [16384, 26624], P('gx', 'gy'), may hold values from -0.046875 to 0.046875
- w_down: bfloat16 [26624, 16384], P('gy', 'gx'), may hold values from -0.0390625 to 0.0390625
- lengths: int32 [8], P('gx'), may hold values from 32 to 96
- segments: int32 [768], P('gx'), may hold values from 0 to 6, as said below
Outputs:
- block_out: bfloat16 [768, 16384], P(None, ('gx', 'gy'))
Inputs may be any that keep to these rules, and one draw needn't show every extreme that they name: `segments`: within each row of 96 tokens the segment ids start at 0 and never fall.
All inputs are finite; a program needn't handle non-finite values.
Results may differ from a plain program's by a relative error of at most 0.023.
Values may be sent and summed in bfloat16 or wider, within the bound.
No kernel may reach another device: no remote copies, remote signals or barrier semaphores. Data moves between devices by JAX's collectives and lax.ppermute only.
A program may use at most 128 MiB of HBM per device.

v0:
```python
import math

import jax
import jax.numpy as jnp
from jax import lax
from jax.sharding import PartitionSpec as P

D = 16384
HEADS = 64
KV_HEADS = 4
HEAD_DIM = 128
SEQ = 96


EPS = 1e-05
ROPE_BASE = 500000.0


def rotate_pairs(heads_block, positions):
    half_dim = HEAD_DIM // 2
    inv_freq = jnp.power(ROPE_BASE, -(jnp.arange(half_dim, dtype=jnp.float32) * 2.0 / HEAD_DIM))
    angles = positions.astype(jnp.float32)[:, None] * inv_freq[None, :]
    cosine = jnp.cos(angles)[:, None, :]
    sine_part = jnp.sin(angles)[:, None, :]
    first_half = heads_block[..., :half_dim]
    second_half = heads_block[..., half_dim:]
    return jnp.concatenate(
        [
            first_half * cosine - second_half * sine_part,
            second_half * cosine + first_half * sine_part,
        ],
        axis=-1,
    )


def normalize(wide, gain_row, square_total):
    inv_rms = lax.rsqrt(square_total / D + EPS)
    return (wide * inv_rms[:, None] * gain_row.astype(jnp.float32)).astype(jnp.bfloat16)


def project(row_block, gain, weight_list):
    wide = row_block.astype(jnp.float32)
    square_total = lax.psum(jnp.sum(wide * wide, axis=1), ("gx", "gy"))
    normed = normalize(wide, gain[None, :], square_total)
    block_rows = lax.all_gather(normed, "gy", axis=1, tiled=True)
    updated = []
    for index in range(len(weight_list)):
        weight_rows = weight_list[index]
        updated.append(jnp.dot(block_rows, weight_rows, preferred_element_type=jnp.float32))
    return tuple(updated)


def attend(query_sum, keys_sum, values_sum, lengths, segments):
    local_tokens = query_sum.shape[0]
    rows_here = lengths.shape[0]
    heads_here = query_sum.shape[1] // HEAD_DIM
    positions = jnp.arange(local_tokens, dtype=jnp.int32) % SEQ
    query = rotate_pairs(query_sum.reshape(local_tokens, heads_here, HEAD_DIM), positions).astype(
        jnp.bfloat16
    )
    keys = rotate_pairs(keys_sum.reshape(local_tokens, KV_HEADS, HEAD_DIM), positions).astype(
        jnp.bfloat16
    )
    values = values_sum.astype(jnp.bfloat16).reshape(local_tokens, KV_HEADS, HEAD_DIM)
    head_ids = lax.axis_index("gy") * heads_here + jnp.arange(heads_here, dtype=jnp.int32)
    kv_owner = head_ids // (HEADS // KV_HEADS)
    selector = (kv_owner[:, None] == jnp.arange(KV_HEADS, dtype=jnp.int32)[None, :]).astype(
        jnp.bfloat16
    )
    keys_sel = jnp.einsum("tgd,hg->thd", keys, selector, preferred_element_type=jnp.float32).astype(
        jnp.bfloat16
    )
    values_sel = jnp.einsum(
        "tgd,hg->thd", values, selector, preferred_element_type=jnp.float32
    ).astype(jnp.bfloat16)
    query_rows = query.reshape(rows_here, SEQ, heads_here, HEAD_DIM)
    keys_rows = keys_sel.reshape(rows_here, SEQ, heads_here, HEAD_DIM)
    values_rows = values_sel.reshape(rows_here, SEQ, heads_here, HEAD_DIM)
    scores = jnp.einsum(
        "rqhd,rkhd->rhqk", query_rows, keys_rows, preferred_element_type=jnp.float32
    ) * (1.0 / math.sqrt(HEAD_DIM))
    seg_rows = segments.reshape(rows_here, SEQ)
    place = jnp.arange(SEQ, dtype=jnp.int32)
    allowed = (
        (seg_rows[:, :, None] == seg_rows[:, None, :])
        & (place[None, None, :] <= place[None, :, None])
        & (place[None, None, :] < lengths[:, None, None])
    )
    allowed = allowed | (place[None, None, :] == place[None, :, None])
    scores = jnp.where(allowed[:, None, :, :], scores, jnp.float32(-1e30))
    row_max = jnp.max(scores, axis=-1, keepdims=True)
    expo = jnp.exp(scores - row_max)
    soft = (expo / jnp.sum(expo, axis=-1, keepdims=True)).astype(jnp.bfloat16)
    attended = jnp.einsum(
        "rhqk,rkhd->rqhd", soft, values_rows, preferred_element_type=jnp.float32
    ).astype(jnp.bfloat16)
    return attended.reshape(local_tokens, heads_here * HEAD_DIM)


def per_device(
    tokens,
    norm_attn,
    w_query,
    w_key,
    w_value,
    w_out,
    norm_ffn,
    w_gate,
    w_up,
    w_down,
    lengths,
    segments,
):
    query_part, key_part, value_part = project(tokens, norm_attn, (w_query, w_key, w_value))
    query_sum, key_sum, value_sum = (
        lax.psum_scatter(query_part, "gx", scatter_dimension=0, tiled=True),
        lax.psum_scatter(key_part, "gx", scatter_dimension=0, tiled=True),
        lax.psum_scatter(value_part, "gx", scatter_dimension=0, tiled=True),
    )
    keys_all, values_all = (
        lax.all_gather(key_sum, "gy", axis=1, tiled=True),
        lax.all_gather(value_sum, "gy", axis=1, tiled=True),
    )
    attended = attend(query_sum, keys_all, values_all, lengths, segments)
    attn_terms = jnp.dot(
        lax.all_gather(attended, "gx", axis=0, tiled=True),
        w_out,
        preferred_element_type=jnp.float32,
    )
    attn_part = lax.psum_scatter(
        attn_terms.astype(jnp.bfloat16), "gy", scatter_dimension=1, tiled=True
    ).astype(jnp.float32)
    residual = (tokens.astype(jnp.float32) + attn_part).astype(jnp.bfloat16)
    gate_part, up_part = project(residual, norm_ffn, (w_gate, w_up))
    gate_sum, up_sum = (
        lax.psum_scatter(
            gate_part.astype(jnp.bfloat16), "gx", scatter_dimension=0, tiled=True
        ).astype(jnp.float32),
        lax.psum_scatter(
            up_part.astype(jnp.bfloat16), "gx", scatter_dimension=0, tiled=True
        ).astype(jnp.float32),
    )
    hidden = (jax.nn.silu(gate_sum) * up_sum).astype(jnp.bfloat16)
    ffn_terms = jnp.dot(
        lax.all_gather(hidden, "gx", axis=0, tiled=True), w_down, preferred_element_type=jnp.float32
    )
    ffn_part = lax.psum_scatter(
        ffn_terms.astype(jnp.bfloat16), "gy", scatter_dimension=1, tiled=True
    ).astype(jnp.float32)
    return (residual.astype(jnp.float32) + ffn_part).astype(jnp.bfloat16)


def solution(mesh):
    in_specs = (
        P(None, ("gx", "gy")),
        P(("gx", "gy")),
        P("gx", "gy"),
        P("gx", "gy"),
        P("gx", "gy"),
        P("gy", "gx"),
        P(("gx", "gy")),
        P("gx", "gy"),
        P("gx", "gy"),
        P("gy", "gx"),
        P("gx"),
        P("gx"),
    )
    out_specs = P(None, ("gx", "gy"))
    return jax.shard_map(
        per_device, mesh=mesh, in_specs=in_specs, out_specs=out_specs, check_vma=False
    )
```

profile of v0, /device:TPU:1, one launch (start us, length us, event | category | flops | bytes accessed | tf_op | source)
XLA Modules:
  0.0 728.0 jit_solution(1338627607034519603)
XLA Ops:
  7.6 81.4 %psum.14 = f32[768]{0:T(1024)S(1)} all-reduce(f32[768]{0:T(1024)S(1)} %fusion.12), channel_id=1, replica_groups=mesh['gx'=8,'gy'=32] {'gx','gy'}, use_global_device_ids=true, to_apply=%region_1.0 | all-reduce | flops 768 | bytes 6144 | tf_op jit(solution)/shard_map/psum | solution.py:43
  91.4 45.8 %all-gather.4.cloned.1.call-done = bf16[768,2048]{0,1:T(8,128)(2,1)} async-done(((bf16[768,64]{0,1:T(8,128)(2,1)}), bf16[768,2048]{0,1:T(8,128)(2,1)}) %all-gather.4.cloned.1.call-update) | async-done | bytes 3145744 | tf_op jit(solution)/shard_map/all_gather | solution.py:45
  137.2 4.0 fusion.58
  141.3 4.0 fusion.57
  145.4 4.1 fusion.56
  151.7 21.0 %reduce-scatter.24.cloned.1.call-done = f32[96,16]{1,0:T(8,128)} async-done(((f32[768,16]{1,0:T(8,128)}), f32[96,16]{1,0:T(8,128)}) %reduce-scatter.24.cloned.1.call-update) | async-done | bytes 6160
  173.6 30.0 %all_gather.20 = f32[96,512]{0,1:T(8,128)S(1)} all-gather(f32[96,16]{0,1:T(8,128)S(1)} %copy.53), channel_id=1, replica_groups=mesh['gx'=8,'gy'=32] {'gy'}, dimensions={1}, use_global_device_ids=true | all-gather | bytes 202752 | tf_op jit(solution)/shard_map/all_gather | solution.py:121
  206.7 4.4 reduce-scatter.22.cloned.1.call-done
  211.9 29.8 %all_gather.19 = bf16[96,512]{0,1:T(8,128)(2,1)S(1)} all-gather(bf16[96,16]{0,1:T(8,128)(2,1)S(1)} %copy.51), channel_id=1, replica_groups=mesh['gx'=8,'gy'=32] {'gy'}, dimensions={1}, use_global_device_ids=true | all-gather | bytes 101376 | tf_op jit(solution)/shard_map/all_gather | solution.py:122
  247.4 2.5 reduce-scatter.12.cloned.1.call-done
  252.0 1.7 fusion.51
  254.9 18.7 %all_gather.21 = bf16[768,256]{1,0:T(8,128)(2,1)S(1)} all-gather(bf16[96,256]{1,0:T(8,128)(2,1)S(1)} %bitcast.39), channel_id=1, replica_groups=mesh['gx'=8,'gy'=32] {'gx'}, dimensions={0}, use_global_device_ids=true | all-gather | bytes 442368 | tf_op jit(solution)/shard_map/all_gather | solution.py:126
  273.5 3.9 convolution_convert_fusion.1
  277.6 96.3 %reduce-scatter.14.cloned.1.call-done = bf16[768,64]{0,1:T(8,128)(2,1)} async-done(((bf16[768,2048]{0,1:T(8,128)(2,1)}), bf16[768,64]{0,1:T(8,128)(2,1)}) %reduce-scatter.14.cloned.1.call-update) | async-done | bytes 98320 | tf_op jit(solution)/shard_map/reduce_scatter | solution.py:130
  374.8 77.2 %psum.15 = f32[768]{0:T(1024)S(1)} all-reduce(f32[768]{0:T(1024)S(1)} %fusion.16), channel_id=1, replica_groups=mesh['gx'=8,'gy'=32] {'gx','gy'}, use_global_device_ids=true, to_apply=%region_9.10 | all-reduce | flops 768 | bytes 6144 | tf_op jit(solution)/shard_map/psum | solution.py:43
  453.9 46.9 %all-gather.6.cloned.1.call-done = bf16[768,2048]{0,1:T(8,128)(2,1)} async-done(((bf16[768,64]{0,1:T(8,128)(2,1)}), bf16[768,2048]{0,1:T(8,128)(2,1)}) %all-gather.6.cloned.1.call-update) | async-done | bytes 3145744 | tf_op jit(solution)/shard_map/all_gather | solution.py:45
  500.9 7.5 %convolution_convert_fusion.3 = bf16[768,832]{1,0:T(8,128)(2,1)} fusion(bf16[768,2048]{0,1:T(8,128)(2,1)} %all-gather.6.cloned.1.call-done, bf16[2048,832]{0,1:T(8,128)(2,1)} %param.19), kind=kOutput, calls=%fused_computation.4 | convolution fusion | flops 2617884672 | bytes 7831552 | tf_op jit(solution)/shard_map/dot_general | solution.py:49
  508.4 7.5 %convolution_convert_fusion.2 = bf16[768,832]{1,0:T(8,128)(2,1)} fusion(bf16[768,2048]{0,1:T(8,128)(2,1)} %all-gather.6.cloned.1.call-done, bf16[2048,832]{0,1:T(8,128)(2,1)} %param.20), kind=kOutput, calls=%fused_computation.3 | convolution fusion | flops 2617884672 | bytes 7831552 | tf_op jit(solution)/shard_map/dot_general | solution.py:49
  516.0 27.2 %reduce-scatter.16.cloned.1.call-done = bf16[96,832]{1,0:T(8,128)(2,1)} async-done(((bf16[768,832]{1,0:T(8,128)(2,1)}), bf16[96,832]{1,0:T(8,128)(2,1)}) %reduce-scatter.16.cloned.1.call-update) | async-done | bytes 159760 | tf_op jit(solution)/shard_map/reduce_scatter | solution.py:136
  543.2 40.9 %reduce-scatter.18.cloned.1.call-done = bf16[96,832]{1,0:T(8,128)(2,1)} async-done(((bf16[768,832]{1,0:T(8,128)(2,1)}), bf16[96,832]{1,0:T(8,128)(2,1)}) %reduce-scatter.18.cloned.1.call-update) | async-done | bytes 159760 | tf_op jit(solution)/shard_map/reduce_scatter | solution.py:139
  584.1 1.8 fusion.11
  586.0 38.1 %all-gather.8.cloned.1.call-done = bf16[768,832]{1,0:T(8,128)(2,1)} async-done(((bf16[96,832]{1,0:T(8,128)(2,1)}), bf16[768,832]{1,0:T(8,128)(2,1)}) %all-gather.8.cloned.1.call-update) | async-done | bytes 1277968 | tf_op jit(solution)/shard_map/all_gather | solution.py:145
  624.1 6.2 convolution_convert_fusion
  630.3 89.2 %reduce-scatter.20.cloned.1.call-done = bf16[768,64]{0,1:T(8,128)(2,1)} async-done(((bf16[768,2048]{0,1:T(8,128)(2,1)}), bf16[768,64]{0,1:T(8,128)(2,1)}) %reduce-scatter.20.cloned.1.call-update) | async-done | bytes 98320 | tf_op jit(solution)/shard_map/reduce_scatter | solution.py:147
  (61 shorter events, 23.6 us)
Async XLA Ops:
  6.5 617.6 %copy-start = (bf16[832,2048]{1,0:T(8,128)(2,1)S(1)}, bf16[832,2048]{1,0:T(8,128)(2,1)}, u32[]{:S(2)}) copy-start(bf16[832,2048]{1,0:T(8,128)(2,1)} %param.21) | copy-start | bytes 10223620
  6.5 134.8 %copy-start.2 = (bf16[2048,16]{0,1:T(8,128)(2,1)S(1)}, bf16[2048,16]{0,1:T(8,128)(2,1)}, u32[]{:S(2)}) copy-start(bf16[2048,16]{0,1:T(8,128)(2,1)} %param.16) | copy-start | bytes 196612
  6.5 130.7 %all-gather.4.cloned.1.call-start = ((), (), s32[]{:S(2)}) async-start(), calls=%async_computation.7 | async-start | bytes 3244032 | tf_op jit(solution)/shard_map/all_gather | solution.py:45
  91.4 81.3 %reduce-scatter.24.cloned.1.call-start = ((), (), s32[]{:S(2)}) async-start(), calls=%async_computation.16 | async-start | bytes 442368
  141.2 69.8 %reduce-scatter.22.cloned.1.call-start = ((), (), s32[]{:S(2)}) async-start(), calls=%async_computation.15 | async-start | bytes 442368
  145.3 5.4 copy-start.3
  145.3 104.7 %reduce-scatter.12.cloned.1.call-start = ((), (), s32[]{:S(2)}) async-start(), calls=%async_computation.8 | async-start | bytes 884736 | tf_op jit(solution)/shard_map/reduce_scatter | solution.py:116
  149.4 224.4 %reduce-scatter.14.cloned.1.call-start = ((), (), s32[]{:S(2)}) async-start(), calls=%async_computation.9 | async-start | bytes 3244032 | tf_op jit(solution)/shard_map/reduce_scatter | solution.py:130
  273.5 4.0 copy-start.4
  273.5 100.4 %copy-start.1 = (bf16[768,64]{0,1:T(8,128)(2,1)S(1)}, bf16[768,64]{0,1:T(8,128)(2,1)}, u32[]{:S(2)}) copy-start(bf16[768,64]{0,1:T(8,128)(2,1)} %param.12) | copy-start | bytes 294916
  277.5 223.4 %all-gather.6.cloned.1.call-start = ((), (), s32[]{:S(2)}) async-start(), calls=%async_computation.10 | async-start | bytes 3244032 | tf_op jit(solution)/shard_map/all_gather | solution.py:45
  453.7 89.5 %reduce-scatter.16.cloned.1.call-start = ((), (), s32[]{:S(2)}) async-start(), calls=%async_computation.11 | async-start | bytes 1548288 | tf_op jit(solution)/shard_map/reduce_scatter | solution.py:136
  508.4 75.8 %reduce-scatter.18.cloned.1.call-start = ((), (), s32[]{:S(2)}) async-start(), calls=%async_computation.12 | async-start | bytes 1548288 | tf_op jit(solution)/shard_map/reduce_scatter | solution.py:139
  515.9 108.2 %all-gather.8.cloned.1.call-start = ((), (), s32[]{:S(2)}) async-start(), calls=%async_computation.13 | async-start | bytes 1548288 | tf_op jit(solution)/shard_map/all_gather | solution.py:145
  585.9 133.6 %reduce-scatter.20.cloned.1.call-start = ((), (), s32[]{:S(2)}) async-start(), calls=%async_computation.14 | async-start | bytes 3244032 | tf_op jit(solution)/shard_map/reduce_scatter | solution.py:147
Sparse Core Ops, SparseCore 0:
  91.5 45.6 all-gather.3
  141.4 31.2 reduce-scatter.23
  175.4 35.6 reduce-scatter.21
  213.5 36.4 reduce-scatter.11
  277.6 96.2 reduce-scatter.13
  453.8 47.0 all-gather.5
  508.5 34.6 reduce-scatter.15
  545.9 38.1 reduce-scatter.17
  586.0 38.0 all-gather.7
  630.5 89.0 reduce-scatter.19
where the time goes:
time: 729 us; the launch traced here: 728 us
  waiting for transfers between devices  413 us (57%)
  blocking collectives  237 us (33%)
  matrix products  42.9 us (6%)
  between operations  14.3 us (2%)
  other arithmetic  12.8 us (2%)
  local copies, waits for them, and re-layouts  7.72 us (1%)
    psum x2, blocking collectives, project(): square_total = lax.psum(jnp.sum(wide * wide, axis=1), ('gx', 'gy'))  159 us
    reduce_scatter x1, waiting for transfers between devices, per_device(): lax.psum_scatter(attn_terms.astype(jnp.bfloat16), 'gy', scatter_dimension...  96.3 us
    all_gather x2, waiting for transfers between devices, project(): block_rows = lax.all_gather(normed, 'gy', axis=1, tiled=True)  92.7 us
    reduce_scatter x1, waiting for transfers between devices, per_device(): lax.psum_scatter(ffn_terms.astype(jnp.bfloat16), 'gy', scatter_dimension=...  89.2 us
    reduce_scatter x1, waiting for transfers between devices, per_device(): lax.psum_scatter(up_part.astype(jnp.bfloat16), 'gx', scatter_dimension=0,...  40.9 us
    all_gather x1, waiting for transfers between devices, per_device(): lax.all_gather(hidden, 'gx', axis=0, tiled=True)  38.1 us
    all_gather x1, blocking collectives, per_device(): lax.all_gather(key_sum, 'gy', axis=1, tiled=True)  30 us
    all_gather x1, blocking collectives, per_device(): lax.all_gather(value_sum, 'gy', axis=1, tiled=True)  29.8 us
  transfers between devices with their start and end apart: 10, of which 10 were waited for; matrix products, arithmetic and copies ran while one was open for 4% of the time, Pallas kernels for 0%

commit v1 on v0

v1 whole, which is shorter than its diff:
```python
import math

import jax
import jax.numpy as jnp
import numpy as np
from jax import lax
from jax.experimental import pallas as pl
from jax.experimental.pallas import tpu as pltpu
from jax.sharding import PartitionSpec as P

D = 16384
HEADS = 64
KV_HEADS = 4
HEAD_DIM = 128
SEQ = 96
EPS = 1e-05
ROPE_BASE = 500000.0

BF = jnp.bfloat16
F32 = jnp.float32

TOK = 768
HALF = 384
CHIPS = 16
LANE = 128
ROWS = 8
KSTEP = 4
FFL = 832
MAIN = 640
REST = FFL - MAIN
SIDE = 512
UP_AT = 256
CHIP_GROUPS = [[2 * i + c for i in range(CHIPS)] for c in range(2)]
KV_GROUPS = [list(range(8 * i, 8 * i + 8)) for i in range(4)]
VMEM = 48 * 1024 * 1024


def swap(x):
    return lax.ppermute(x, "gy", [(i, i ^ 1) for i in range(32)])


def over_chips(x):
    return lax.all_to_all(x, "gy", 0, 0, axis_index_groups=CHIP_GROUPS, tiled=True)


def over_rows(x):
    return lax.all_to_all(x, "gx", 0, 0, tiled=True)


def params(**kw):
    return pltpu.CompilerParams(vmem_limit_bytes=VMEM, **kw)


def nt(a, b):
    return lax.dot_general(a, b, (((1,), (1,)), ((), ())), preferred_element_type=F32)


def nn(a, b):
    return jnp.dot(a, b, preferred_element_type=F32)


def fold_squares(wide):
    total = None
    for j in range(wide.shape[1] // LANE):
        part = wide[:, j * LANE : (j + 1) * LANE]
        total = part * part if total is None else total + part * part
    return total


def split_two(total):
    high = total.astype(BF).astype(F32)
    return high, total - high


def qkv_kernel(h_ref, x_ref, g_ref, wq_ref, wk_ref, wv_ref, *rest):
    out_ref, acc_q, acc_kv, acc_sq = rest[-4:]
    k = pl.program_id(0)

    @pl.when(k == 0)
    def _():
        acc_q[...] = jnp.zeros_like(acc_q)
        acc_kv[...] = jnp.zeros_like(acc_kv)
        acc_sq[...] = jnp.zeros_like(acc_sq)

    wide = jnp.concatenate([x_ref[j] for j in range(x_ref.shape[0])], axis=1).astype(F32)
    acc_sq[...] += fold_squares(wide)
    gained = (wide * g_ref[...]).astype(BF)
    acc_q[...] += nn(gained, wq_ref[...])
    depth = gained.shape[1]
    kv = jnp.concatenate([wk_ref[...], wv_ref[...], jnp.zeros((LANE - 32, depth), BF)], axis=0)
    acc_kv[...] += nt(gained, kv)

    @pl.when(k == pl.num_programs(0) - 1)
    def _():
        high, low = split_two(jnp.sum(acc_sq[...], axis=1, keepdims=True))
        lane = lax.broadcasted_iota(jnp.int32, (HALF, LANE), 1)
        tail = jnp.where(lane == 32, high, jnp.where(lane == 33, low, acc_kv[...]))
        out_ref[:, :256] = acc_q[...].astype(BF)
        out_ref[:, 256:] = tail.astype(BF)


def qkv_half(h, x, gain, wq, wk_t, wv_t, held=None):
    depth = 2048 // KSTEP
    in_specs = [
        pl.BlockSpec((CHIPS // KSTEP, HALF, LANE), lambda k, h: (k, 0, 0)),
        pl.BlockSpec((1, depth), lambda k, h: (0, k)),
        pl.BlockSpec((depth, 256), lambda k, h: (k, 0)),
        pl.BlockSpec((16, depth), lambda k, h: (0, k)),
        pl.BlockSpec((16, depth), lambda k, h: (0, k)),
    ]
    operands = [h, x, gain, wq, wk_t, wv_t]
    aliases = {}
    if held is not None:
        in_specs.append(pl.BlockSpec(memory_space=pl.ANY))
        operands.append(held)
        aliases = {6: 0}
    return pl.pallas_call(
        qkv_kernel,
        grid_spec=pltpu.PrefetchScalarGridSpec(
            num_scalar_prefetch=1,
            grid=(KSTEP,),
            in_specs=in_specs,
            out_specs=pl.BlockSpec((HALF, 384), lambda k, h: (h[0], 0)),
            scratch_shapes=[
                pltpu.VMEM((HALF, 256), F32),
                pltpu.VMEM((HALF, LANE), F32),
                pltpu.VMEM((HALF, LANE), F32),
            ],
        ),
        out_shape=jax.ShapeDtypeStruct((TOK, 384), BF),
        input_output_aliases=aliases,
        compiler_params=params(),
        cost_estimate=pl.CostEstimate(
            flops=2 * HALF * 2048 * 384, bytes_accessed=4 * 1024 * 1024, transcendentals=0
        ),
        name="qkv_half",
    )(*operands)


def qkv_sum_kernel(p_ref, q_ref, kv_ref):
    total = p_ref[0].astype(F32)
    for j in range(1, ROWS):
        total = total + p_ref[j].astype(F32)
    tail = total[:, 256:]
    squares = tail[:, 32:33] + tail[:, 33:34]
    inv = lax.rsqrt(squares / D + EPS)
    q_ref[...] = total[:, :256] * inv
    kv = tail[:, :32] * inv
    for j in range(8):
        kv_ref[j] = kv


def qkv_sum(parts):
    return pl.pallas_call(
        qkv_sum_kernel,
        out_shape=(
            jax.ShapeDtypeStruct((SEQ, 256), F32),
            jax.ShapeDtypeStruct((8, SEQ, 32), F32),
        ),
        compiler_params=params(),
        name="qkv_sum",
    )(parts)


def attend_kernel(len_ref, q_ref, kv_ref, segr_ref, segc_ref, cos_ref, sin_ref, out_ref):
    def rotate(x):
        return (x * cos_ref[...] + pltpu.roll(x, 64, 1) * sin_ref[...]).astype(BF)

    keys = rotate(jnp.concatenate([kv_ref[j][:, :16] for j in range(8)], axis=1))
    values = jnp.concatenate([kv_ref[j][:, 16:32] for j in range(8)], axis=1).astype(BF)
    q_at = lax.broadcasted_iota(jnp.int32, (SEQ, SEQ), 0)
    k_at = lax.broadcasted_iota(jnp.int32, (SEQ, SEQ), 1)
    allowed = (segr_ref[...] == segc_ref[...]) & (k_at <= q_at) & (k_at < len_ref[0])
    allowed = allowed | (k_at == q_at)
    for head in range(2):
        query = rotate(q_ref[:, head * HEAD_DIM : (head + 1) * HEAD_DIM])
        scores = nt(query, keys) * (1.0 / math.sqrt(HEAD_DIM))
        scores = jnp.where(allowed, scores, F32(-1e30))
        expo = jnp.exp(scores - jnp.max(scores, axis=1, keepdims=True))
        soft = (expo / jnp.sum(expo, axis=1, keepdims=True)).astype(BF)
        attended = nn(soft, values).astype(BF)
        for j in range(ROWS):
            out_ref[j, :, head * HEAD_DIM : (head + 1) * HEAD_DIM] = attended


def attend(lengths, q, kv, segments, cos, sin):
    vmem = pl.BlockSpec(memory_space=pltpu.VMEM)
    return pl.pallas_call(
        attend_kernel,
        in_specs=[pl.BlockSpec(memory_space=pltpu.SMEM)] + [vmem] * 6,
        out_specs=vmem,
        out_shape=jax.ShapeDtypeStruct((ROWS, SEQ, 256), BF),
        compiler_params=params(),
        name="attend",
    )(lengths, q, kv, segments.reshape(1, SEQ), segments.reshape(SEQ, 1), cos, sin)


def proj_kernel(h_ref, x_ref, w_ref, out_ref):
    result = nn(x_ref[...], w_ref[...]).astype(out_ref.dtype)
    for j in range(out_ref.shape[0]):
        out_ref[j] = result[:, j * LANE : (j + 1) * LANE]


def proj_half(h, x, w, dtype):
    depth = x.shape[1]
    steps = 4
    wide = 2048 // steps
    return pl.pallas_call(
        proj_kernel,
        grid_spec=pltpu.PrefetchScalarGridSpec(
            num_scalar_prefetch=1,
            grid=(steps,),
            in_specs=[
                pl.BlockSpec((HALF, depth), lambda i, h: (h[0], 0)),
                pl.BlockSpec((depth, wide), lambda i, h: (0, i)),
            ],
            out_specs=pl.BlockSpec((wide // LANE, HALF, LANE), lambda i, h: (i, 0, 0)),
        ),
        out_shape=jax.ShapeDtypeStruct((CHIPS, HALF, LANE), dtype),
        compiler_params=params(),
        cost_estimate=pl.CostEstimate(
            flops=2 * HALF * 2048 * depth, bytes_accessed=4 * 1024 * 1024, transcendentals=0
        ),
        name="proj_half",
    )(h, x, w)


def project_out(c, x, w):
    given = proj_half(1 - c, x, w, BF)
    got = swap(given)
    kept = proj_half(c, x, w, F32)
    return over_chips((kept + got.astype(F32)).astype(BF))


def residual_kernel(base_ref, p_ref, out_ref, copies_ref):
    total = p_ref[0].astype(F32)
    for j in range(1, CHIPS):
        total = total + p_ref[j].astype(F32)
    result = (base_ref[...].astype(F32) + total).astype(BF)
    out_ref[...] = result
    for j in range(CHIPS):
        copies_ref[j] = result


def residual_copies(base, parts):
    return pl.pallas_call(
        residual_kernel,
        out_shape=(
            jax.ShapeDtypeStruct((HALF, LANE), BF),
            jax.ShapeDtypeStruct((CHIPS, HALF, LANE), BF),
        ),
        compiler_params=params(),
        name="residual_copies",
    )(base, parts)


def final_kernel(base_ref, p_ref, out_ref):
    total = p_ref[0].astype(F32)
    for j in range(1, CHIPS):
        total = total + p_ref[j].astype(F32)
    out_ref[...] = (base_ref[...].astype(F32) + total).astype(BF)


def final_sum(base, parts):
    return pl.pallas_call(
        final_kernel,
        out_shape=jax.ShapeDtypeStruct((HALF, LANE), BF),
        compiler_params=params(),
        name="final_sum",
    )(base, parts)


def gate_up_kernel(h_ref, x_ref, g_ref, wg_ref, wu_ref, *rest):
    main_ref, side_ref, acc_g, acc_u, acc_sq = rest[-5:]
    k = pl.program_id(0)

    @pl.when(k == 0)
    def _():
        acc_g[...] = jnp.zeros_like(acc_g)
        acc_u[...] = jnp.zeros_like(acc_u)
        acc_sq[...] = jnp.zeros_like(acc_sq)

    wide = jnp.concatenate([x_ref[j] for j in range(x_ref.shape[0])], axis=1).astype(F32)
    acc_sq[...] += fold_squares(wide)
    gained = (wide * g_ref[...]).astype(BF)
    acc_g[...] += nt(gained, wg_ref[...])
    acc_u[...] += nt(gained, wu_ref[...])

    @pl.when(k == pl.num_programs(0) - 1)
    def _():
        high, low = split_two(jnp.sum(acc_sq[...], axis=1, keepdims=True))
        main_ref[:, :MAIN] = acc_g[:, :MAIN].astype(BF)
        main_ref[:, MAIN:] = acc_u[:, :MAIN].astype(BF)
        lane = lax.broadcasted_iota(jnp.int32, (HALF, 64), 1)
        extra = jnp.where(lane == 0, high, jnp.where(lane == 1, low, 0.0))
        side_ref[:, :UP_AT] = jnp.concatenate([acc_g[:, MAIN:], extra], axis=1).astype(BF)
        side_ref[:, UP_AT:] = jnp.concatenate(
            [acc_u[:, MAIN:], jnp.zeros((HALF, 64), F32)], axis=1
        ).astype(BF)


def gate_up_half(h, x, gain, wg_t, wu_t, held=None):
    depth = 2048 // KSTEP
    in_specs = [
        pl.BlockSpec((CHIPS // KSTEP, HALF, LANE), lambda k, h: (k, 0, 0)),
        pl.BlockSpec((1, depth), lambda k, h: (0, k)),
        pl.BlockSpec((FFL, depth), lambda k, h: (0, k)),
        pl.BlockSpec((FFL, depth), lambda k, h: (0, k)),
    ]
    operands = [h, x, gain, wg_t, wu_t]
    aliases = {}
    if held is not None:
        in_specs += [pl.BlockSpec(memory_space=pl.ANY)] * 2
        operands += list(held)
        aliases = {5: 0, 6: 1}
    return pl.pallas_call(
        gate_up_kernel,
        grid_spec=pltpu.PrefetchScalarGridSpec(
            num_scalar_prefetch=1,
            grid=(KSTEP,),
            in_specs=in_specs,
            out_specs=[
                pl.BlockSpec((HALF, 2 * MAIN), lambda k, h: (h[0], 0)),
                pl.BlockSpec((HALF, SIDE), lambda k, h: (h[0], 0)),
            ],
            scratch_shapes=[
                pltpu.VMEM((HALF, FFL), F32),
                pltpu.VMEM((HALF, FFL), F32),
                pltpu.VMEM((HALF, LANE), F32),
            ],
        ),
        out_shape=(
            jax.ShapeDtypeStruct((TOK, 2 * MAIN), BF),
            jax.ShapeDtypeStruct((TOK, SIDE), BF),
        ),
        input_output_aliases=aliases,
        compiler_params=params(),
        cost_estimate=pl.CostEstimate(
            flops=2 * HALF * 2048 * 2 * FFL, bytes_accessed=10 * 1024 * 1024, transcendentals=0
        ),
        name="gate_up_half",
    )(*operands)


def hidden_kernel(main_ref, side_ref, out_ref):
    side = side_ref[0].astype(F32)
    for j in range(1, ROWS):
        side = side + side_ref[j].astype(F32)
    squares = side[:, REST : REST + 1] + side[:, REST + 1 : REST + 2]
    inv = lax.rsqrt(squares / D + EPS)

    def gated(gate, up):
        gate, up = gate * inv, up * inv
        return (gate / (1.0 + jnp.exp(-gate)) * up).astype(BF)

    first = gated(main_ref[:, :MAIN].astype(F32), main_ref[:, MAIN:].astype(F32))
    second = gated(side[:, :REST], side[:, UP_AT : UP_AT + REST])
    for j in range(ROWS):
        out_ref[j, :, :MAIN] = first
        out_ref[j, :, MAIN:] = second


def hidden_copies(main, side):
    return pl.pallas_call(
        hidden_kernel,
        out_shape=jax.ShapeDtypeStruct((ROWS, SEQ, FFL), BF),
        compiler_params=params(),
        name="hidden_copies",
    )(main, side)


def rope_tables():
    inv_freq = np.power(
        np.float32(ROPE_BASE), -(np.arange(64, dtype=np.float32) * np.float32(2.0 / HEAD_DIM))
    ).astype(np.float32)
    angles = np.arange(SEQ, dtype=np.float32)[:, None] * inv_freq[None, :]
    cos, sin = np.cos(angles.astype(np.float64)), np.sin(angles.astype(np.float64))
    return (
        np.concatenate([cos, cos], axis=1).astype(np.float32),
        np.concatenate([-sin, sin], axis=1).astype(np.float32),
    )


def per_device(
    tokens,
    norm_attn,
    w_query,
    w_key,
    w_value,
    w_out,
    norm_ffn,
    w_gate,
    w_up,
    w_down,
    lengths,
    segments,
):
    core = lax.axis_index("gy") % 2
    c = jnp.reshape(core, (1,)).astype(jnp.int32)
    gains = lax.all_gather(jnp.stack([norm_attn, norm_ffn]), "gy", axis=1, tiled=True).astype(F32)
    gain_a, gain_f = gains[0:1], gains[1:2]
    cos, sin = rope_tables()

    mine = lax.dynamic_slice_in_dim(tokens, core * HALF, HALF, 0)
    theirs = swap(lax.dynamic_slice_in_dim(tokens, (1 - core) * HALF, HALF, 0))
    base = jnp.where(
        core == 0,
        jnp.concatenate([mine, theirs], axis=1),
        jnp.concatenate([theirs, mine], axis=1),
    )

    own = over_chips(jnp.broadcast_to(base[None], (CHIPS, HALF, LANE)))
    other = swap(own)
    held = qkv_half(c, own, gain_a, w_query, w_key.T, w_value.T)
    parts = qkv_half(1 - c, other, gain_a, w_query, w_key.T, w_value.T, held)
    q, kv = qkv_sum(over_rows(parts.reshape(ROWS, SEQ, 384)))
    kv = lax.all_to_all(kv, "gy", 0, 0, axis_index_groups=KV_GROUPS, tiled=True)
    attended = attend(lengths, q, kv, segments, cos, sin)
    attended = over_rows(attended).reshape(TOK, 256)
    residual, copies = residual_copies(base, project_out(c, attended, w_out))

    own = over_chips(copies)
    other = swap(own)
    held = gate_up_half(c, own, gain_f, w_gate.T, w_up.T)
    main, side = gate_up_half(1 - c, other, gain_f, w_gate.T, w_up.T, held)
    main = lax.psum_scatter(main, "gx", scatter_dimension=0, tiled=True)
    side = over_rows(side.reshape(ROWS, SEQ, SIDE))
    hidden = over_rows(hidden_copies(main, side)).reshape(TOK, FFL)
    done = final_sum(residual, project_out(c, hidden, w_down))

    keep = lax.dynamic_slice_in_dim(done, core * 64, 64, 1)
    got = swap(lax.dynamic_slice_in_dim(done, (1 - core) * 64, 64, 1))
    return jnp.where(
        core == 0,
        jnp.concatenate([keep, got], axis=0),
        jnp.concatenate([got, keep], axis=0),
    )


def solution(mesh):
    in_specs = (
        P(None, ("gx", "gy")),
        P(("gx", "gy")),
        P("gx", "gy"),
        P("gx", "gy"),
        P("gx", "gy"),
        P("gy", "gx"),
        P(("gx", "gy")),
        P("gx", "gy"),
        P("gx", "gy"),
        P("gy", "gx"),
        P("gx"),
        P("gx"),
    )
    out_specs = P(None, ("gx", "gy"))
    return jax.shard_map(
        per_device, mesh=mesh, in_specs=in_specs, out_specs=out_specs, check_vma=False
    )
```

time: 729 us -> 334 us (0.46)
  waiting for transfers between devices: 413 us -> 45.4 us
  matrix products: 42.9 us -> 0 us
  Pallas kernels: 0 us -> 32.6 us
  blocking collectives: 237 us -> 212 us
  starting transfers between devices: 0.56 us -> 22.8 us
  other arithmetic: 12.8 us -> 2.18 us
    reduce_scatter x5 -> x1, waiting for transfers between devices: 256 us -> 10.5 us  [per_device(): main = lax.psum_scatter(main, 'gx', scatter_dimension=0, tiled=True)]
    all_to_all x0 -> x7, blocking collectives: none -> 192 us  [the longest x4 115 us: over_rows(): return lax.all_to_all(x, 'gx', 0, 0, tiled=True)]
    psum x2 -> x0, blocking collectives: 159 us -> none  [project(): square_total = lax.psum(jnp.sum(wide * wide, axis=1), ('gx', 'gy'))]
    all_gather x3 -> x0, waiting for transfers between devices: 131 us -> none  [the longest x2 92.7 us: project(): block_rows = lax.all_gather(normed, 'gy', axis=1, tiled=True)]
    all_gather x3 -> x1, blocking collectives: 78.4 us -> 19.4 us  [per_device(): lax.all_gather(jnp.stack([norm_attn, norm_ffn]), 'gy', axis=1, tiled=True)]
    dot_general x8 -> x0, matrix products: 33.2 us -> none  [the longest x3 19 us: project(): jnp.dot(block_rows, weight_rows, preferred_element_type=jnp.float32)]
    pallas_call x0 -> x13, Pallas kernels: none -> 32.6 us  [the longest x2 15 us: gate_up_half(): pl.pallas_call(gate_up_kernel, grid_spec=pltpu.PrefetchScalarGridSpec(num...]
    all_to_all x0 -> x2, waiting for transfers between devices: none -> 31.2 us  [the longest x1 26.7 us: over_chips(): lax.all_to_all(x, 'gy', 0, 0, axis_index_groups=CHIP_GROUPS, tiled=True)]
  transfers between devices with their start and end apart: 10 -> 9, of which waited for: 10 -> 6; matrix products, arithmetic and copies ran while one was open for 4% -> 0% of each run, Pallas kernels for 0% -> 4%
where the time goes in v1:
time: 334 us; the launch traced here: 333 us
  blocking collectives  212 us (63%)
  waiting for transfers between devices  45.4 us (14%)
  Pallas kernels  32.6 us (10%)
  starting transfers between devices  22.8 us (7%)
  between operations  14.3 us (4%)
  local copies, waits for them, and re-layouts  4.45 us (1%)
    all_to_all x4, blocking collectives, over_rows(): return lax.all_to_all(x, 'gx', 0, 0, tiled=True)  115 us
    all_to_all x3, blocking collectives, over_chips(): lax.all_to_all(x, 'gy', 0, 0, axis_index_groups=CHIP_GROUPS, tiled=True)  77.4 us
    all_to_all x1, waiting for transfers between devices, over_chips(): lax.all_to_all(x, 'gy', 0, 0, axis_index_groups=CHIP_GROUPS, tiled=True)  26.7 us
    all_gather x1, blocking collectives, per_device(): lax.all_gather(jnp.stack([norm_attn, norm_ffn]), 'gy', axis=1, tiled=True)  19.4 us
    pallas_call x2, Pallas kernels, gate_up_half(): pl.pallas_call(gate_up_kernel, grid_spec=pltpu.PrefetchScalarGridSpec(num...  15 us
    ppermute x6, starting transfers between devices, swap(): return lax.ppermute(x, 'gy', [(i, i ^ 1) for i in range(32)])  14.7 us
    pallas_call x4, Pallas kernels, proj_half(): pl.pallas_call(proj_kernel, grid_spec=pltpu.PrefetchScalarGridSpec(num_sc...  10.6 us
    reduce_scatter x1, waiting for transfers between devices, per_device(): main = lax.psum_scatter(main, 'gx', scatter_dimension=0, tiled=True)  10.5 us
  transfers between devices with their start and end apart: 9, of which 6 were waited for; matrix products, arithmetic and copies ran while one was open for 0% of the time, Pallas kernels for 4%

profile of v1, /device:TPU:1, one launch (start us, length us, event | category | flops | bytes accessed | tf_op | source)
XLA Modules:
  0.0 333.3 jit_solution(10587015608988202429)
XLA Ops:
  7.5 3.3 collective-permute-start
  12.3 26.9 %all_to_all.45.x_ref = bf16[16,384,128]{2,1,0:T(8,128)(2,1)S(1)} all-to-all(bf16[16,384,128]{2,1,0:T(8,128)(2,1)S(1)} %broadcast_in_dim.2), channel_id=1, replica_groups={{0,2,4,6,8,10,12,14,16,18,20,22,24,26,28,30},{1,3,5,7,9,11,13,15,17,19,..., dimensions={0} | all-to-all | bytes 3145728 | tf_op jit(solution)/shard_map/all_to_all | solution.py:43
  39.2 1.8 collective-permute-start.1
  41.0 19.4 %all-gather = bf16[32,64,2]{1,2,0:T(2,128)(2,1)S(1)} all-gather(bf16[1,64,2]{1,2,0:T(2,128)(2,1)S(1)} %maximum_bitcast_fusion), channel_id=1, replica_groups=mesh['gx'=8,'gy'=32] {'gy'}, dimensions={0}, use_global_device_ids=true | all-gather | bytes 8448 | tf_op jit(solution)/shard_map/all_gather | solution.py:400
  62.3 3.3 %qkv_half.3 = bf16[768,384]{1,0:T(8,128)(2,1)S(1)} custom-call(s32[1]{0:T(128)S(6)} %sub.5.h_ref, bf16[16,384,128]{2,1,0:T(8,128)(2,1)} %collective-permute-done.1.x_ref, f32[1,2048]{1,0:T(1,128)S(1)} %get-tuple-element.26.g_ref, bf16[2048,256]{1,0:T(8,128)(2,1)S(1)} %copy-done.1, bf16[16,2048]{1,0:T(8,128)(2,1)S(1)} %bitcast.27, ...), custom_call_target="tpu_custom_call", output_to_operand_aliasing={{}: (6, {})} | custom-call | flops 603979776 | bytes 4194304 | tf_op jit(solution)/shard_map/qkv_half/pallas_call | solution.py:117
  65.7 26.8 %all_to_all.46.p_ref = bf16[8,96,384]{2,1,0:T(8,128)(2,1)S(1)} all-to-all(bf16[8,96,384]{2,1,0:T(8,128)(2,1)S(1)} %bitcast.22), channel_id=1, replica_groups=mesh['gx'=8,'gy'=32] {'gx'}, dimensions={0} | all-to-all | bytes 1179648 | tf_op jit(solution)/shard_map/all_to_all | solution.py:47
  93.5 4.4 %all-to-all-start.2 = ((f32[8,96,32]{1,2,0:T(8,128)}), f32[8,96,32]{1,2,0:T(8,128)S(1)}, u32[]{:S(2)}, u32[]{:S(2)}) async-start(f32[8,96,32]{1,2,0:T(8,128)} %copy.33), calls=%async_computation.2 | async-start | bytes 262144 | tf_op jit(solution)/shard_map/all_to_all | solution.py:417
  98.7 4.5 %all-to-all-done.2 = f32[8,96,32]{1,2,0:T(8,128)S(1)} async-done(((f32[8,96,32]{1,2,0:T(8,128)}), f32[8,96,32]{1,2,0:T(8,128)S(1)}, u32[]{:S(2)}, u32[]{:S(2)}) %all-to-all-start.2) | async-done | bytes 98336 | tf_op jit(solution)/shard_map/all_to_all | solution.py:417
  104.4 15.9 %all_to_all.47 = bf16[8,96,256]{2,1,0:T(8,128)(2,1)S(1)} all-to-all(bf16[8,96,256]{2,1,0:T(8,128)(2,1)S(1)} %attend.1), channel_id=1, replica_groups=mesh['gx'=8,'gy'=32] {'gx'}, dimensions={0} | all-to-all | bytes 786432 | tf_op jit(solution)/shard_map/all_to_all | solution.py:47
  121.5 2.2 collective-permute-start.2
  124.9 1.9 collective-permute-done.2
  127.2 25.8 %all_to_all.48.p_ref = bf16[16,384,128]{2,1,0:T(8,128)(2,1)S(1)} all-to-all(bf16[16,384,128]{2,1,0:T(8,128)(2,1)S(1)} %add_convert_fusion.1), channel_id=1, replica_groups={{0,2,4,6,8,10,12,14,16,18,20,22,24,26,28,30},{1,3,5,7,9,11,13,15,17,19,..., dimensions={0} | all-to-all | bytes 3145728 | tf_op jit(solution)/shard_map/all_to_all | solution.py:43
  153.2 24.7 %all_to_all.49.x_ref = bf16[16,384,128]{2,1,0:T(8,128)(2,1)S(1)} all-to-all(bf16[16,384,128]{2,1,0:T(8,128)(2,1)S(1)} %get-tuple-element.16), channel_id=1, replica_groups={{0,2,4,6,8,10,12,14,16,18,20,22,24,26,28,30},{1,3,5,7,9,11,13,15,17,19,..., dimensions={0} | all-to-all | bytes 3145728 | tf_op jit(solution)/shard_map/all_to_all | solution.py:43
  177.9 2.3 collective-permute-start.3
  180.3 7.5 %gate_up_half.2 = (bf16[768,1280]{1,0:T(8,128)(2,1)}, bf16[768,512]{1,0:T(8,128)(2,1)S(1)}) custom-call(s32[1]{0:T(128)} %bitcast.h_ref, bf16[16,384,128]{2,1,0:T(8,128)(2,1)S(1)} %all_to_all.49.x_ref, f32[1,2048]{1,0:T(1,128)S(1)} %get-tuple-element.25.g_ref, bf16[832,2048]{1,0:T(8,128)(2,1)} %bitcast.32, bf16[832,2048]{1,0:T(8,128)(2,1)} %bitcast.34), custom_call_target="tpu_custom_call" | custom-call | flops 2617245696 | bytes 10485760 | tf_op jit(solution)/shard_map/gate_up_half/pallas_call | solution.py:316
  187.7 7.5 %gate_up_half.3 = (bf16[768,1280]{1,0:T(8,128)(2,1)}, bf16[768,512]{1,0:T(8,128)(2,1)S(1)}) custom-call(s32[1]{0:T(128)S(6)} %sub.5.h_ref, bf16[16,384,128]{2,1,0:T(8,128)(2,1)S(1)} %collective-permute-done.3.x_ref, f32[1,2048]{1,0:T(1,128)S(1)} %get-tuple-element.25.g_ref, ...), custom_call_target="tpu_custom_call", output_to_operand_aliasing={{0}: (5, {}), {1}: (6, {})} | custom-call | flops 2617245696 | bytes 10485760 | tf_op jit(solution)/shard_map/gate_up_half/pallas_call | solution.py:316
  195.3 34.0 %all_to_all.50.side_ref = bf16[8,96,512]{2,1,0:T(8,128)(2,1)S(1)} all-to-all(bf16[8,96,512]{2,1,0:T(8,128)(2,1)S(1)} %bitcast.25), channel_id=1, replica_groups=mesh['gx'=8,'gy'=32] {'gx'}, dimensions={0} | all-to-all | bytes 1572864 | tf_op jit(solution)/shard_map/all_to_all | solution.py:47
  229.2 10.5 %reduce-scatter.2.cloned.1.call-done.main_ref = bf16[96,1280]{1,0:T(8,128)(2,1)} async-done(((bf16[768,1280]{1,0:T(8,128)(2,1)}), bf16[96,1280]{1,0:T(8,128)(2,1)}) %reduce-scatter.2.cloned.1.call-update) | async-done | bytes 245776 | tf_op jit(solution)/shard_map/reduce_scatter | solution.py:426
  241.0 38.0 %all_to_all.51 = bf16[8,96,832]{2,1,0:T(8,128)(2,1)S(1)} all-to-all(bf16[8,96,832]{2,1,0:T(8,128)(2,1)S(1)} %hidden_copies.1), channel_id=1, replica_groups=mesh['gx'=8,'gy'=32] {'gx'}, dimensions={0} | all-to-all | bytes 2555904 | tf_op jit(solution)/shard_map/all_to_all | solution.py:47
  279.0 4.1 %proj_half.7 = bf16[16,384,128]{2,1,0:T(8,128)(2,1)S(1)} custom-call(s32[1]{0:T(128)S(6)} %sub.5.h_ref, bf16[768,832]{1,0:T(8,128)(2,1)S(1)} %bitcast.20, bf16[832,2048]{1,0:T(8,128)(2,1)} %w_ref.7), custom_call_target="tpu_custom_call" | custom-call | flops 1308622848 | bytes 4194304 | tf_op jit(solution)/shard_map/proj_half/pallas_call | solution.py:208
  283.1 4.2 %collective-permute-start.4 = (bf16[16,384,128]{2,1,0:T(8,128)(2,1)S(1)}, bf16[16,384,128]{2,1,0:T(8,128)(2,1)S(1)}, u32[]{:S(2)}, u32[]{:S(2)}) collective-permute-start(bf16[16,384,128]{2,1,0:T(8,128)(2,1)S(1)} %proj_half.7), channel_id=1, source_target_pairs={{0,1},{1,0},{2,3},{3,2},{4,5},{5,4},{6,7},{7,6},{8,9},{9,8},{10,11... | collective-permute-start | bytes 4718600 | tf_op jit(solution)/shard_map/ppermute | solution.py:39
  287.3 4.1 %proj_half.6 = f32[16,384,128]{2,1,0:T(8,128)S(1)} custom-call(s32[1]{0:T(128)} %bitcast.h_ref, bf16[768,832]{1,0:T(8,128)(2,1)S(1)} %bitcast.21, bf16[832,2048]{1,0:T(8,128)(2,1)} %w_ref.7), custom_call_target="tpu_custom_call" | custom-call | flops 1308622848 | bytes 4194304 | tf_op jit(solution)/shard_map/proj_half/pallas_call | solution.py:208
  293.0 3.7 %all-to-all-start.8 = ((bf16[16,384,128]{2,1,0:T(8,128)(2,1)}), bf16[16,384,128]{2,1,0:T(8,128)(2,1)S(1)}, u32[]{:S(2)}, u32[]{:S(2)}) async-start(bf16[16,384,128]{2,1,0:T(8,128)(2,1)} %add_convert_fusion), calls=%async_computation.9 | async-start | bytes 3145728 | tf_op jit(solution)/shard_map/all_to_all | solution.py:43
  296.8 26.7 %all-to-all-done.8.p_ref = bf16[16,384,128]{2,1,0:T(8,128)(2,1)S(1)} async-done(((bf16[16,384,128]{2,1,0:T(8,128)(2,1)}), bf16[16,384,128]{2,1,0:T(8,128)(2,1)S(1)}, u32[]{:S(2)}, u32[]{:S(2)}) %all-to-all-start.8) | async-done | bytes 1572896 | tf_op jit(solution)/shard_map/all_to_all | solution.py:43
  (53 shorter events, 15.4 us)
Async XLA Ops:
  7.5 4.3 %collective-permute-start = (bf16[384,64]{1,0:T(8,128)(2,1)S(1)}, bf16[384,64]{1,0:T(8,128)(2,1)S(1)}, u32[]{:S(2)}, u32[]{:S(2)}) collective-permute-start(bf16[384,64]{1,0:T(8,128)(2,1)S(1)} %copy.38), channel_id=1, source_target_pairs={{0,1},{1,0},{2,3},{3,2},{4,5},{5,4},{6,7},{7,6},{8,9},{9,8},{10,11... | collective-permute-start | bytes 147464 | tf_op jit(solution)/shard_map/ppermute | solution.py:39
  12.2 28.7 %copy-start.8 = (bf16[64]{0:T(256)(128)(2,1)S(1)}, bf16[64]{0:T(256)(128)(2,1)}, u32[]{:S(2)}) copy-start(bf16[64]{0:T(256)(128)(2,1)} %param.20) | copy-start | bytes 388
  12.2 28.7 %copy-start.9 = (bf16[64]{0:T(256)(128)(2,1)S(1)}, bf16[64]{0:T(256)(128)(2,1)}, u32[]{:S(2)}) copy-start(bf16[64]{0:T(256)(128)(2,1)} %param.15) | copy-start | bytes 388
  12.2 48.3 %copy-start.1 = (bf16[2048,256]{1,0:T(8,128)(2,1)S(1)}, bf16[2048,256]{1,0:T(8,128)(2,1)}, u32[]{:S(2)}) copy-start(bf16[2048,256]{1,0:T(8,128)(2,1)} %wq_ref.3) | copy-start | bytes 3145732
  12.2 48.3 %copy-start.2 = (bf16[2048,16]{0,1:T(8,128)(2,1)S(1)}, bf16[2048,16]{0,1:T(8,128)(2,1)}, u32[]{:S(2)}) copy-start(bf16[2048,16]{0,1:T(8,128)(2,1)} %param.17) | copy-start | bytes 196612
  12.3 48.3 %copy-start.3 = (bf16[2048,16]{0,1:T(8,128)(2,1)S(1)}, bf16[2048,16]{0,1:T(8,128)(2,1)}, u32[]{:S(2)}) copy-start(bf16[2048,16]{0,1:T(8,128)(2,1)} %param.18) | copy-start | bytes 196612
  39.2 23.1 %collective-permute-start.1 = (bf16[16,384,128]{2,1,0:T(8,128)(2,1)S(1)}, bf16[16,384,128]{2,1,0:T(8,128)(2,1)}, u32[]{:S(2)}, u32[]{:S(2)}) collective-permute-start(bf16[16,384,128]{2,1,0:T(8,128)(2,1)S(1)} %all_to_all.45.x_ref), channel_id=1, source_target_pairs={{0,1},{1,0},{2,3},{3,2},{4,5},{5,4},{6,7},{7,6},{8,9},{9,8},{10,11... | collective-permute-start | bytes 4718600 | tf_op jit(solution)/shard_map/ppermute | solution.py:39
  65.6 32.9 %copy-start.7 = (s32[96]{0:T(128)S(1)}, s32[96]{0:T(128)}, u32[]{:S(2)}) copy-start(s32[96]{0:T(128)} %param.25) | copy-start | bytes 1156
  65.6 37.7 %copy-start.5 = (f32[96,128]{1,0:T(8,128)S(1)}, f32[96,128]{1,0:T(8,128)}, u32[]{:S(2)}) copy-start(f32[96,128]{1,0:T(8,128)} %constant.33.clone.cos_ref) | copy-start | bytes 147460
  65.7 37.7 %copy-start.6 = (f32[96,128]{1,0:T(8,128)S(1)}, f32[96,128]{1,0:T(8,128)}, u32[]{:S(2)}) copy-start(f32[96,128]{1,0:T(8,128)} %constant.34.clone.sin_ref) | copy-start | bytes 147460
  92.7 27.7 %copy-start = (bf16[256,2048]{1,0:T(8,128)(2,1)S(1)}, bf16[256,2048]{1,0:T(8,128)(2,1)}, u32[]{:S(2)}) copy-start(bf16[256,2048]{1,0:T(8,128)(2,1)} %w_ref.5) | copy-start | bytes 3145732
  93.5 9.7 %all-to-all-start.2 = ((f32[8,96,32]{1,2,0:T(8,128)}), f32[8,96,32]{1,2,0:T(8,128)S(1)}, u32[]{:S(2)}, u32[]{:S(2)}) async-start(f32[8,96,32]{1,2,0:T(8,128)} %copy.33), calls=%async_computation.2 | async-start | bytes 262144 | tf_op jit(solution)/shard_map/all_to_all | solution.py:417
  97.9 141.8 %reduce-scatter.2.cloned.1.call-start = ((), (), s32[]{:S(2)}) async-start(), calls=%async_computation.10 | async-start | bytes 2211840 | tf_op jit(solution)/shard_map/reduce_scatter | solution.py:426
  121.5 5.2 %collective-permute-start.2 = (bf16[16,384,128]{2,1,0:T(8,128)(2,1)S(1)}, bf16[16,384,128]{2,1,0:T(8,128)(2,1)S(1)}, u32[]{:S(2)}, u32[]{:S(2)}) collective-permute-start(bf16[16,384,128]{2,1,0:T(8,128)(2,1)S(1)} %proj_half.5), channel_id=1, source_target_pairs={{0,1},{1,0},{2,3},{3,2},{4,5},{5,4},{6,7},{7,6},{8,9},{9,8},{10,11... | collective-permute-start | bytes 4718600 | tf_op jit(solution)/shard_map/ppermute | solution.py:39
  177.9 9.8 %collective-permute-start.3 = (bf16[16,384,128]{2,1,0:T(8,128)(2,1)S(1)}, bf16[16,384,128]{2,1,0:T(8,128)(2,1)S(1)}, u32[]{:S(2)}, u32[]{:S(2)}) collective-permute-start(bf16[16,384,128]{2,1,0:T(8,128)(2,1)S(1)} %all_to_all.49.x_ref), channel_id=1, source_target_pairs={{0,1},{1,0},{2,3},{3,2},{4,5},{5,4},{6,7},{7,6},{8,9},{9,8},{10,11... | collective-permute-start | bytes 4718600 | tf_op jit(solution)/shard_map/ppermute | solution.py:39
  239.7 0.9 copy-start.4
  283.1 8.3 %collective-permute-start.4 = (bf16[16,384,128]{2,1,0:T(8,128)(2,1)S(1)}, bf16[16,384,128]{2,1,0:T(8,128)(2,1)S(1)}, u32[]{:S(2)}, u32[]{:S(2)}) collective-permute-start(bf16[16,384,128]{2,1,0:T(8,128)(2,1)S(1)} %proj_half.7), channel_id=1, source_target_pairs={{0,1},{1,0},{2,3},{3,2},{4,5},{5,4},{6,7},{7,6},{8,9},{9,8},{10,11... | collective-permute-start | bytes 4718600 | tf_op jit(solution)/shard_map/ppermute | solution.py:39
  293.0 30.4 %all-to-all-start.8 = ((bf16[16,384,128]{2,1,0:T(8,128)(2,1)}), bf16[16,384,128]{2,1,0:T(8,128)(2,1)S(1)}, u32[]{:S(2)}, u32[]{:S(2)}) async-start(bf16[16,384,128]{2,1,0:T(8,128)(2,1)} %add_convert_fusion), calls=%async_computation.9 | async-start | bytes 3145728 | tf_op jit(solution)/shard_map/all_to_all | solution.py:43
  323.8 1.8 collective-permute-start.5
Sparse Core Ops, SparseCore 0:
  195.4 44.2 reduce-scatter.1

commit v2 on v1

v2 whole, which is shorter than its diff:
```python
import functools
import math

import jax
import jax.numpy as jnp
import numpy as np
from jax import lax
from jax.experimental import pallas as pl
from jax.experimental.pallas import tpu as pltpu
from jax.sharding import PartitionSpec as P

D = 16384
HEADS = 64
KV_HEADS = 4
HEAD_DIM = 128
SEQ = 96
EPS = 1e-05
ROPE_BASE = 500000.0

BF = jnp.bfloat16
F32 = jnp.float32

TOK = 768
HALF = 384
CHIPS = 16
LANE = 128
ROWS = 8
KSTEP = 4
FFL = 832
MAIN = 512
REST = FFL - MAIN
SIDE = 768
CHIP_GROUPS = [[2 * i + c for i in range(CHIPS)] for c in range(2)]
KV_GROUPS = [list(range(8 * i, 8 * i + 8)) for i in range(4)]
VMEM = 48 * 1024 * 1024


def swap(x):
    return lax.ppermute(x, "gy", [(i, i ^ 1) for i in range(32)])


def over_chips(x):
    return lax.all_to_all(x, "gy", 0, 0, axis_index_groups=CHIP_GROUPS, tiled=True)


def over_rows(x):
    return lax.all_to_all(x, "gx", 0, 0, tiled=True)


def params(**kw):
    return pltpu.CompilerParams(vmem_limit_bytes=VMEM, **kw)


def nt(a, b):
    return lax.dot_general(a, b, (((1,), (1,)), ((), ())), preferred_element_type=F32)


def nn(a, b):
    return jnp.dot(a, b, preferred_element_type=F32)


def fold_squares(wide):
    total = None
    for j in range(wide.shape[1] // LANE):
        part = wide[:, j * LANE : (j + 1) * LANE]
        total = part * part if total is None else total + part * part
    return total


def split_two(total):
    high = total.astype(BF).astype(F32)
    return high, total - high


def gained_block(x_ref, g_ref, row):
    chips = range(x_ref.shape[0])
    wide = jnp.concatenate([x_ref[j, :HALF] for j in chips], axis=1).astype(F32)
    gain = jnp.concatenate([g_ref[j, row : row + 1] for j in chips], axis=1).astype(F32)
    return wide, (wide * gain).astype(BF)


def qkv_kernel(h_ref, x_ref, g_ref, wq_ref, wk_ref, wv_ref, *rest):
    out_ref, acc_q, acc_kv, acc_sq = rest[-4:]
    k = pl.program_id(0)

    @pl.when(k == 0)
    def _():
        acc_q[...] = jnp.zeros_like(acc_q)
        acc_kv[...] = jnp.zeros_like(acc_kv)
        acc_sq[...] = jnp.zeros_like(acc_sq)

    wide, gained = gained_block(x_ref, g_ref, 0)
    acc_sq[...] += fold_squares(wide)
    acc_q[...] += nn(gained, wq_ref[...])
    acc_kv[...] += nt(jnp.concatenate([wk_ref[...], wv_ref[...]], axis=0), gained)

    @pl.when(k == pl.num_programs(0) - 1)
    def _():
        high, low = split_two(jnp.sum(jnp.transpose(acc_sq[...]), axis=0, keepdims=True))
        at = lax.broadcasted_iota(jnp.int32, (16, SEQ), 0)
        gap = jnp.zeros((16, LANE - SEQ), F32)
        for r in range(HALF // SEQ):
            here = slice(r * SEQ, (r + 1) * SEQ)
            out_ref[r, :SEQ] = acc_q[here].astype(BF)
            kv = acc_kv[:, here]
            sums = jnp.where(at == 0, high[:, here], jnp.where(at == 1, low[:, here], 0.0))
            top = jnp.concatenate([kv[:16], gap, kv[16:], gap], axis=1)
            bottom = jnp.concatenate([sums, gap, sums, gap], axis=1)
            out_ref[r, SEQ:] = jnp.concatenate([top, bottom], axis=0).astype(BF)


def qkv_half(h, x, gains, wq, wk_t, wv_t, held=None):
    depth = 2048 // KSTEP
    chips = CHIPS // KSTEP
    in_specs = [
        pl.BlockSpec((chips, HALF, LANE), lambda k, h: (k, 0, 0)),
        pl.BlockSpec((chips, 16, LANE), lambda k, h: (k, HALF // 16, 0)),
        pl.BlockSpec((depth, 256), lambda k, h: (k, 0)),
        pl.BlockSpec((16, depth), lambda k, h: (0, k)),
        pl.BlockSpec((16, depth), lambda k, h: (0, k)),
    ]
    operands = [h, x, gains, wq, wk_t, wv_t]
    aliases = {}
    if held is not None:
        in_specs.append(pl.BlockSpec(memory_space=pl.ANY))
        operands.append(held)
        aliases = {6: 0}
    return pl.pallas_call(
        qkv_kernel,
        grid_spec=pltpu.PrefetchScalarGridSpec(
            num_scalar_prefetch=1,
            grid=(KSTEP,),
            in_specs=in_specs,
            out_specs=pl.BlockSpec((HALF // SEQ, 128, 256), lambda k, h: (h[0], 0, 0)),
            scratch_shapes=[
                pltpu.VMEM((HALF, 256), F32),
                pltpu.VMEM((32, HALF), F32),
                pltpu.VMEM((HALF, LANE), F32),
            ],
        ),
        out_shape=jax.ShapeDtypeStruct((ROWS, 128, 256), BF),
        input_output_aliases=aliases,
        compiler_params=params(),
        cost_estimate=pl.CostEstimate(
            flops=2 * HALF * 2048 * 384, bytes_accessed=4 * 1024 * 1024, transcendentals=0
        ),
        name="qkv_half",
    )(*operands)


def qkv_sum_kernel(p_ref, q_ref, kv_ref):
    total = p_ref[0].astype(F32)
    for j in range(1, ROWS):
        total = total + p_ref[j].astype(F32)
    squares = total[112:113, :LANE] + total[113:114, :LANE]
    inv = lax.rsqrt(squares / D + EPS)
    down = jnp.transpose(jnp.broadcast_to(inv, (LANE, LANE)))[:SEQ]
    q_ref[...] = total[:SEQ] * jnp.concatenate([down, down], axis=1)
    kv = jnp.concatenate([total[96:112, :SEQ], total[96:112, LANE : LANE + SEQ]], axis=0)
    kv = kv * inv[:, :SEQ]
    for j in range(8):
        kv_ref[j] = kv


def qkv_sum(parts):
    return pl.pallas_call(
        qkv_sum_kernel,
        out_shape=(
            jax.ShapeDtypeStruct((SEQ, 256), F32),
            jax.ShapeDtypeStruct((8, 32, SEQ), F32),
        ),
        compiler_params=params(),
        name="qkv_sum",
    )(parts)


def attend_kernel(
    len_ref, q_ref, kv_ref, segr_ref, segc_ref, cos_ref, sin_ref, cost_ref, sint_ref, out_ref
):
    keys = jnp.concatenate([kv_ref[j, :16] for j in range(8)], axis=0)
    turned = jnp.concatenate([keys[64:], keys[:64]], axis=0)
    keys = (keys * cost_ref[...] + turned * sint_ref[...]).astype(BF)
    values = jnp.concatenate([kv_ref[j, 16:] for j in range(8)], axis=0).astype(BF)
    q_at = lax.broadcasted_iota(jnp.int32, (SEQ, SEQ), 0)
    k_at = lax.broadcasted_iota(jnp.int32, (SEQ, SEQ), 1)
    allowed = (segr_ref[...] == segc_ref[...]) & (k_at <= q_at) & (k_at < len_ref[0])
    allowed = allowed | (k_at == q_at)
    for head in range(2):
        query = q_ref[:, head * HEAD_DIM : (head + 1) * HEAD_DIM]
        query = (query * cos_ref[...] + pltpu.roll(query, 64, 1) * sin_ref[...]).astype(BF)
        scores = nn(query, keys) * (1.0 / math.sqrt(HEAD_DIM))
        scores = jnp.where(allowed, scores, F32(-1e30))
        expo = jnp.exp(scores - jnp.max(scores, axis=1, keepdims=True))
        soft = (expo / jnp.sum(expo, axis=1, keepdims=True)).astype(BF)
        attended = nt(soft, values).astype(BF)
        for j in range(ROWS):
            out_ref[j, :, head * HEAD_DIM : (head + 1) * HEAD_DIM] = attended


def attend(lengths, q, kv, segments):
    cos, sin = rope_tables()
    vmem = pl.BlockSpec(memory_space=pltpu.VMEM)
    return pl.pallas_call(
        attend_kernel,
        in_specs=[pl.BlockSpec(memory_space=pltpu.SMEM)] + [vmem] * 8,
        out_specs=vmem,
        out_shape=jax.ShapeDtypeStruct((ROWS, SEQ, 256), BF),
        compiler_params=params(),
        name="attend",
    )(
        lengths,
        q,
        kv,
        segments.reshape(1, SEQ),
        segments.reshape(SEQ, 1),
        cos,
        sin,
        np.ascontiguousarray(cos.T),
        np.ascontiguousarray(sin.T),
    )


def proj_kernel(h_ref, x_ref, w_ref, out_ref):
    result = nn(x_ref[...], w_ref[...]).astype(out_ref.dtype)
    for j in range(out_ref.shape[0]):
        out_ref[j] = result[:, j * LANE : (j + 1) * LANE]


def proj_half(h, x, w, dtype):
    depth = x.shape[1]
    steps = 4
    wide = 2048 // steps
    return pl.pallas_call(
        proj_kernel,
        grid_spec=pltpu.PrefetchScalarGridSpec(
            num_scalar_prefetch=1,
            grid=(steps,),
            in_specs=[
                pl.BlockSpec((HALF, depth), lambda i, h: (h[0], 0)),
                pl.BlockSpec((depth, wide), lambda i, h: (0, i)),
            ],
            out_specs=pl.BlockSpec((wide // LANE, HALF, LANE), lambda i, h: (i, 0, 0)),
        ),
        out_shape=jax.ShapeDtypeStruct((CHIPS, HALF, LANE), dtype),
        compiler_params=params(),
        cost_estimate=pl.CostEstimate(
            flops=2 * HALF * 2048 * depth, bytes_accessed=4 * 1024 * 1024, transcendentals=0
        ),
        name="proj_half",
    )(h, x, w)


def project_out(c, x, w):
    given = proj_half(1 - c, x, w, BF)
    got = swap(given)
    kept = proj_half(c, x, w, F32)
    return over_chips((kept + got.astype(F32)).astype(BF))


def residual_kernel(base_ref, p_ref, out_ref, copies_ref):
    total = p_ref[0].astype(F32)
    for j in range(1, CHIPS):
        total = total + p_ref[j].astype(F32)
    result = (base_ref[:HALF].astype(F32) + total).astype(BF)
    out_ref[...] = result
    for j in range(CHIPS):
        copies_ref[j] = result


def residual_copies(base, parts):
    return pl.pallas_call(
        residual_kernel,
        out_shape=(
            jax.ShapeDtypeStruct((HALF, LANE), BF),
            jax.ShapeDtypeStruct((CHIPS, HALF, LANE), BF),
        ),
        compiler_params=params(),
        name="residual_copies",
    )(base, parts)


def final_kernel(base_ref, p_ref, out_ref):
    total = p_ref[0].astype(F32)
    for j in range(1, CHIPS):
        total = total + p_ref[j].astype(F32)
    out_ref[...] = (base_ref[...].astype(F32) + total).astype(BF)


def final_sum(base, parts):
    return pl.pallas_call(
        final_kernel,
        out_shape=jax.ShapeDtypeStruct((HALF, LANE), BF),
        compiler_params=params(),
        name="final_sum",
    )(base, parts)


def gate_up_kernel(with_sums, h_ref, x_ref, g_ref, wg_ref, wu_ref, *rest):
    if with_sums:
        out_ref, acc_g, acc_u, acc_sq = rest[-4:]
    else:
        out_ref, acc_g, acc_u = rest[-3:]
    k = pl.program_id(0)

    @pl.when(k == 0)
    def _():
        acc_g[...] = jnp.zeros_like(acc_g)
        acc_u[...] = jnp.zeros_like(acc_u)
        if with_sums:
            acc_sq[...] = jnp.zeros_like(acc_sq)

    wide, gained = gained_block(x_ref, g_ref, 1)
    acc_g[...] += nt(gained, wg_ref[...])
    acc_u[...] += nt(gained, wu_ref[...])
    if with_sums:
        acc_sq[...] += fold_squares(wide)

    @pl.when(k == pl.num_programs(0) - 1)
    def _():
        half = out_ref.shape[1] // 2
        if with_sums:
            high, low = split_two(jnp.sum(acc_sq[...], axis=1, keepdims=True))
            lane = lax.broadcasted_iota(jnp.int32, (HALF, half - REST), 1)
            extra = jnp.where(lane == 0, high, jnp.where(lane == 1, low, 0.0))
            blank = jnp.zeros_like(extra)
            out_ref[:, :half] = jnp.concatenate([acc_g[...], extra], axis=1).astype(BF)
            out_ref[:, half:] = jnp.concatenate([acc_u[...], blank], axis=1).astype(BF)
        else:
            out_ref[:, :half] = acc_g[...].astype(BF)
            out_ref[:, half:] = acc_u[...].astype(BF)


def gate_up_half(h, x, gains, wg_t, wu_t, with_sums, held=None):
    depth = 2048 // KSTEP
    chips = CHIPS // KSTEP
    at, width, out_width = (MAIN, REST, SIDE) if with_sums else (0, MAIN, 2 * MAIN)
    weight_spec = pl.BlockSpec((pl.Element(width), pl.Element(depth)), lambda k, h: (at, k * depth))
    in_specs = [
        pl.BlockSpec((chips, HALF, LANE), lambda k, h: (k, 0, 0)),
        pl.BlockSpec((chips, 16, LANE), lambda k, h: (k, HALF // 16, 0)),
        weight_spec,
        weight_spec,
    ]
    operands = [h, x, gains, wg_t, wu_t]
    aliases = {}
    if held is not None:
        in_specs.append(pl.BlockSpec(memory_space=pl.ANY))
        operands.append(held)
        aliases = {5: 0}
    scratch = [pltpu.VMEM((HALF, width), F32), pltpu.VMEM((HALF, width), F32)]
    if with_sums:
        scratch.append(pltpu.VMEM((HALF, LANE), F32))
    return pl.pallas_call(
        functools.partial(gate_up_kernel, with_sums),
        grid_spec=pltpu.PrefetchScalarGridSpec(
            num_scalar_prefetch=1,
            grid=(KSTEP,),
            in_specs=in_specs,
            out_specs=pl.BlockSpec((HALF, out_width), lambda k, h: (h[0], 0)),
            scratch_shapes=scratch,
        ),
        out_shape=jax.ShapeDtypeStruct((TOK, out_width), BF),
        input_output_aliases=aliases,
        compiler_params=params(),
        cost_estimate=pl.CostEstimate(
            flops=2 * HALF * 2048 * 2 * width,
            bytes_accessed=4 * 2048 * width + 2 * 1024 * 1024,
            transcendentals=0,
        ),
        name="gate_up_side" if with_sums else "gate_up_main",
    )(*operands)


def hidden_kernel(main_ref, side_ref, out_ref):
    side = side_ref[0].astype(F32)
    for j in range(1, ROWS):
        side = side + side_ref[j].astype(F32)
    squares = side[:, REST : REST + 1] + side[:, REST + 1 : REST + 2]
    inv = lax.rsqrt(squares / D + EPS)

    def gated(gate, up):
        gate, up = gate * inv, up * inv
        return (gate / (1.0 + jnp.exp(-gate)) * up).astype(BF)

    first = gated(main_ref[:, :MAIN].astype(F32), main_ref[:, MAIN:].astype(F32))
    second = gated(side[:, :REST], side[:, SIDE // 2 : SIDE // 2 + REST])
    for j in range(ROWS):
        out_ref[j, :, :MAIN] = first
        out_ref[j, :, MAIN:] = second


def hidden_copies(main, side):
    return pl.pallas_call(
        hidden_kernel,
        out_shape=jax.ShapeDtypeStruct((ROWS, SEQ, FFL), BF),
        compiler_params=params(),
        name="hidden_copies",
    )(main, side)


def rope_tables():
    inv_freq = np.power(
        np.float32(ROPE_BASE), -(np.arange(64, dtype=np.float32) * np.float32(2.0 / HEAD_DIM))
    ).astype(np.float32)
    angles = np.arange(SEQ, dtype=np.float32)[:, None] * inv_freq[None, :]
    cos, sin = np.cos(angles.astype(np.float64)), np.sin(angles.astype(np.float64))
    return (
        np.concatenate([cos, cos], axis=1).astype(np.float32),
        np.concatenate([-sin, sin], axis=1).astype(np.float32),
    )


def per_device(
    tokens,
    norm_attn,
    w_query,
    w_key,
    w_value,
    w_out,
    norm_ffn,
    w_gate,
    w_up,
    w_down,
    lengths,
    segments,
):
    core = lax.axis_index("gy") % 2
    c = jnp.reshape(core, (1,)).astype(jnp.int32)

    gains = jnp.concatenate([norm_attn[None], norm_ffn[None], jnp.zeros((14, 64), BF)], axis=0)

    def with_gains(start):
        return jnp.concatenate([lax.dynamic_slice_in_dim(tokens, start, HALF, 0), gains], axis=0)

    mine = with_gains(core * HALF)
    theirs = swap(with_gains((1 - core) * HALF))
    base = jnp.where(
        core == 0,
        jnp.concatenate([mine, theirs], axis=1),
        jnp.concatenate([theirs, mine], axis=1),
    )

    first = over_chips(jnp.broadcast_to(base[None], (CHIPS,) + base.shape))
    other = swap(first)
    held = qkv_half(c, first, first, w_query, w_key.T, w_value.T)
    parts = qkv_half(1 - c, other, first, w_query, w_key.T, w_value.T, held)
    q, kv = qkv_sum(over_rows(parts))
    kv = lax.all_to_all(kv, "gy", 0, 0, axis_index_groups=KV_GROUPS, tiled=True)
    attended = over_rows(attend(lengths, q, kv, segments)).reshape(TOK, 256)
    residual, copies = residual_copies(base, project_out(c, attended, w_out))

    own = over_chips(copies)
    other = swap(own)
    weights = (w_gate.T, w_up.T)
    held = gate_up_half(c, own, first, *weights, False)
    main = gate_up_half(1 - c, other, first, *weights, False, held)
    own, other, later = lax.optimization_barrier((own, other, main))
    main = lax.psum_scatter(later, "gx", scatter_dimension=0, tiled=True)
    held = gate_up_half(c, own, first, *weights, True)
    side = gate_up_half(1 - c, other, first, *weights, True, held)
    side = over_rows(side.reshape(ROWS, SEQ, SIDE))
    hidden = over_rows(hidden_copies(main, side)).reshape(TOK, FFL)
    done = final_sum(residual, project_out(c, hidden, w_down))

    keep = lax.dynamic_slice_in_dim(done, core * 64, 64, 1)
    got = swap(lax.dynamic_slice_in_dim(done, (1 - core) * 64, 64, 1))
    return jnp.where(
        core == 0,
        jnp.concatenate([keep, got], axis=0),
        jnp.concatenate([got, keep], axis=0),
    )


def solution(mesh):
    in_specs = (
        P(None, ("gx", "gy")),
        P(("gx", "gy")),
        P("gx", "gy"),
        P("gx", "gy"),
        P("gx", "gy"),
        P("gy", "gx"),
        P(("gx", "gy")),
        P("gx", "gy"),
        P("gx", "gy"),
        P("gy", "gx"),
        P("gx"),
        P("gx"),
    )
    out_specs = P(None, ("gx", "gy"))
    return jax.shard_map(
        per_device, mesh=mesh, in_specs=in_specs, out_specs=out_specs, check_vma=False
    )
```

time: 334 us -> 316 us (0.946)
  blocking collectives: 212 us -> 198 us
  waiting for transfers between devices: 45.4 us -> 35 us
  Pallas kernels: 32.6 us -> 36.2 us
    all_gather x1 -> x0, blocking collectives: 19.4 us -> none  [per_device(): lax.all_gather(jnp.stack([norm_attn, norm_ffn]), 'gy', axis=1, tiled=True)]
    reduce_scatter x1, waiting for transfers between devices: 10.5 us -> 0.01 us  [per_device(): main = lax.psum_scatter(later, 'gx', scatter_dimension=0, tiled=True)]
    all_to_all x4, blocking collectives: 115 us -> 121 us  [over_rows(): return lax.all_to_all(x, 'gx', 0, 0, tiled=True)]
    pallas_call x2 -> x4, Pallas kernels: 15 us -> 19.8 us  [gate_up_half(): pl.pallas_call(functools.partial(gate_up_kernel, with_sums), grid_spec=pl...]
  transfers between devices with their start and end apart: 9 -> 9, of which waited for: 6 -> 6; matrix products, arithmetic and copies ran while one was open for 0% -> 0% of each run, Pallas kernels for 4% -> 7%
where the time goes in v2:
time: 316 us; the launch traced here: 315 us
  blocking collectives  198 us (63%)
  Pallas kernels  36.2 us (11%)
  waiting for transfers between devices  35 us (11%)
  starting transfers between devices  24.3 us (8%)
  between operations  14.3 us (5%)
  local copies, waits for them, and re-layouts  4.42 us (1%)
  other arithmetic  3.59 us (1%)
    all_to_all x4, blocking collectives, over_rows(): return lax.all_to_all(x, 'gx', 0, 0, tiled=True)  121 us
    all_to_all x3, blocking collectives, over_chips(): lax.all_to_all(x, 'gy', 0, 0, axis_index_groups=CHIP_GROUPS, tiled=True)  76.9 us
    all_to_all x1, waiting for transfers between devices, over_chips(): lax.all_to_all(x, 'gy', 0, 0, axis_index_groups=CHIP_GROUPS, tiled=True)  25.6 us
    pallas_call x4, Pallas kernels, gate_up_half(): pl.pallas_call(functools.partial(gate_up_kernel, with_sums), grid_spec=pl...  19.8 us
    ppermute x6, starting transfers between devices, swap(): return lax.ppermute(x, 'gy', [(i, i ^ 1) for i in range(32)])  13.5 us
    pallas_call x4, Pallas kernels, proj_half(): pl.pallas_call(proj_kernel, grid_spec=pltpu.PrefetchScalarGridSpec(num_sc...  10.6 us
  transfers between devices with their start and end apart: 9, of which 6 were waited for; matrix products, arithmetic and copies ran while one was open for 0% of the time, Pallas kernels for 7%

profile of v2, /device:TPU:1, one launch (start us, length us, event | category | flops | bytes accessed | tf_op | source)
XLA Modules:
  0.0 315.4 jit_solution(2908851923200186602)
XLA Ops:
  8.2 3.3 %collective-permute-start = (bf16[400,64]{1,0:T(8,128)(2,1)S(1)}, bf16[400,64]{1,0:T(8,128)(2,1)S(1)}, u32[]{:S(2)}, u32[]{:S(2)}) collective-permute-start(bf16[400,64]{1,0:T(8,128)(2,1)S(1)} %pad_maximum_fusion), channel_id=1, source_target_pairs={{0,1},{1,0},{2,3},{3,2},{4,5},{5,4},{6,7},{7,6},{8,9},{9,8},{10,11... | collective-permute-start | bytes 153608 | tf_op jit(solution)/shard_map/ppermute | solution.py:39
  13.6 27.6 %all_to_all.45.x_ref.g_ref = bf16[16,400,128]{2,1,0:T(8,128)(2,1)S(1)} all-to-all(bf16[16,400,128]{2,1,0:T(8,128)(2,1)S(1)} %broadcast_in_dim.18), channel_id=1, replica_groups={{0,2,4,6,8,10,12,14,16,18,20,22,24,26,28,30},{1,3,5,7,9,11,13,15,17,19,..., dimensions={0} | all-to-all | bytes 3276800 | tf_op jit(solution)/shard_map/all_to_all | solution.py:43
  43.0 1.9 qkv_half.2.rest_0_
  46.2 1.9 qkv_half.3
  48.1 24.8 %all_to_all.46.p_ref = bf16[8,128,256]{2,1,0:T(8,128)(2,1)S(1)} all-to-all(bf16[8,128,256]{2,1,0:T(8,128)(2,1)S(1)} %qkv_half.3), channel_id=1, replica_groups=mesh['gx'=8,'gy'=32] {'gx'}, dimensions={0} | all-to-all | bytes 1048576 | tf_op jit(solution)/shard_map/all_to_all | solution.py:47
  73.6 5.0 %all-to-all-start.2 = ((f32[8,32,96]{2,1,0:T(8,128)}), f32[8,32,96]{2,1,0:T(8,128)S(1)}, u32[]{:S(2)}, u32[]{:S(2)}) async-start(f32[8,32,96]{2,1,0:T(8,128)} %get-tuple-element.13), calls=%async_computation.2 | async-start | bytes 262144 | tf_op jit(solution)/shard_map/all_to_all | solution.py:448
  79.4 4.5 %all-to-all-done.2.kv_ref = f32[8,32,96]{2,1,0:T(8,128)S(1)} async-done(((f32[8,32,96]{2,1,0:T(8,128)}), f32[8,32,96]{2,1,0:T(8,128)S(1)}, u32[]{:S(2)}, u32[]{:S(2)}) %all-to-all-start.2) | async-done | bytes 98336 | tf_op jit(solution)/shard_map/all_to_all | solution.py:448
  84.5 15.9 %all_to_all.47 = bf16[8,96,256]{2,1,0:T(8,128)(2,1)S(1)} all-to-all(bf16[8,96,256]{2,1,0:T(8,128)(2,1)S(1)} %attend.1), channel_id=1, replica_groups=mesh['gx'=8,'gy'=32] {'gx'}, dimensions={0} | all-to-all | bytes 786432 | tf_op jit(solution)/shard_map/all_to_all | solution.py:47
  101.6 2.2 collective-permute-start.2
  105.0 1.9 collective-permute-done.2
  107.3 24.6 %all_to_all.48.p_ref = bf16[16,384,128]{2,1,0:T(8,128)(2,1)S(1)} all-to-all(bf16[16,384,128]{2,1,0:T(8,128)(2,1)S(1)} %add_convert_fusion.1), channel_id=1, replica_groups={{0,2,4,6,8,10,12,14,16,18,20,22,24,26,28,30},{1,3,5,7,9,11,13,15,17,19,..., dimensions={0} | all-to-all | bytes 3145728 | tf_op jit(solution)/shard_map/all_to_all | solution.py:43
  132.1 24.7 %all_to_all.49.x_ref = bf16[16,384,128]{2,1,0:T(8,128)(2,1)S(1)} all-to-all(bf16[16,384,128]{2,1,0:T(8,128)(2,1)S(1)} %get-tuple-element.15), channel_id=1, replica_groups={{0,2,4,6,8,10,12,14,16,18,20,22,24,26,28,30},{1,3,5,7,9,11,13,15,17,19,..., dimensions={0} | all-to-all | bytes 3145728 | tf_op jit(solution)/shard_map/all_to_all | solution.py:43
  156.9 2.3 collective-permute-start.3
  159.2 5.5 %gate_up_main.2.rest_0_ = bf16[768,1024]{1,0:T(8,128)(2,1)} custom-call(s32[1]{0:T(128)} %bitcast.2.h_ref, bf16[16,384,128]{2,1,0:T(8,128)(2,1)S(1)} %all_to_all.49.x_ref, bf16[16,400,128]{2,1,0:T(8,128)(2,1)S(1)} %all_to_all.45.x_ref.g_ref, bf16[832,2048]{1,0:T(8,128)(2,1)} %bitcast.23, bf16[832,2048]{1,0:T(8,128)(2,1)} %bitcast.27), custom_call_target="tpu_custom_call" | custom-call | flops 1610612736 | bytes 6291456 | tf_op jit(solution)/shard_map/gate_up_main/pallas_call | solution.py:353
  164.7 5.5 %gate_up_main.3 = bf16[768,1024]{1,0:T(8,128)(2,1)} custom-call(s32[1]{0:T(128)S(6)} %sub.5.h_ref, bf16[16,384,128]{2,1,0:T(8,128)(2,1)S(1)} %collective-permute-done.3.x_ref, bf16[16,400,128]{2,1,0:T(8,128)(2,1)S(1)} %all_to_all.45.x_ref.g_ref, bf16[832,2048]{1,0:T(8,128)(2,1)} %bitcast.24, ...), custom_call_target="tpu_custom_call", output_to_operand_aliasing={{}: (5, {})} | custom-call | flops 1610612736 | bytes 6291456 | tf_op jit(solution)/shard_map/gate_up_main/pallas_call | solution.py:353
  171.4 4.4 %gate_up_side.2.rest_0_ = bf16[768,768]{1,0:T(8,128)(2,1)S(1)} custom-call(s32[1]{0:T(128)} %bitcast.2.h_ref, bf16[16,384,128]{2,1,0:T(8,128)(2,1)S(1)} %all_to_all.49.x_ref, bf16[16,400,128]{2,1,0:T(8,128)(2,1)S(1)} %all_to_all.45.x_ref.g_ref, bf16[832,2048]{1,0:T(8,128)(2,1)} %bitcast.25, bf16[832,2048]{1,0:T(8,128)(2,1)} %bitcast.29), custom_call_target="tpu_custom_call" | custom-call | flops 1006632960 | bytes 4718592 | tf_op jit(solution)/shard_map/gate_up_side/pallas_call | solution.py:353
  175.8 4.3 %gate_up_side.3 = bf16[768,768]{1,0:T(8,128)(2,1)S(1)} custom-call(s32[1]{0:T(128)S(6)} %sub.5.h_ref, bf16[16,384,128]{2,1,0:T(8,128)(2,1)S(1)} %copy-done.1, bf16[16,400,128]{2,1,0:T(8,128)(2,1)S(1)} %all_to_all.45.x_ref.g_ref, bf16[832,2048]{1,0:T(8,128)(2,1)} %bitcast.26, bf16[832,2048]{1,0:T(8,128)(2,1)} %bitcast.30, ...), custom_call_target="tpu_custom_call", output_to_operand_aliasing={{}: (5, {})} | custom-call | flops 1006632960 | bytes 4718592 | tf_op jit(solution)/shard_map/gate_up_side/pallas_call | solution.py:353
  180.1 43.3 %all_to_all.50.side_ref = bf16[8,96,768]{2,1,0:T(8,128)(2,1)S(1)} all-to-all(bf16[8,96,768]{2,1,0:T(8,128)(2,1)S(1)} %bitcast.14), channel_id=1, replica_groups=mesh['gx'=8,'gy'=32] {'gx'}, dimensions={0} | all-to-all | bytes 2359296 | tf_op jit(solution)/shard_map/all_to_all | solution.py:47
  224.7 36.6 %all_to_all.51 = bf16[8,96,832]{2,1,0:T(8,128)(2,1)S(1)} all-to-all(bf16[8,96,832]{2,1,0:T(8,128)(2,1)S(1)} %hidden_copies.1), channel_id=1, replica_groups=mesh['gx'=8,'gy'=32] {'gx'}, dimensions={0} | all-to-all | bytes 2555904 | tf_op jit(solution)/shard_map/all_to_all | solution.py:47
  261.3 4.1 %proj_half.7 = bf16[16,384,128]{2,1,0:T(8,128)(2,1)S(1)} custom-call(s32[1]{0:T(128)S(6)} %sub.5.h_ref, bf16[768,832]{1,0:T(8,128)(2,1)S(1)} %bitcast.12, bf16[832,2048]{1,0:T(8,128)(2,1)} %w_ref.7), custom_call_target="tpu_custom_call" | custom-call | flops 1308622848 | bytes 4194304 | tf_op jit(solution)/shard_map/proj_half/pallas_call | solution.py:233
  265.4 2.6 collective-permute-start.4
  268.1 4.1 %proj_half.6 = f32[16,384,128]{2,1,0:T(8,128)S(1)} custom-call(s32[1]{0:T(128)} %bitcast.2.h_ref, bf16[768,832]{1,0:T(8,128)(2,1)S(1)} %bitcast.13, bf16[832,2048]{1,0:T(8,128)(2,1)} %w_ref.7), custom_call_target="tpu_custom_call" | custom-call | flops 1308622848 | bytes 4194304 | tf_op jit(solution)/shard_map/proj_half/pallas_call | solution.py:233
  273.8 5.8 %all-to-all-start.8 = ((bf16[16,384,128]{2,1,0:T(8,128)(2,1)}), bf16[16,384,128]{2,1,0:T(8,128)(2,1)S(1)}, u32[]{:S(2)}, u32[]{:S(2)}) async-start(bf16[16,384,128]{2,1,0:T(8,128)(2,1)} %add_convert_fusion), calls=%async_computation.9 | async-start | bytes 3145728 | tf_op jit(solution)/shard_map/all_to_all | solution.py:43
  279.6 25.6 %all-to-all-done.8.p_ref = bf16[16,384,128]{2,1,0:T(8,128)(2,1)S(1)} async-done(((bf16[16,384,128]{2,1,0:T(8,128)(2,1)}), bf16[16,384,128]{2,1,0:T(8,128)(2,1)S(1)}, u32[]{:S(2)}, u32[]{:S(2)}) %all-to-all-start.8) | async-done | bytes 1572896 | tf_op jit(solution)/shard_map/all_to_all | solution.py:43
  (54 shorter events, 18.4 us)
Async XLA Ops:
  8.2 4.3 %collective-permute-start = (bf16[400,64]{1,0:T(8,128)(2,1)S(1)}, bf16[400,64]{1,0:T(8,128)(2,1)S(1)}, u32[]{:S(2)}, u32[]{:S(2)}) collective-permute-start(bf16[400,64]{1,0:T(8,128)(2,1)S(1)} %pad_maximum_fusion), channel_id=1, source_target_pairs={{0,1},{1,0},{2,3},{3,2},{4,5},{5,4},{6,7},{7,6},{8,9},{9,8},{10,11... | collective-permute-start | bytes 153608 | tf_op jit(solution)/shard_map/ppermute | solution.py:39
  13.6 29.4 %copy-start.3 = (bf16[2048,256]{1,0:T(8,128)(2,1)S(1)}, bf16[2048,256]{1,0:T(8,128)(2,1)}, u32[]{:S(2)}) copy-start(bf16[2048,256]{1,0:T(8,128)(2,1)} %wq_ref.3) | copy-start | bytes 3145732
  13.6 29.4 %copy-start.4 = (bf16[2048,16]{0,1:T(8,128)(2,1)S(1)}, bf16[2048,16]{0,1:T(8,128)(2,1)}, u32[]{:S(2)}) copy-start(bf16[2048,16]{0,1:T(8,128)(2,1)} %param.19) | copy-start | bytes 196612
  13.6 29.4 %copy-start.5 = (bf16[2048,16]{0,1:T(8,128)(2,1)S(1)}, bf16[2048,16]{0,1:T(8,128)(2,1)}, u32[]{:S(2)}) copy-start(bf16[2048,16]{0,1:T(8,128)(2,1)} %param.20) | copy-start | bytes 196612
  41.2 4.9 %collective-permute-start.1 = (bf16[16,400,128]{2,1,0:T(8,128)(2,1)S(1)}, bf16[16,400,128]{2,1,0:T(8,128)(2,1)S(1)}, u32[]{:S(2)}, u32[]{:S(2)}) collective-permute-start(bf16[16,400,128]{2,1,0:T(8,128)(2,1)S(1)} %all_to_all.45.x_ref.g_ref), channel_id=1, source_target_pairs={{0,1},{1,0},{2,3},{3,2},{4,5},{5,4},{6,7},{7,6},{8,9},{9,8},{10,11... | collective-permute-start | bytes 4915208 | tf_op jit(solution)/shard_map/ppermute | solution.py:39
  48.0 30.6 %copy-start.11 = (s32[96]{0:T(128)S(1)}, s32[96]{0:T(128)}, u32[]{:S(2)}) copy-start(s32[96]{0:T(128)} %param.27) | copy-start | bytes 1156
  48.0 35.9 %copy-start.7 = (f32[128,96]{1,0:T(8,128)S(1)}, f32[128,96]{1,0:T(8,128)}, u32[]{:S(2)}) copy-start(f32[128,96]{1,0:T(8,128)} %constant.41.clone.cost_ref) | copy-start | bytes 147460
  48.1 35.9 %copy-start.8 = (f32[128,96]{1,0:T(8,128)S(1)}, f32[128,96]{1,0:T(8,128)}, u32[]{:S(2)}) copy-start(f32[128,96]{1,0:T(8,128)} %constant.42.clone.sint_ref) | copy-start | bytes 147460
  48.1 35.9 %copy-start.9 = (f32[96,128]{1,0:T(8,128)S(1)}, f32[96,128]{1,0:T(8,128)}, u32[]{:S(2)}) copy-start(f32[96,128]{1,0:T(8,128)} %constant.39.clone.cos_ref) | copy-start | bytes 147460
  48.1 35.9 %copy-start.10 = (f32[96,128]{1,0:T(8,128)S(1)}, f32[96,128]{1,0:T(8,128)}, u32[]{:S(2)}) copy-start(f32[96,128]{1,0:T(8,128)} %constant.40.clone.sin_ref) | copy-start | bytes 147460
  48.1 52.3 %copy-start.2 = (bf16[256,2048]{1,0:T(8,128)(2,1)S(1)}, bf16[256,2048]{1,0:T(8,128)(2,1)}, u32[]{:S(2)}) copy-start(bf16[256,2048]{1,0:T(8,128)(2,1)} %w_ref.5) | copy-start | bytes 3145732
  73.6 10.3 %all-to-all-start.2 = ((f32[8,32,96]{2,1,0:T(8,128)}), f32[8,32,96]{2,1,0:T(8,128)S(1)}, u32[]{:S(2)}, u32[]{:S(2)}) async-start(f32[8,32,96]{2,1,0:T(8,128)} %get-tuple-element.13), calls=%async_computation.2 | async-start | bytes 262144 | tf_op jit(solution)/shard_map/all_to_all | solution.py:448
  78.6 144.8 %reduce-scatter.2.cloned.1.call-start = ((), (), s32[]{:S(2)}) async-start(), calls=%async_computation.10 | async-start | bytes 1769472 | tf_op jit(solution)/shard_map/reduce_scatter | solution.py:458
  101.6 5.2 %collective-permute-start.2 = (bf16[16,384,128]{2,1,0:T(8,128)(2,1)S(1)}, bf16[16,384,128]{2,1,0:T(8,128)(2,1)S(1)}, u32[]{:S(2)}, u32[]{:S(2)}) collective-permute-start(bf16[16,384,128]{2,1,0:T(8,128)(2,1)S(1)} %proj_half.5), channel_id=1, source_target_pairs={{0,1},{1,0},{2,3},{3,2},{4,5},{5,4},{6,7},{7,6},{8,9},{9,8},{10,11... | collective-permute-start | bytes 4718600 | tf_op jit(solution)/shard_map/ppermute | solution.py:39
  156.9 7.8 %collective-permute-start.3 = (bf16[16,384,128]{2,1,0:T(8,128)(2,1)S(1)}, bf16[16,384,128]{2,1,0:T(8,128)(2,1)S(1)}, u32[]{:S(2)}, u32[]{:S(2)}) collective-permute-start(bf16[16,384,128]{2,1,0:T(8,128)(2,1)S(1)} %all_to_all.49.x_ref), channel_id=1, source_target_pairs={{0,1},{1,0},{2,3},{3,2},{4,5},{5,4},{6,7},{7,6},{8,9},{9,8},{10,11... | collective-permute-start | bytes 4718600 | tf_op jit(solution)/shard_map/ppermute | solution.py:39
  170.2 1.1 copy-start
  171.3 4.4 %copy-start.1 = (bf16[16,384,128]{2,1,0:T(8,128)(2,1)S(1)}, bf16[16,384,128]{2,1,0:T(8,128)(2,1)}, u32[]{:S(2)}) copy-start(bf16[16,384,128]{2,1,0:T(8,128)(2,1)} %copy-done) | copy-start | bytes 4718596
  223.5 0.9 copy-start.6
  265.4 6.8 %collective-permute-start.4 = (bf16[16,384,128]{2,1,0:T(8,128)(2,1)S(1)}, bf16[16,384,128]{2,1,0:T(8,128)(2,1)S(1)}, u32[]{:S(2)}, u32[]{:S(2)}) collective-permute-start(bf16[16,384,128]{2,1,0:T(8,128)(2,1)S(1)} %proj_half.7), channel_id=1, source_target_pairs={{0,1},{1,0},{2,3},{3,2},{4,5},{5,4},{6,7},{7,6},{8,9},{9,8},{10,11... | collective-permute-start | bytes 4718600 | tf_op jit(solution)/shard_map/ppermute | solution.py:39
  273.8 31.4 %all-to-all-start.8 = ((bf16[16,384,128]{2,1,0:T(8,128)(2,1)}), bf16[16,384,128]{2,1,0:T(8,128)(2,1)S(1)}, u32[]{:S(2)}, u32[]{:S(2)}) async-start(bf16[16,384,128]{2,1,0:T(8,128)(2,1)} %add_convert_fusion), calls=%async_computation.9 | async-start | bytes 3145728 | tf_op jit(solution)/shard_map/all_to_all | solution.py:43
  305.6 2.2 collective-permute-start.5
Sparse Core Ops, SparseCore 0:
  171.5 46.4 reduce-scatter.1

commit v3 on v2

--- a/solution.py
+++ b/solution.py
@@ -32,7 +32,6 @@
 SIDE = 768
 CHIP_GROUPS = [[2 * i + c for i in range(CHIPS)] for c in range(2)]
 KV_GROUPS = [list(range(8 * i, 8 * i + 8)) for i in range(4)]
-VMEM = 48 * 1024 * 1024
 
 
 def swap(x):
@@ -47,8 +46,8 @@
     return lax.all_to_all(x, "gx", 0, 0, tiled=True)
 
 
-def params(**kw):
-    return pltpu.CompilerParams(vmem_limit_bytes=VMEM, **kw)
+def params(mib=16):
+    return pltpu.CompilerParams(vmem_limit_bytes=mib * 1024 * 1024)
 
 
 def nt(a, b):
@@ -228,7 +227,7 @@
 
 def proj_half(h, x, w, dtype):
     depth = x.shape[1]
-    steps = 4
+    steps = 2
     wide = 2048 // steps
     return pl.pallas_call(
         proj_kernel,
@@ -261,7 +260,7 @@
     total = p_ref[0].astype(F32)
     for j in range(1, CHIPS):
         total = total + p_ref[j].astype(F32)
-    result = (base_ref[:HALF].astype(F32) + total).astype(BF)
+    result = (base_ref[0, :HALF].astype(F32) + total).astype(BF)
     out_ref[...] = result
     for j in range(CHIPS):
         copies_ref[j] = result
@@ -279,67 +278,119 @@
     )(base, parts)
 
 
-def final_kernel(base_ref, p_ref, out_ref):
+def final_kernel(h_ref, base_ref, p_ref, keep_ref, give_ref):
     total = p_ref[0].astype(F32)
     for j in range(1, CHIPS):
         total = total + p_ref[j].astype(F32)
-    out_ref[...] = (base_ref[...].astype(F32) + total).astype(BF)
-
-
-def final_sum(base, parts):
+    done = (base_ref[...].astype(F32) + total).astype(BF)
+    first, second = done[:, :64], done[:, 64:]
+    keep_ref[...] = jnp.where(h_ref[0] == 0, first, second)
+    give_ref[...] = jnp.where(h_ref[0] == 0, second, first)
+
+
+def final_sum(h, base, parts):
+    vmem = pl.BlockSpec(memory_space=pltpu.VMEM)
     return pl.pallas_call(
         final_kernel,
-        out_shape=jax.ShapeDtypeStruct((HALF, LANE), BF),
+        in_specs=[pl.BlockSpec(memory_space=pltpu.SMEM), vmem, vmem],
+        out_specs=(vmem, vmem),
+        out_shape=(jax.ShapeDtypeStruct((HALF, 64), BF),) * 2,
         compiler_params=params(),
         name="final_sum",
-    )(base, parts)
-
-
-def gate_up_kernel(with_sums, h_ref, x_ref, g_ref, wg_ref, wu_ref, *rest):
-    if with_sums:
-        out_ref, acc_g, acc_u, acc_sq = rest[-4:]
-    else:
-        out_ref, acc_g, acc_u = rest[-3:]
-    k = pl.program_id(0)
-
-    @pl.when(k == 0)
+    )(h, base, parts)
+
+
+def place_kernel(h_ref, keep_ref, got_ref, out_ref):
+    keep, got = keep_ref[...], got_ref[...]
+    out_ref[:, :HALF] = jnp.transpose(jnp.where(h_ref[0] == 0, keep, got))
+    out_ref[:, HALF:] = jnp.transpose(jnp.where(h_ref[0] == 0, got, keep))
+
+
+def place_halves(h, keep, got):
+    vmem = pl.BlockSpec(memory_space=pltpu.VMEM)
+    return pl.pallas_call(
+        place_kernel,
+        in_specs=[pl.BlockSpec(memory_space=pltpu.SMEM), vmem, vmem],
+        out_specs=vmem,
+        out_shape=jax.ShapeDtypeStruct((64, TOK), BF),
+        compiler_params=params(),
+        name="place_halves",
+    )(h, keep, got).T
+
+
+def cut_kernel(h_ref, t_ref, ga_ref, gf_ref, keep_ref, give_ref):
+    row = lax.broadcasted_iota(jnp.int32, (16, 64), 0)
+    ga, gf = ga_ref[...].astype(F32), gf_ref[...].astype(F32)
+    gains = jnp.where(row == 0, ga, jnp.where(row == 1, gf, 0.0)).astype(BF)
+    keep_ref[HALF:] = gains
+    give_ref[HALF:] = gains
+    first = jnp.transpose(t_ref[:, :HALF])
+    second = jnp.transpose(t_ref[:, HALF:])
+    keep_ref[:HALF] = jnp.where(h_ref[0] == 0, first, second)
+    give_ref[:HALF] = jnp.where(h_ref[0] == 0, second, first)
+
+
+def cut_tokens(h, tokens_t, norm_attn, norm_ffn):
+    vmem = pl.BlockSpec(memory_space=pltpu.VMEM)
+    return pl.pallas_call(
+        cut_kernel,
+        in_specs=[pl.BlockSpec(memory_space=pltpu.SMEM), vmem, vmem, vmem],
+        out_specs=(vmem, vmem),
+        out_shape=(jax.ShapeDtypeStruct((HALF + 16, 64), BF),) * 2,
+        compiler_params=params(),
+        name="cut_tokens",
+    )(h, tokens_t, norm_attn.reshape(1, 64), norm_ffn.reshape(1, 64))
+
+
+def join_kernel(h_ref, keep_ref, got_ref, copies_ref):
+    keep, got = keep_ref[...], got_ref[...]
+    mine_first = jnp.concatenate([keep, got], axis=1)
+    mine_last = jnp.concatenate([got, keep], axis=1)
+    base = jnp.where(h_ref[0] == 0, mine_first, mine_last)
+    for j in range(CHIPS):
+        copies_ref[j] = base
+
+
+def join_copies(h, keep, got):
+    vmem = pl.BlockSpec(memory_space=pltpu.VMEM)
+    return pl.pallas_call(
+        join_kernel,
+        in_specs=[pl.BlockSpec(memory_space=pltpu.SMEM), vmem, vmem],
+        out_specs=vmem,
+        out_shape=jax.ShapeDtypeStruct((CHIPS, HALF + 16, LANE), BF),
+        compiler_params=params(),
+        name="join_copies",
+    )(h, keep, got)
+
+
+def gained_rows(x_ref, g_ref, xs):
+    for j in range(CHIPS):
+        gain = g_ref[j, 1:2].astype(F32)
+        xs[:, j * LANE : (j + 1) * LANE] = (x_ref[j].astype(F32) * gain).astype(BF)
+
+
+def gate_up_main_kernel(h_ref, x_ref, g_ref, wg_ref, wu_ref, *rest):
+    out_ref, xs = rest[-2:]
+    step = pl.program_id(0)
+
+    @pl.when(step == 0)
     def _():
-        acc_g[...] = jnp.zeros_like(acc_g)
-        acc_u[...] = jnp.zeros_like(acc_u)
-        if with_sums:
-            acc_sq[...] = jnp.zeros_like(acc_sq)
-
-    wide, gained = gained_block(x_ref, g_ref, 1)
-    acc_g[...] += nt(gained, wg_ref[...])
-    acc_u[...] += nt(gained, wu_ref[...])
-    if with_sums:
-        acc_sq[...] += fold_squares(wide)
-
-    @pl.when(k == pl.num_programs(0) - 1)
-    def _():
-        half = out_ref.shape[1] // 2
-        if with_sums:
-            high, low = split_two(jnp.sum(acc_sq[...], axis=1, keepdims=True))
-            lane = lax.broadcasted_iota(jnp.int32, (HALF, half - REST), 1)
-            extra = jnp.where(lane == 0, high, jnp.where(lane == 1, low, 0.0))
-            blank = jnp.zeros_like(extra)
-            out_ref[:, :half] = jnp.concatenate([acc_g[...], extra], axis=1).astype(BF)
-            out_ref[:, half:] = jnp.concatenate([acc_u[...], blank], axis=1).astype(BF)
-        else:
-            out_ref[:, :half] = acc_g[...].astype(BF)
-            out_ref[:, half:] = acc_u[...].astype(BF)
-
-
-def gate_up_half(h, x, gains, wg_t, wu_t, with_sums, held=None):
-    depth = 2048 // KSTEP
-    chips = CHIPS // KSTEP
-    at, width, out_width = (MAIN, REST, SIDE) if with_sums else (0, MAIN, 2 * MAIN)
-    weight_spec = pl.BlockSpec((pl.Element(width), pl.Element(depth)), lambda k, h: (at, k * depth))
+        gained_rows(x_ref, g_ref, xs)
+
+    wide = wg_ref.shape[0]
+    at = pl.multiple_of(step * wide, wide)
+    out_ref[:, pl.ds(at, wide)] = nt(xs[...], wg_ref[...]).astype(BF)
+    out_ref[:, pl.ds(MAIN + at, wide)] = nt(xs[...], wu_ref[...]).astype(BF)
+
+
+def gate_up_main(h, x, gains, wg_t, wu_t, held=None):
+    steps = 2
+    wide = MAIN // steps
     in_specs = [
-        pl.BlockSpec((chips, HALF, LANE), lambda k, h: (k, 0, 0)),
-        pl.BlockSpec((chips, 16, LANE), lambda k, h: (k, HALF // 16, 0)),
-        weight_spec,
-        weight_spec,
+        pl.BlockSpec((CHIPS, HALF, LANE), lambda i, h: (0, 0, 0)),
+        pl.BlockSpec((CHIPS, 16, LANE), lambda i, h: (0, HALF // 16, 0)),
+        pl.BlockSpec((wide, 2048), lambda i, h: (i, 0)),
+        pl.BlockSpec((wide, 2048), lambda i, h: (i, 0)),
     ]
     operands = [h, x, gains, wg_t, wu_t]
     aliases = {}
@@ -347,28 +398,69 @@
         in_specs.append(pl.BlockSpec(memory_space=pl.ANY))
         operands.append(held)
         aliases = {5: 0}
-    scratch = [pltpu.VMEM((HALF, width), F32), pltpu.VMEM((HALF, width), F32)]
-    if with_sums:
-        scratch.append(pltpu.VMEM((HALF, LANE), F32))
-    return pl.pallas_call(
-        functools.partial(gate_up_kernel, with_sums),
+    return pl.pallas_call(
+        gate_up_main_kernel,
         grid_spec=pltpu.PrefetchScalarGridSpec(
             num_scalar_prefetch=1,
-            grid=(KSTEP,),
+            grid=(steps,),
             in_specs=in_specs,
-            out_specs=pl.BlockSpec((HALF, out_width), lambda k, h: (h[0], 0)),
-            scratch_shapes=scratch,
-        ),
-        out_shape=jax.ShapeDtypeStruct((TOK, out_width), BF),
+            out_specs=pl.BlockSpec((HALF, 2 * MAIN), lambda i, h: (h[0], 0)),
+            scratch_shapes=[pltpu.VMEM((HALF, 2048), BF)],
+        ),
+        out_shape=jax.ShapeDtypeStruct((TOK, 2 * MAIN), BF),
         input_output_aliases=aliases,
-        compiler_params=params(),
+        compiler_params=params(24),
         cost_estimate=pl.CostEstimate(
-            flops=2 * HALF * 2048 * 2 * width,
-            bytes_accessed=4 * 2048 * width + 2 * 1024 * 1024,
+            flops=4 * HALF * 2048 * MAIN,
+            bytes_accessed=8 * 1024 * 1024,
             transcendentals=0,
         ),
-        name="gate_up_side" if with_sums else "gate_up_main",
+        name="gate_up_main",
     )(*operands)
+
+
+def gate_up_side_kernel(h_ref, own_ref, other_ref, g_ref, wg_ref, wu_ref, out_ref, xs):
+    lane = lax.broadcasted_iota(jnp.int32, (HALF, SIDE // 2 - REST), 1)
+    for x_ref, half in ((own_ref, h_ref[0]), (other_ref, 1 - h_ref[0])):
+        gained_rows(x_ref, g_ref, xs)
+        squares = None
+        for j in range(CHIPS):
+            wide = x_ref[j].astype(F32)
+            squares = wide * wide if squares is None else squares + wide * wide
+        high, low = split_two(jnp.sum(squares, axis=1, keepdims=True))
+        extra = jnp.where(lane == 0, high, jnp.where(lane == 1, low, 0.0))
+        rows = pl.ds(pl.multiple_of(half * HALF, HALF), HALF)
+        gate = jnp.concatenate([nt(xs[...], wg_ref[...]), extra], axis=1)
+        out_ref[rows, : SIDE // 2] = gate.astype(BF)
+        up = jnp.concatenate([nt(xs[...], wu_ref[...]), jnp.zeros_like(extra)], axis=1)
+        out_ref[rows, SIDE // 2 :] = up.astype(BF)
+
+
+def gate_up_side(h, own, other, gains, wg_t, wu_t):
+    x_spec = pl.BlockSpec((CHIPS, HALF, LANE), lambda i, h: (0, 0, 0))
+    w_spec = pl.BlockSpec((pl.Element(REST), pl.Element(2048)), lambda i, h: (MAIN, 0))
+    return pl.pallas_call(
+        gate_up_side_kernel,
+        grid_spec=pltpu.PrefetchScalarGridSpec(
+            num_scalar_prefetch=1,
+            grid=(1,),
+            in_specs=[
+                x_spec,
+                x_spec,
+                pl.BlockSpec((CHIPS, 16, LANE), lambda i, h: (0, HALF // 16, 0)),
+                w_spec,
+                w_spec,
+            ],
+            out_specs=pl.BlockSpec((TOK, SIDE), lambda i, h: (0, 0)),
+            scratch_shapes=[pltpu.VMEM((HALF, 2048), BF)],
+        ),
+        out_shape=jax.ShapeDtypeStruct((TOK, SIDE), BF),
+        compiler_params=params(24),
+        cost_estimate=pl.CostEstimate(
+            flops=4 * TOK * 2048 * REST, bytes_accessed=6 * 1024 * 1024, transcendentals=0
+        ),
+        name="gate_up_side",
+    )(h, own, other, gains, wg_t, wu_t)
 
 
 def hidden_kernel(main_ref, side_ref, out_ref):
@@ -427,20 +519,9 @@
     core = lax.axis_index("gy") % 2
     c = jnp.reshape(core, (1,)).astype(jnp.int32)
 
-    gains = jnp.concatenate([norm_attn[None], norm_ffn[None], jnp.zeros((14, 64), BF)], axis=0)
-
-    def with_gains(start):
-        return jnp.concatenate([lax.dynamic_slice_in_dim(tokens, start, HALF, 0), gains], axis=0)
-
-    mine = with_gains(core * HALF)
-    theirs = swap(with_gains((1 - core) * HALF))
-    base = jnp.where(
-        core == 0,
-        jnp.concatenate([mine, theirs], axis=1),
-        jnp.concatenate([theirs, mine], axis=1),
-    )
-
-    first = over_chips(jnp.broadcast_to(base[None], (CHIPS,) + base.shape))
+    keep, give = cut_tokens(c, tokens.T, norm_attn, norm_ffn)
+    base = join_copies(c, keep, swap(give))
+    first = over_chips(base)
     other = swap(first)
     held = qkv_half(c, first, first, w_query, w_key.T, w_value.T)
     parts = qkv_half(1 - c, other, first, w_query, w_key.T, w_value.T, held)
@@ -452,23 +533,15 @@
     own = over_chips(copies)
     other = swap(own)
     weights = (w_gate.T, w_up.T)
-    held = gate_up_half(c, own, first, *weights, False)
-    main = gate_up_half(1 - c, other, first, *weights, False, held)
+    held = gate_up_main(c, own, first, *weights)
+    main = gate_up_main(1 - c, other, first, *weights, held)
     own, other, later = lax.optimization_barrier((own, other, main))
     main = lax.psum_scatter(later, "gx", scatter_dimension=0, tiled=True)
-    held = gate_up_half(c, own, first, *weights, True)
-    side = gate_up_half(1 - c, other, first, *weights, True, held)
+    side = gate_up_side(c, own, other, first, *weights)
     side = over_rows(side.reshape(ROWS, SEQ, SIDE))
     hidden = over_rows(hidden_copies(main, side)).reshape(TOK, FFL)
-    done = final_sum(residual, project_out(c, hidden, w_down))
-
-    keep = lax.dynamic_slice_in_dim(done, core * 64, 64, 1)
-    got = swap(lax.dynamic_slice_in_dim(done, (1 - core) * 64, 64, 1))
-    return jnp.where(
-        core == 0,
-        jnp.concatenate([keep, got], axis=0),
-        jnp.concatenate([got, keep], axis=0),
-    )
+    keep, give = final_sum(c, residual, project_out(c, hidden, w_down))
+    return place_halves(c, keep, swap(give))
 
 
 def solution(mesh):

time: 316 us -> 309 us (0.978)
  blocking collectives: 198 us -> 225 us
  waiting for transfers between devices: 35 us -> 10.5 us
  Pallas kernels: 36.2 us -> 22.1 us
  local copies, waits for them, and re-layouts: 4.42 us -> 15.6 us
  starting transfers between devices: 24.3 us -> 19.1 us
    all_to_all x3 -> x4, blocking collectives: 76.9 us -> 105 us  [over_chips(): lax.all_to_all(x, 'gy', 0, 0, axis_index_groups=CHIP_GROUPS, tiled=True)]
    all_to_all x1 -> x0, waiting for transfers between devices: 25.6 us -> none  [over_chips(): lax.all_to_all(x, 'gy', 0, 0, axis_index_groups=CHIP_GROUPS, tiled=True)]
    unnamed x26 -> x42, local copies, waits for them, and re-layouts: 2.37 us -> 14.9 us
    pallas_call x5 -> x7, Pallas kernels: 20 us -> 10.3 us  [the longest x2 5.07 us: gate_up_main(): pl.pallas_call(gate_up_main_kernel, grid_spec=pltpu.PrefetchScalarGridSpe...]
    all_to_all x1 -> x0, starting transfers between devices: 5.78 us -> none  [over_chips(): lax.all_to_all(x, 'gy', 0, 0, axis_index_groups=CHIP_GROUPS, tiled=True)]
    pallas_call x4, Pallas kernels: 10.6 us -> 6.14 us  [proj_half(): pl.pallas_call(proj_kernel, grid_spec=pltpu.PrefetchScalarGridSpec(num_sc...]
  transfers between devices with their start and end apart: 9 -> 8, of which waited for: 6 -> 7; matrix products, arithmetic and copies ran while one was open for 0% -> 0% of each run, Pallas kernels for 7% -> 4%
where the time goes in v3:
time: 309 us; the launch traced here: 308 us
  blocking collectives  225 us (73%)
  Pallas kernels  22.1 us (7%)
  starting transfers between devices  19.1 us (6%)
  local copies, waits for them, and re-layouts  15.6 us (5%)
  between operations  14.2 us (5%)
  waiting for transfers between devices  10.5 us (3%)
    all_to_all x4, blocking collectives, over_rows(): return lax.all_to_all(x, 'gx', 0, 0, tiled=True)  120 us
    all_to_all x4, blocking collectives, over_chips(): lax.all_to_all(x, 'gy', 0, 0, axis_index_groups=CHIP_GROUPS, tiled=True)  105 us
    unnamed x42, local copies, waits for them, and re-layouts  14.9 us
    ppermute x6, starting transfers between devices, swap(): return lax.ppermute(x, 'gy', [(i, i ^ 1) for i in range(32)])  14.1 us
    ppermute x6, waiting for transfers between devices, swap(): return lax.ppermute(x, 'gy', [(i, i ^ 1) for i in range(32)])  6.63 us
  transfers between devices with their start and end apart: 8, of which 7 were waited for; matrix products, arithmetic and copies ran while one was open for 0% of the time, Pallas kernels for 4%

profile of v3, /device:TPU:1, one launch (start us, length us, event | category | flops | bytes accessed | tf_op | source)
XLA Modules:
  0.0 307.8 jit_solution(7531345687279856943)
XLA Ops:
  8.9 3.3 %collective-permute-start = (bf16[400,64]{1,0:T(8,128)(2,1)S(1)}, bf16[400,64]{1,0:T(8,128)(2,1)S(1)}, u32[]{:S(2)}, u32[]{:S(2)}) collective-permute-start(bf16[400,64]{1,0:T(8,128)(2,1)S(1)} %get-tuple-element.17), channel_id=1, source_target_pairs={{0,1},{1,0},{2,3},{3,2},{4,5},{5,4},{6,7},{7,6},{8,9},{9,8},{10,11... | collective-permute-start | bytes 153608 | tf_op jit(solution)/shard_map/ppermute | solution.py:38
  13.5 27.6 %all_to_all.45.x_ref.g_ref = bf16[16,400,128]{2,1,0:T(8,128)(2,1)S(1)} all-to-all(bf16[16,400,128]{2,1,0:T(8,128)(2,1)S(1)} %join_copies.1.base_ref), channel_id=1, replica_groups={{0,2,4,6,8,10,12,14,16,18,20,22,24,26,28,30},{1,3,5,7,9,11,13,15,17,19,..., dimensions={0} | all-to-all | bytes 3276800 | tf_op jit(solution)/shard_map/all_to_all | solution.py:42
  42.9 1.9 qkv_half.2.rest_0_
  46.0 1.9 qkv_half.3
  47.9 24.7 %all_to_all.46.p_ref = bf16[8,128,256]{2,1,0:T(8,128)(2,1)S(1)} all-to-all(bf16[8,128,256]{2,1,0:T(8,128)(2,1)S(1)} %qkv_half.3), channel_id=1, replica_groups=mesh['gx'=8,'gy'=32] {'gx'}, dimensions={0} | all-to-all | bytes 1048576 | tf_op jit(solution)/shard_map/all_to_all | solution.py:46
  73.3 5.0 %all-to-all-start.2 = ((f32[8,32,96]{2,1,0:T(8,128)}), f32[8,32,96]{2,1,0:T(8,128)S(1)}, u32[]{:S(2)}, u32[]{:S(2)}) async-start(f32[8,32,96]{2,1,0:T(8,128)} %get-tuple-element.19), calls=%async_computation.2 | async-start | bytes 262144 | tf_op jit(solution)/shard_map/all_to_all | solution.py:529
  79.7 3.9 %all-to-all-done.2.kv_ref = f32[8,32,96]{2,1,0:T(8,128)S(1)} async-done(((f32[8,32,96]{2,1,0:T(8,128)}), f32[8,32,96]{2,1,0:T(8,128)S(1)}, u32[]{:S(2)}, u32[]{:S(2)}) %all-to-all-start.2) | async-done | bytes 98336 | tf_op jit(solution)/shard_map/all_to_all | solution.py:529
  88.1 15.9 %all_to_all.47 = bf16[8,96,256]{2,1,0:T(8,128)(2,1)S(1)} all-to-all(bf16[8,96,256]{2,1,0:T(8,128)(2,1)S(1)} %attend.1), channel_id=1, replica_groups=mesh['gx'=8,'gy'=32] {'gx'}, dimensions={0} | all-to-all | bytes 786432 | tf_op jit(solution)/shard_map/all_to_all | solution.py:46
  104.9 2.2 collective-permute-start.2
  108.0 2.2 collective-permute-done.2
  110.6 24.9 %all_to_all.48.p_ref = bf16[16,384,128]{2,1,0:T(8,128)(2,1)S(1)} all-to-all(bf16[16,384,128]{2,1,0:T(8,128)(2,1)S(1)} %add_convert_fusion.1), channel_id=1, replica_groups={{0,2,4,6,8,10,12,14,16,18,20,22,24,26,28,30},{1,3,5,7,9,11,13,15,17,19,..., dimensions={0} | all-to-all | bytes 3145728 | tf_op jit(solution)/shard_map/all_to_all | solution.py:42
  135.8 24.8 %all_to_all.49.x_ref.own_ref = bf16[16,384,128]{2,1,0:T(8,128)(2,1)S(1)} all-to-all(bf16[16,384,128]{2,1,0:T(8,128)(2,1)S(1)} %get-tuple-element.21), channel_id=1, replica_groups={{0,2,4,6,8,10,12,14,16,18,20,22,24,26,28,30},{1,3,5,7,9,11,13,15,17,19,..., dimensions={0} | all-to-all | bytes 3145728 | tf_op jit(solution)/shard_map/all_to_all | solution.py:42
  160.6 2.3 collective-permute-start.3
  162.9 2.5 gate_up_main.2.rest_0_
  166.0 2.5 gate_up_main.3
  170.9 2.0 copy-done.1
  172.8 2.0 copy-done.3
  176.3 3.8 %gate_up_side.1 = bf16[768,768]{1,0:T(8,128)(2,1)S(1)} custom-call(s32[1]{0:T(128)} %bitcast.h_ref, bf16[16,384,128]{2,1,0:T(8,128)(2,1)S(1)} %all_to_all.49.x_ref.own_ref, bf16[16,384,128]{2,1,0:T(8,128)(2,1)S(1)} %copy-done.7, bf16[16,400,128]{2,1,0:T(8,128)(2,1)S(1)} %all_to_all.45.x_ref.g_ref, bf16[832,2048]{1,0:T(8,128)(2,1)S(1)} %bitcast.16, ...), custom_call_target="tpu_custom_call" | custom-call | flops 2013265920 | bytes 6291456 | tf_op jit(solution)/shard_map/gate_up_side/pallas_call | solution.py:442
  180.0 43.1 %all_to_all.50.side_ref = bf16[8,96,768]{2,1,0:T(8,128)(2,1)S(1)} all-to-all(bf16[8,96,768]{2,1,0:T(8,128)(2,1)S(1)} %bitcast.22), channel_id=1, replica_groups=mesh['gx'=8,'gy'=32] {'gx'}, dimensions={0} | all-to-all | bytes 2359296 | tf_op jit(solution)/shard_map/all_to_all | solution.py:46
  224.4 36.8 %all_to_all.51 = bf16[8,96,832]{2,1,0:T(8,128)(2,1)S(1)} all-to-all(bf16[8,96,832]{2,1,0:T(8,128)(2,1)S(1)} %hidden_copies.1), channel_id=1, replica_groups=mesh['gx'=8,'gy'=32] {'gx'}, dimensions={0} | all-to-all | bytes 2555904 | tf_op jit(solution)/shard_map/all_to_all | solution.py:46
  261.2 2.2 proj_half.7
  263.4 2.6 collective-permute-start.4
  266.0 2.2 proj_half.6
  269.5 27.6 %all_to_all.52.p_ref = bf16[16,384,128]{2,1,0:T(8,128)(2,1)S(1)} all-to-all(bf16[16,384,128]{2,1,0:T(8,128)(2,1)S(1)} %add_convert_fusion), channel_id=1, replica_groups={{0,2,4,6,8,10,12,14,16,18,20,22,24,26,28,30},{1,3,5,7,9,11,13,15,17,19,..., dimensions={0} | all-to-all | bytes 3145728 | tf_op jit(solution)/shard_map/all_to_all | solution.py:42
  (63 shorter events, 25.6 us)
Async XLA Ops:
  6.5 0.9 copy-start.13
  8.9 4.3 %collective-permute-start = (bf16[400,64]{1,0:T(8,128)(2,1)S(1)}, bf16[400,64]{1,0:T(8,128)(2,1)S(1)}, u32[]{:S(2)}, u32[]{:S(2)}) collective-permute-start(bf16[400,64]{1,0:T(8,128)(2,1)S(1)} %get-tuple-element.17), channel_id=1, source_target_pairs={{0,1},{1,0},{2,3},{3,2},{4,5},{5,4},{6,7},{7,6},{8,9},{9,8},{10,11... | collective-permute-start | bytes 153608 | tf_op jit(solution)/shard_map/ppermute | solution.py:38
  13.4 29.4 %copy-start.9 = (bf16[2048,256]{1,0:T(8,128)(2,1)S(1)}, bf16[2048,256]{1,0:T(8,128)(2,1)}, u32[]{:S(2)}) copy-start(bf16[2048,256]{1,0:T(8,128)(2,1)} %wq_ref.3) | copy-start | bytes 3145732
  13.5 29.4 %copy-start.10 = (bf16[2048,16]{0,1:T(8,128)(2,1)S(1)}, bf16[2048,16]{0,1:T(8,128)(2,1)}, u32[]{:S(2)}) copy-start(bf16[2048,16]{0,1:T(8,128)(2,1)} %param.19) | copy-start | bytes 196612
  13.5 29.4 %copy-start.11 = (bf16[2048,16]{0,1:T(8,128)(2,1)S(1)}, bf16[2048,16]{0,1:T(8,128)(2,1)}, u32[]{:S(2)}) copy-start(bf16[2048,16]{0,1:T(8,128)(2,1)} %param.20) | copy-start | bytes 196612
  41.1 4.9 %collective-permute-start.1 = (bf16[16,400,128]{2,1,0:T(8,128)(2,1)S(1)}, bf16[16,400,128]{2,1,0:T(8,128)(2,1)S(1)}, u32[]{:S(2)}, u32[]{:S(2)}) collective-permute-start(bf16[16,400,128]{2,1,0:T(8,128)(2,1)S(1)} %all_to_all.45.x_ref.g_ref), channel_id=1, source_target_pairs={{0,1},{1,0},{2,3},{3,2},{4,5},{5,4},{6,7},{7,6},{8,9},{9,8},{10,11... | collective-permute-start | bytes 4915208 | tf_op jit(solution)/shard_map/ppermute | solution.py:38
  73.3 10.3 %all-to-all-start.2 = ((f32[8,32,96]{2,1,0:T(8,128)}), f32[8,32,96]{2,1,0:T(8,128)S(1)}, u32[]{:S(2)}, u32[]{:S(2)}) async-start(f32[8,32,96]{2,1,0:T(8,128)} %get-tuple-element.19), calls=%async_computation.2 | async-start | bytes 262144 | tf_op jit(solution)/shard_map/all_to_all | solution.py:529
  78.3 144.9 %reduce-scatter.2.cloned.1.call-start = ((), (), s32[]{:S(2)}) async-start(), calls=%async_computation.10 | async-start | bytes 1769472 | tf_op jit(solution)/shard_map/reduce_scatter | solution.py:539
  83.6 20.5 %copy-start.8 = (bf16[256,2048]{1,0:T(8,128)(2,1)S(1)}, bf16[256,2048]{1,0:T(8,128)(2,1)}, u32[]{:S(2)}) copy-start(bf16[256,2048]{1,0:T(8,128)(2,1)} %w_ref.5) | copy-start | bytes 3145732
  83.6 0.9 copy-start.14
  84.5 0.8 copy-start.15
  104.9 5.2 %collective-permute-start.2 = (bf16[16,384,128]{2,1,0:T(8,128)(2,1)S(1)}, bf16[16,384,128]{2,1,0:T(8,128)(2,1)S(1)}, u32[]{:S(2)}, u32[]{:S(2)}) collective-permute-start(bf16[16,384,128]{2,1,0:T(8,128)(2,1)S(1)} %proj_half.5), channel_id=1, source_target_pairs={{0,1},{1,0},{2,3},{3,2},{4,5},{5,4},{6,7},{7,6},{8,9},{9,8},{10,11... | collective-permute-start | bytes 4718600 | tf_op jit(solution)/shard_map/ppermute | solution.py:38
  110.6 52.3 %copy-start.2 = (bf16[2048,832]{0,1:T(8,128)(2,1)S(1)}, bf16[2048,832]{0,1:T(8,128)(2,1)}, u32[]{:S(2)}) copy-start(bf16[2048,832]{0,1:T(8,128)(2,1)} %param.24) | copy-start | bytes 10223620
  135.5 27.5 %copy-start = (bf16[2048,832]{0,1:T(8,128)(2,1)S(1)}, bf16[2048,832]{0,1:T(8,128)(2,1)}, u32[]{:S(2)}) copy-start(bf16[2048,832]{0,1:T(8,128)(2,1)} %param.23) | copy-start | bytes 10223620
  160.6 5.4 %collective-permute-start.3 = (bf16[16,384,128]{2,1,0:T(8,128)(2,1)S(1)}, bf16[16,384,128]{2,1,0:T(8,128)(2,1)S(1)}, u32[]{:S(2)}, u32[]{:S(2)}) collective-permute-start(bf16[16,384,128]{2,1,0:T(8,128)(2,1)S(1)} %all_to_all.49.x_ref.own_ref), channel_id=1, source_target_pairs={{0,1},{1,0},{2,3},{3,2},{4,5},{5,4},{6,7},{7,6},{8,9},{9,8},{10,11... | collective-permute-start | bytes 4718600 | tf_op jit(solution)/shard_map/ppermute | solution.py:38
  168.5 1.2 copy-start.4
  169.7 1.1 copy-start.6
  170.9 2.0 copy-start.1
  172.8 2.0 copy-start.3
  174.8 1.4 copy-start.7
  223.2 0.9 copy-start.12
  224.1 37.1 %copy-start.5 = (bf16[832,2048]{1,0:T(8,128)(2,1)S(1)}, bf16[832,2048]{1,0:T(8,128)(2,1)}, u32[]{:S(2)}) copy-start(bf16[832,2048]{1,0:T(8,128)(2,1)} %w_ref.7) | copy-start | bytes 10223620
  263.4 5.7 %collective-permute-start.4 = (bf16[16,384,128]{2,1,0:T(8,128)(2,1)S(1)}, bf16[16,384,128]{2,1,0:T(8,128)(2,1)S(1)}, u32[]{:S(2)}, u32[]{:S(2)}) collective-permute-start(bf16[16,384,128]{2,1,0:T(8,128)(2,1)S(1)} %proj_half.7), channel_id=1, source_target_pairs={{0,1},{1,0},{2,3},{3,2},{4,5},{5,4},{6,7},{7,6},{8,9},{9,8},{10,11... | collective-permute-start | bytes 4718600 | tf_op jit(solution)/shard_map/ppermute | solution.py:38
  297.4 2.8 collective-permute-start.5
  (5 other events, 3.6 us)
Sparse Core Ops, SparseCore 0:
  171.0 46.1 reduce-scatter.1

commit v4 on v3

--- a/solution.py
+++ b/solution.py
@@ -27,9 +27,9 @@
 ROWS = 8
 KSTEP = 4
 FFL = 832
-MAIN = 512
+MAIN = 640
 REST = FFL - MAIN
-SIDE = 768
+SIDE = 512
 CHIP_GROUPS = [[2 * i + c for i in range(CHIPS)] for c in range(2)]
 KV_GROUPS = [list(range(8 * i, 8 * i + 8)) for i in range(4)]
 
@@ -173,20 +173,24 @@
     )(parts)
 
 
-def attend_kernel(
-    len_ref, q_ref, kv_ref, segr_ref, segc_ref, cos_ref, sin_ref, cost_ref, sint_ref, out_ref
-):
+def attend_kernel(len_ref, q_ref, kv_ref, seg_ref, table_ref, out_ref):
+    cos, sin = table_ref[0], table_ref[1]
+    cos_t, sin_t = jnp.transpose(cos)[:, :SEQ], jnp.transpose(sin)[:, :SEQ]
+    cos, sin = cos[:SEQ], sin[:SEQ]
     keys = jnp.concatenate([kv_ref[j, :16] for j in range(8)], axis=0)
     turned = jnp.concatenate([keys[64:], keys[:64]], axis=0)
-    keys = (keys * cost_ref[...] + turned * sint_ref[...]).astype(BF)
+    keys = (keys * cos_t + turned * sin_t).astype(BF)
     values = jnp.concatenate([kv_ref[j, 16:] for j in range(8)], axis=0).astype(BF)
+    seg = jnp.concatenate([seg_ref[...].astype(F32), jnp.zeros((1, LANE - SEQ), F32)], axis=1)
+    seg = jnp.broadcast_to(seg, (LANE, LANE))
+    same = (seg == jnp.transpose(seg))[:SEQ, :SEQ]
     q_at = lax.broadcasted_iota(jnp.int32, (SEQ, SEQ), 0)
     k_at = lax.broadcasted_iota(jnp.int32, (SEQ, SEQ), 1)
-    allowed = (segr_ref[...] == segc_ref[...]) & (k_at <= q_at) & (k_at < len_ref[0])
+    allowed = same & (k_at <= q_at) & (k_at < len_ref[0])
     allowed = allowed | (k_at == q_at)
     for head in range(2):
         query = q_ref[:, head * HEAD_DIM : (head + 1) * HEAD_DIM]
-        query = (query * cos_ref[...] + pltpu.roll(query, 64, 1) * sin_ref[...]).astype(BF)
+        query = (query * cos + pltpu.roll(query, 64, 1) * sin).astype(BF)
         scores = nn(query, keys) * (1.0 / math.sqrt(HEAD_DIM))
         scores = jnp.where(allowed, scores, F32(-1e30))
         expo = jnp.exp(scores - jnp.max(scores, axis=1, keepdims=True))
@@ -197,26 +201,15 @@
 
 
 def attend(lengths, q, kv, segments):
-    cos, sin = rope_tables()
     vmem = pl.BlockSpec(memory_space=pltpu.VMEM)
     return pl.pallas_call(
         attend_kernel,
-        in_specs=[pl.BlockSpec(memory_space=pltpu.SMEM)] + [vmem] * 8,
+        in_specs=[pl.BlockSpec(memory_space=pltpu.SMEM)] + [vmem] * 4,
         out_specs=vmem,
         out_shape=jax.ShapeDtypeStruct((ROWS, SEQ, 256), BF),
         compiler_params=params(),
         name="attend",
-    )(
-        lengths,
-        q,
-        kv,
-        segments.reshape(1, SEQ),
-        segments.reshape(SEQ, 1),
-        cos,
-        sin,
-        np.ascontiguousarray(cos.T),
-        np.ascontiguousarray(sin.T),
-    )
+    )(lengths, q, kv, segments.reshape(1, SEQ), rope_table())
 
 
 def proj_kernel(h_ref, x_ref, w_ref, out_ref):
@@ -331,11 +324,17 @@
 
 
 def cut_tokens(h, tokens_t, norm_attn, norm_ffn):
-    vmem = pl.BlockSpec(memory_space=pltpu.VMEM)
+    whole = lambda *shape: pl.BlockSpec(shape, lambda i: (0, 0))
     return pl.pallas_call(
         cut_kernel,
-        in_specs=[pl.BlockSpec(memory_space=pltpu.SMEM), vmem, vmem, vmem],
-        out_specs=(vmem, vmem),
+        grid=(1,),
+        in_specs=[
+            pl.BlockSpec(memory_space=pltpu.SMEM),
+            whole(64, TOK),
+            whole(1, 64),
+            whole(1, 64),
+        ],
+        out_specs=(whole(HALF + 16, 64), whole(HALF + 16, 64)),
         out_shape=(jax.ShapeDtypeStruct((HALF + 16, 64), BF),) * 2,
         compiler_params=params(),
         name="cut_tokens",
@@ -384,7 +383,7 @@
 
 
 def gate_up_main(h, x, gains, wg_t, wu_t, held=None):
-    steps = 2
+    steps = 1
     wide = MAIN // steps
     in_specs = [
         pl.BlockSpec((CHIPS, HALF, LANE), lambda i, h: (0, 0, 0)),
@@ -419,7 +418,7 @@
     )(*operands)
 
 
-def gate_up_side_kernel(h_ref, own_ref, other_ref, g_ref, wg_ref, wu_ref, out_ref, xs):
+def gate_up_side_kernel(h_ref, own_ref, other_ref, g_ref, wg_ref, wu_ref, _, out_ref, xs):
     lane = lax.broadcasted_iota(jnp.int32, (HALF, SIDE // 2 - REST), 1)
     for x_ref, half in ((own_ref, h_ref[0]), (other_ref, 1 - h_ref[0])):
         gained_rows(x_ref, g_ref, xs)
@@ -436,7 +435,7 @@
         out_ref[rows, SIDE // 2 :] = up.astype(BF)
 
 
-def gate_up_side(h, own, other, gains, wg_t, wu_t):
+def gate_up_side(h, own, other, gains, wg_t, wu_t, main):
     x_spec = pl.BlockSpec((CHIPS, HALF, LANE), lambda i, h: (0, 0, 0))
     w_spec = pl.BlockSpec((pl.Element(REST), pl.Element(2048)), lambda i, h: (MAIN, 0))
     return pl.pallas_call(
@@ -450,6 +449,7 @@
                 pl.BlockSpec((CHIPS, 16, LANE), lambda i, h: (0, HALF // 16, 0)),
                 w_spec,
                 w_spec,
+                pl.BlockSpec(memory_space=pl.ANY),
             ],
             out_specs=pl.BlockSpec((TOK, SIDE), lambda i, h: (0, 0)),
             scratch_shapes=[pltpu.VMEM((HALF, 2048), BF)],
@@ -460,7 +460,7 @@
             flops=4 * TOK * 2048 * REST, bytes_accessed=6 * 1024 * 1024, transcendentals=0
         ),
         name="gate_up_side",
-    )(h, own, other, gains, wg_t, wu_t)
+    )(h, own, other, gains, wg_t, wu_t, main)
 
 
 def hidden_kernel(main_ref, side_ref, out_ref):
@@ -476,30 +476,58 @@
 
     first = gated(main_ref[:, :MAIN].astype(F32), main_ref[:, MAIN:].astype(F32))
     second = gated(side[:, :REST], side[:, SIDE // 2 : SIDE // 2 + REST])
-    for j in range(ROWS):
-        out_ref[j, :, :MAIN] = first
-        out_ref[j, :, MAIN:] = second
-
-
-def hidden_copies(main, side):
+    out_ref[:, :MAIN] = first
+    out_ref[:, MAIN:] = second
+
+
+def hidden_row(main, side):
     return pl.pallas_call(
         hidden_kernel,
-        out_shape=jax.ShapeDtypeStruct((ROWS, SEQ, FFL), BF),
-        compiler_params=params(),
-        name="hidden_copies",
+        out_shape=jax.ShapeDtypeStruct((SEQ, FFL), BF),
+        compiler_params=params(),
+        name="hidden_row",
     )(main, side)
 
 
-def rope_tables():
+def from_ahead(x, k):
+    return lax.ppermute(x, "gx", [(i, (i - k) % ROWS) for i in range(ROWS)])
+
+
+def order_kernel(at_ref, *refs):
+    out_ref = refs[-1]
+    for k, ref in enumerate(refs[:-1]):
+        out_ref[lax.rem(at_ref[0] + k, ROWS)] = ref[...]
+
+
+def all_rows(x):
+    ahead = {0: x}
+    for k in (1, 7, 3, 5):
+        ahead[k] = from_ahead(x, k)
+    ahead[2] = from_ahead(ahead[1], 1)
+    ahead[6] = from_ahead(ahead[7], 7)
+    ahead[4] = from_ahead(ahead[3], 1)
+    vmem = pl.BlockSpec(memory_space=pltpu.VMEM)
+    at = jnp.reshape(lax.axis_index("gx"), (1,)).astype(jnp.int32)
+    return pl.pallas_call(
+        order_kernel,
+        in_specs=[pl.BlockSpec(memory_space=pltpu.SMEM)] + [vmem] * ROWS,
+        out_specs=vmem,
+        out_shape=jax.ShapeDtypeStruct((ROWS,) + x.shape, x.dtype),
+        compiler_params=params(),
+        name="order_rows",
+    )(at, *[ahead[k] for k in range(ROWS)])
+
+
+def rope_table():
     inv_freq = np.power(
         np.float32(ROPE_BASE), -(np.arange(64, dtype=np.float32) * np.float32(2.0 / HEAD_DIM))
     ).astype(np.float32)
-    angles = np.arange(SEQ, dtype=np.float32)[:, None] * inv_freq[None, :]
-    cos, sin = np.cos(angles.astype(np.float64)), np.sin(angles.astype(np.float64))
-    return (
-        np.concatenate([cos, cos], axis=1).astype(np.float32),
-        np.concatenate([-sin, sin], axis=1).astype(np.float32),
-    )
+    angles = (np.arange(SEQ, dtype=np.float32)[:, None] * inv_freq[None, :]).astype(np.float64)
+    cos, sin = np.cos(angles), np.sin(angles)
+    table = np.zeros((2, LANE, LANE), np.float32)
+    table[0, :SEQ] = np.concatenate([cos, cos], axis=1)
+    table[1, :SEQ] = np.concatenate([-sin, sin], axis=1)
+    return table
 
 
 def per_device(
@@ -535,11 +563,10 @@
     weights = (w_gate.T, w_up.T)
     held = gate_up_main(c, own, first, *weights)
     main = gate_up_main(1 - c, other, first, *weights, held)
-    own, other, later = lax.optimization_barrier((own, other, main))
-    main = lax.psum_scatter(later, "gx", scatter_dimension=0, tiled=True)
-    side = gate_up_side(c, own, other, first, *weights)
+    side = gate_up_side(c, own, other, first, *weights, main)
+    main = lax.psum_scatter(main, "gx", scatter_dimension=0, tiled=True)
     side = over_rows(side.reshape(ROWS, SEQ, SIDE))
-    hidden = over_rows(hidden_copies(main, side)).reshape(TOK, FFL)
+    hidden = all_rows(hidden_row(main, side)).reshape(TOK, FFL)
     keep, give = final_sum(c, residual, project_out(c, hidden, w_down))
     return place_halves(c, keep, swap(give))
 

time: 309 us -> 292 us (0.945)
  blocking collectives: 225 us -> 182 us
  starting transfers between devices: 19.1 us -> 36.3 us
  waiting for transfers between devices: 10.5 us -> 19.6 us
    all_to_all x4 -> x3, blocking collectives: 120 us -> 75.2 us  [over_rows(): return lax.all_to_all(x, 'gx', 0, 0, tiled=True)]
    ppermute x0 -> x7, starting transfers between devices: none -> 17.5 us  [from_ahead(): return lax.ppermute(x, 'gx', [(i, (i - k) % ROWS) for i in range(ROWS)])]
    ppermute x0 -> x7, waiting for transfers between devices: none -> 8.41 us  [from_ahead(): return lax.ppermute(x, 'gx', [(i, (i - k) % ROWS) for i in range(ROWS)])]
    unnamed x42 -> x44, local copies, waits for them, and re-layouts: 14.9 us -> 15.3 us
  transfers between devices with their start and end apart: 8 -> 15, of which waited for: 7 -> 11; matrix products, arithmetic and copies ran while one was open for 0% -> 0% of each run, Pallas kernels for 4% -> 3%
where the time goes in v4:
time: 292 us
  blocking collectives  182 us (62%)
  starting transfers between devices  36.3 us (12%)
  Pallas kernels  23.2 us (8%)
  waiting for transfers between devices  19.6 us (7%)
  local copies, waits for them, and re-layouts  15.3 us (5%)
  between operations  14.3 us (5%)
    all_to_all x4, blocking collectives, over_chips(): lax.all_to_all(x, 'gy', 0, 0, axis_index_groups=CHIP_GROUPS, tiled=True)  107 us
    all_to_all x3, blocking collectives, over_rows(): return lax.all_to_all(x, 'gx', 0, 0, tiled=True)  75.2 us
    ppermute x7, starting transfers between devices, from_ahead(): return lax.ppermute(x, 'gx', [(i, (i - k) % ROWS) for i in range(ROWS)])  17.5 us
    unnamed x44, local copies, waits for them, and re-layouts  15.3 us
    ppermute x6, starting transfers between devices, swap(): return lax.ppermute(x, 'gy', [(i, i ^ 1) for i in range(32)])  13.8 us
    ppermute x7, waiting for transfers between devices, from_ahead(): return lax.ppermute(x, 'gx', [(i, (i - k) % ROWS) for i in range(ROWS)])  8.41 us
    ppermute x6, waiting for transfers between devices, swap(): return lax.ppermute(x, 'gy', [(i, i ^ 1) for i in range(32)])  6.48 us
    pallas_call x4, Pallas kernels, proj_half(): pl.pallas_call(proj_kernel, grid_spec=pltpu.PrefetchScalarGridSpec(num_sc...  6.15 us
  transfers between devices with their start and end apart: 15, of which 11 were waited for; matrix products, arithmetic and copies ran while one was open for 0% of the time, Pallas kernels for 3%

profile of v4, /device:TPU:1, one launch (start us, length us, event | category | flops | bytes accessed | tf_op | source)
XLA Modules:
  0.0 291.5 jit_solution(1408770625630881012)
XLA Ops:
  8.9 3.3 %collective-permute-start = (bf16[400,64]{1,0:T(8,128)(2,1)S(1)}, bf16[400,64]{1,0:T(8,128)(2,1)S(1)}, u32[]{:S(2)}, u32[]{:S(2)}) collective-permute-start(bf16[400,64]{1,0:T(8,128)(2,1)S(1)} %get-tuple-element.14), channel_id=1, source_target_pairs={{0,1},{1,0},{2,3},{3,2},{4,5},{5,4},{6,7},{7,6},{8,9},{9,8},{10,11... | collective-permute-start | bytes 153608 | tf_op jit(solution)/shard_map/ppermute | solution.py:38
  13.5 27.6 %all_to_all.40.x_ref.g_ref = bf16[16,400,128]{2,1,0:T(8,128)(2,1)S(1)} all-to-all(bf16[16,400,128]{2,1,0:T(8,128)(2,1)S(1)} %join_copies.1.base_ref), channel_id=1, replica_groups={{0,2,4,6,8,10,12,14,16,18,20,22,24,26,28,30},{1,3,5,7,9,11,13,15,17,19,..., dimensions={0} | all-to-all | bytes 3276800 | tf_op jit(solution)/shard_map/all_to_all | solution.py:42
  47.9 24.8 %all_to_all.41.p_ref = bf16[8,128,256]{2,1,0:T(8,128)(2,1)S(1)} all-to-all(bf16[8,128,256]{2,1,0:T(8,128)(2,1)S(1)} %qkv_half.3), channel_id=1, replica_groups=mesh['gx'=8,'gy'=32] {'gx'}, dimensions={0} | all-to-all | bytes 1048576 | tf_op jit(solution)/shard_map/all_to_all | solution.py:46
  74.0 5.1 %all-to-all-start.2 = ((f32[8,32,96]{2,1,0:T(8,128)}), f32[8,32,96]{2,1,0:T(8,128)S(1)}, u32[]{:S(2)}, u32[]{:S(2)}) async-start(f32[8,32,96]{2,1,0:T(8,128)} %get-tuple-element.16), calls=%async_computation.2 | async-start | bytes 262144 | tf_op jit(solution)/shard_map/all_to_all | solution.py:557
  79.7 4.6 %all-to-all-done.2.kv_ref = f32[8,32,96]{2,1,0:T(8,128)S(1)} async-done(((f32[8,32,96]{2,1,0:T(8,128)}), f32[8,32,96]{2,1,0:T(8,128)S(1)}, u32[]{:S(2)}, u32[]{:S(2)}) %all-to-all-start.2) | async-done | bytes 98336 | tf_op jit(solution)/shard_map/all_to_all | solution.py:557
  86.0 15.9 %all_to_all.42 = bf16[8,96,256]{2,1,0:T(8,128)(2,1)S(1)} all-to-all(bf16[8,96,256]{2,1,0:T(8,128)(2,1)S(1)} %attend.1), channel_id=1, replica_groups=mesh['gx'=8,'gy'=32] {'gx'}, dimensions={0} | all-to-all | bytes 786432 | tf_op jit(solution)/shard_map/all_to_all | solution.py:46
  102.8 2.2 collective-permute-start.2
  105.8 2.2 collective-permute-done.2
  108.4 24.9 %all_to_all.43.p_ref = bf16[16,384,128]{2,1,0:T(8,128)(2,1)S(1)} all-to-all(bf16[16,384,128]{2,1,0:T(8,128)(2,1)S(1)} %add_convert_fusion.1), channel_id=1, replica_groups={{0,2,4,6,8,10,12,14,16,18,20,22,24,26,28,30},{1,3,5,7,9,11,13,15,17,19,..., dimensions={0} | all-to-all | bytes 3145728 | tf_op jit(solution)/shard_map/all_to_all | solution.py:42
  133.6 24.8 %all_to_all.44.x_ref.own_ref = bf16[16,384,128]{2,1,0:T(8,128)(2,1)S(1)} all-to-all(bf16[16,384,128]{2,1,0:T(8,128)(2,1)S(1)} %get-tuple-element.18), channel_id=1, replica_groups={{0,2,4,6,8,10,12,14,16,18,20,22,24,26,28,30},{1,3,5,7,9,11,13,15,17,19,..., dimensions={0} | all-to-all | bytes 3145728 | tf_op jit(solution)/shard_map/all_to_all | solution.py:42
  158.4 2.3 collective-permute-start.3
  160.8 2.7 gate_up_main.2.rest_0_
  163.8 2.7 gate_up_main.3._
  172.5 2.0 copy-done.5
  175.9 2.5 gate_up_side.1
  178.3 34.5 %all_to_all.45.side_ref = bf16[8,96,512]{2,1,0:T(8,128)(2,1)} all-to-all(bf16[8,96,512]{2,1,0:T(8,128)(2,1)S(1)} %bitcast.24), channel_id=1, replica_groups=mesh['gx'=8,'gy'=32] {'gx'}, dimensions={0} | all-to-all | bytes 1572864 | tf_op jit(solution)/shard_map/all_to_all | solution.py:46
  217.1 2.2 collective-permute-start.6
  223.9 8.4 %collective-permute-start.7 = (bf16[96,832]{1,0:T(8,128)(2,1)}, bf16[96,832]{1,0:T(8,128)(2,1)}, u32[]{:S(2)}, u32[]{:S(2)}) collective-permute-start(bf16[96,832]{1,0:T(8,128)(2,1)} %collective-permute-done.6.refs_3_), channel_id=1, source_target_pairs={{0,224},{32,0},{64,32},{96,64},{128,96},{160,128},{192,160},{224,1... | collective-permute-start | bytes 479240 | tf_op jit(solution)/shard_map/ppermute | solution.py:493
  236.0 3.5 %collective-permute-done.10.refs_6_ = bf16[96,832]{1,0:T(8,128)(2,1)} collective-permute-done((bf16[96,832]{1,0:T(8,128)(2,1)}, bf16[96,832]{1,0:T(8,128)(2,1)}, u32[]{:S(2)}, u32[]{:S(2)}) %collective-permute-start.10) | collective-permute-done | bytes 159776 | tf_op jit(solution)/shard_map/ppermute | solution.py:493
  239.5 2.3 collective-permute-done.5.refs_2_
  243.3 2.2 proj_half.7
  245.6 2.3 collective-permute-start.11
  247.9 2.2 proj_half.6
  251.3 29.5 %all_to_all.46.p_ref = bf16[16,384,128]{2,1,0:T(8,128)(2,1)S(1)} all-to-all(bf16[16,384,128]{2,1,0:T(8,128)(2,1)S(1)} %add_convert_fusion), channel_id=1, replica_groups={{0,2,4,6,8,10,12,14,16,18,20,22,24,26,28,30},{1,3,5,7,9,11,13,15,17,19,..., dimensions={0} | all-to-all | bytes 3145728 | tf_op jit(solution)/shard_map/all_to_all | solution.py:42
  (78 shorter events, 42.6 us)
Async XLA Ops:
  8.9 4.3 %collective-permute-start = (bf16[400,64]{1,0:T(8,128)(2,1)S(1)}, bf16[400,64]{1,0:T(8,128)(2,1)S(1)}, u32[]{:S(2)}, u32[]{:S(2)}) collective-permute-start(bf16[400,64]{1,0:T(8,128)(2,1)S(1)} %get-tuple-element.14), channel_id=1, source_target_pairs={{0,1},{1,0},{2,3},{3,2},{4,5},{5,4},{6,7},{7,6},{8,9},{9,8},{10,11... | collective-permute-start | bytes 153608 | tf_op jit(solution)/shard_map/ppermute | solution.py:38
  13.4 29.4 %copy-start.10 = (bf16[2048,256]{1,0:T(8,128)(2,1)S(1)}, bf16[2048,256]{1,0:T(8,128)(2,1)}, u32[]{:S(2)}) copy-start(bf16[2048,256]{1,0:T(8,128)(2,1)} %wq_ref.3) | copy-start | bytes 3145732
  13.5 29.4 %copy-start.12 = (bf16[2048,16]{0,1:T(8,128)(2,1)S(1)}, bf16[2048,16]{0,1:T(8,128)(2,1)}, u32[]{:S(2)}) copy-start(bf16[2048,16]{0,1:T(8,128)(2,1)} %param.16) | copy-start | bytes 196612
  13.5 29.4 %copy-start.13 = (bf16[2048,16]{0,1:T(8,128)(2,1)S(1)}, bf16[2048,16]{0,1:T(8,128)(2,1)}, u32[]{:S(2)}) copy-start(bf16[2048,16]{0,1:T(8,128)(2,1)} %param.17) | copy-start | bytes 196612
  41.1 4.9 %collective-permute-start.1 = (bf16[16,400,128]{2,1,0:T(8,128)(2,1)S(1)}, bf16[16,400,128]{2,1,0:T(8,128)(2,1)S(1)}, u32[]{:S(2)}, u32[]{:S(2)}) collective-permute-start(bf16[16,400,128]{2,1,0:T(8,128)(2,1)S(1)} %all_to_all.40.x_ref.g_ref), channel_id=1, source_target_pairs={{0,1},{1,0},{2,3},{3,2},{4,5},{5,4},{6,7},{7,6},{8,9},{9,8},{10,11... | collective-permute-start | bytes 4915208 | tf_op jit(solution)/shard_map/ppermute | solution.py:38
  47.9 36.5 %copy-start.15 = (f32[2,128,128]{2,1,0:T(8,128)S(1)}, f32[2,128,128]{2,1,0:T(8,128)}, u32[]{:S(2)}) copy-start(f32[2,128,128]{2,1,0:T(8,128)} %constant.26.clone.table_ref) | copy-start | bytes 393220
  47.9 36.5 %copy-start.21 = (s32[96]{0:T(128)S(1)}, s32[96]{0:T(128)}, u32[]{:S(2)}) copy-start(s32[96]{0:T(128)} %param.24) | copy-start | bytes 1156
  74.0 10.4 %all-to-all-start.2 = ((f32[8,32,96]{2,1,0:T(8,128)}), f32[8,32,96]{2,1,0:T(8,128)S(1)}, u32[]{:S(2)}, u32[]{:S(2)}) async-start(f32[8,32,96]{2,1,0:T(8,128)} %get-tuple-element.16), calls=%async_computation.2 | async-start | bytes 262144 | tf_op jit(solution)/shard_map/all_to_all | solution.py:557
  79.1 133.8 %reduce-scatter.2.cloned.1.call-start = ((), (), s32[]{:S(2)}) async-start(), calls=%async_computation.9 | async-start | bytes 2211840 | tf_op jit(solution)/shard_map/reduce_scatter | solution.py:567
  84.4 17.5 %copy-start.9 = (bf16[256,2048]{1,0:T(8,128)(2,1)S(1)}, bf16[256,2048]{1,0:T(8,128)(2,1)}, u32[]{:S(2)}) copy-start(bf16[256,2048]{1,0:T(8,128)(2,1)} %w_ref.5) | copy-start | bytes 3145732
  102.8 5.2 %collective-permute-start.2 = (bf16[16,384,128]{2,1,0:T(8,128)(2,1)S(1)}, bf16[16,384,128]{2,1,0:T(8,128)(2,1)S(1)}, u32[]{:S(2)}, u32[]{:S(2)}) collective-permute-start(bf16[16,384,128]{2,1,0:T(8,128)(2,1)S(1)} %proj_half.5), channel_id=1, source_target_pairs={{0,1},{1,0},{2,3},{3,2},{4,5},{5,4},{6,7},{7,6},{8,9},{9,8},{10,11... | collective-permute-start | bytes 4718600 | tf_op jit(solution)/shard_map/ppermute | solution.py:38
  108.4 52.4 %copy-start.4 = (bf16[2048,832]{0,1:T(8,128)(2,1)S(1)}, bf16[2048,832]{0,1:T(8,128)(2,1)}, u32[]{:S(2)}) copy-start(bf16[2048,832]{0,1:T(8,128)(2,1)} %param.21) | copy-start | bytes 10223620
  133.3 27.5 %copy-start.2 = (bf16[2048,832]{0,1:T(8,128)(2,1)S(1)}, bf16[2048,832]{0,1:T(8,128)(2,1)}, u32[]{:S(2)}) copy-start(bf16[2048,832]{0,1:T(8,128)(2,1)} %param.20) | copy-start | bytes 10223620
  158.4 5.4 %collective-permute-start.3 = (bf16[16,384,128]{2,1,0:T(8,128)(2,1)S(1)}, bf16[16,384,128]{2,1,0:T(8,128)(2,1)S(1)}, u32[]{:S(2)}, u32[]{:S(2)}) collective-permute-start(bf16[16,384,128]{2,1,0:T(8,128)(2,1)S(1)} %all_to_all.44.x_ref.own_ref), channel_id=1, source_target_pairs={{0,1},{1,0},{2,3},{3,2},{4,5},{5,4},{6,7},{7,6},{8,9},{9,8},{10,11... | collective-permute-start | bytes 4718600 | tf_op jit(solution)/shard_map/ppermute | solution.py:38
  214.9 28.4 %copy-start.6 = (bf16[832,2048]{1,0:T(8,128)(2,1)S(1)}, bf16[832,2048]{1,0:T(8,128)(2,1)}, u32[]{:S(2)}) copy-start(bf16[832,2048]{1,0:T(8,128)(2,1)} %w_ref.7) | copy-start | bytes 10223620
  215.9 5.9 %collective-permute-start.9 = (bf16[96,832]{1,0:T(8,128)(2,1)}, bf16[96,832]{1,0:T(8,128)(2,1)}, u32[]{:S(2)}, u32[]{:S(2)}) collective-permute-start(bf16[96,832]{1,0:T(8,128)(2,1)} %hidden_row.1.refs_0_), channel_id=1, source_target_pairs={{0,32},{32,64},{64,96},{96,128},{128,160},{160,192},{192,224},{224... | collective-permute-start | bytes 479240 | tf_op jit(solution)/shard_map/ppermute | solution.py:493
  217.1 6.8 %collective-permute-start.6 = (bf16[96,832]{1,0:T(8,128)(2,1)}, bf16[96,832]{1,0:T(8,128)(2,1)}, u32[]{:S(2)}, u32[]{:S(2)}) collective-permute-start(bf16[96,832]{1,0:T(8,128)(2,1)} %hidden_row.1.refs_0_), channel_id=1, source_target_pairs={{0,160},{32,192},{64,224},{96,0},{128,32},{160,64},{192,96},{224,1... | collective-permute-start | bytes 479240 | tf_op jit(solution)/shard_map/ppermute | solution.py:493
  219.3 14.9 %collective-permute-start.4 = (bf16[96,832]{1,0:T(8,128)(2,1)}, bf16[96,832]{1,0:T(8,128)(2,1)}, u32[]{:S(2)}, u32[]{:S(2)}) collective-permute-start(bf16[96,832]{1,0:T(8,128)(2,1)} %hidden_row.1.refs_0_), channel_id=1, source_target_pairs={{0,224},{32,0},{64,32},{96,64},{128,96},{160,128},{192,160},{224,1... | collective-permute-start | bytes 479240 | tf_op jit(solution)/shard_map/ppermute | solution.py:493
  220.8 15.2 %collective-permute-start.8 = (bf16[96,832]{1,0:T(8,128)(2,1)}, bf16[96,832]{1,0:T(8,128)(2,1)}, u32[]{:S(2)}, u32[]{:S(2)}) collective-permute-start(bf16[96,832]{1,0:T(8,128)(2,1)} %hidden_row.1.refs_0_), channel_id=1, source_target_pairs={{0,96},{32,128},{64,160},{96,192},{128,224},{160,0},{192,32},{224,... | collective-permute-start | bytes 479240 | tf_op jit(solution)/shard_map/ppermute | solution.py:493
  221.8 17.7 %collective-permute-start.10 = (bf16[96,832]{1,0:T(8,128)(2,1)}, bf16[96,832]{1,0:T(8,128)(2,1)}, u32[]{:S(2)}, u32[]{:S(2)}) collective-permute-start(bf16[96,832]{1,0:T(8,128)(2,1)} %collective-permute-done.9.refs_7_), channel_id=1, source_target_pairs={{0,32},{32,64},{64,96},{96,128},{128,160},{160,192},{192,224},{224... | collective-permute-start | bytes 479240 | tf_op jit(solution)/shard_map/ppermute | solution.py:493
  223.9 15.6 %collective-permute-start.7 = (bf16[96,832]{1,0:T(8,128)(2,1)}, bf16[96,832]{1,0:T(8,128)(2,1)}, u32[]{:S(2)}, u32[]{:S(2)}) collective-permute-start(bf16[96,832]{1,0:T(8,128)(2,1)} %collective-permute-done.6.refs_3_), channel_id=1, source_target_pairs={{0,224},{32,0},{64,32},{96,64},{128,96},{160,128},{192,160},{224,1... | collective-permute-start | bytes 479240 | tf_op jit(solution)/shard_map/ppermute | solution.py:493
  234.2 7.6 %collective-permute-start.5 = (bf16[96,832]{1,0:T(8,128)(2,1)}, bf16[96,832]{1,0:T(8,128)(2,1)}, u32[]{:S(2)}, u32[]{:S(2)}) collective-permute-start(bf16[96,832]{1,0:T(8,128)(2,1)} %collective-permute-done.4.refs_1_), channel_id=1, source_target_pairs={{0,224},{32,0},{64,32},{96,64},{128,96},{160,128},{192,160},{224,1... | collective-permute-start | bytes 479240 | tf_op jit(solution)/shard_map/ppermute | solution.py:493
  245.6 5.3 %collective-permute-start.11 = (bf16[16,384,128]{2,1,0:T(8,128)(2,1)S(1)}, bf16[16,384,128]{2,1,0:T(8,128)(2,1)S(1)}, u32[]{:S(2)}, u32[]{:S(2)}) collective-permute-start(bf16[16,384,128]{2,1,0:T(8,128)(2,1)S(1)} %proj_half.7), channel_id=1, source_target_pairs={{0,1},{1,0},{2,3},{3,2},{4,5},{5,4},{6,7},{7,6},{8,9},{9,8},{10,11... | collective-permute-start | bytes 4718600 | tf_op jit(solution)/shard_map/ppermute | solution.py:38
  281.2 2.8 collective-permute-start.12
  (13 other events, 15.3 us)
Sparse Core Ops, SparseCore 0:
  169.1 43.7 reduce-scatter.1

commit v5 on v4

--- a/solution.py
+++ b/solution.py
@@ -242,10 +242,49 @@
     )(h, x, w)
 
 
-def project_out(c, x, w):
-    given = proj_half(1 - c, x, w, BF)
-    got = swap(given)
-    kept = proj_half(c, x, w, F32)
+def proj_rows_kernel(h_ref, *refs):
+    w_ref, out_ref, xs = refs[-3:]
+
+    @pl.when(pl.program_id(0) == 0)
+    def _():
+        for k, ref in enumerate(refs[:-3]):
+            row = lax.rem(h_ref[1] + k, ROWS)
+
+            @pl.when(row // 4 == h_ref[0])
+            def _():
+                xs[pl.ds(pl.multiple_of(lax.rem(row, 4) * SEQ, SEQ), SEQ)] = ref[...]
+
+    result = nn(xs[...], w_ref[...]).astype(out_ref.dtype)
+    for j in range(out_ref.shape[0]):
+        out_ref[j] = result[:, j * LANE : (j + 1) * LANE]
+
+
+def proj_rows_half(h, pieces, w, dtype):
+    depth = pieces[0].shape[1]
+    steps = 2
+    wide = 2048 // steps
+    return pl.pallas_call(
+        proj_rows_kernel,
+        grid_spec=pltpu.PrefetchScalarGridSpec(
+            num_scalar_prefetch=1,
+            grid=(steps,),
+            in_specs=[pl.BlockSpec((SEQ, depth), lambda i, h: (0, 0))] * ROWS
+            + [pl.BlockSpec((depth, wide), lambda i, h: (0, i))],
+            out_specs=pl.BlockSpec((wide // LANE, HALF, LANE), lambda i, h: (i, 0, 0)),
+            scratch_shapes=[pltpu.VMEM((HALF, depth), BF)],
+        ),
+        out_shape=jax.ShapeDtypeStruct((CHIPS, HALF, LANE), dtype),
+        compiler_params=params(24),
+        cost_estimate=pl.CostEstimate(
+            flops=2 * HALF * 2048 * depth, bytes_accessed=4 * 1024 * 1024, transcendentals=0
+        ),
+        name="proj_rows_half",
+    )(h, *pieces, w)
+
+
+def project_out(product, mine, theirs, x, w):
+    got = swap(product(theirs, x, w, BF))
+    kept = product(mine, x, w, F32)
     return over_chips((kept + got.astype(F32)).astype(BF))
 
 
@@ -311,7 +350,13 @@
     )(h, keep, got).T
 
 
-def cut_kernel(h_ref, t_ref, ga_ref, gf_ref, keep_ref, give_ref):
+def cut_kernel(h_ref, t_hbm, ga_hbm, gf_hbm, keep_ref, give_ref, t_ref, ga_ref, gf_ref, sems):
+    pairs = ((t_hbm, t_ref), (ga_hbm, ga_ref), (gf_hbm, gf_ref))
+    copies = [pltpu.make_async_copy(a, b, sems.at[n]) for n, (a, b) in enumerate(pairs)]
+    for copy in copies:
+        copy.start()
+    for copy in copies:
+        copy.wait()
     row = lax.broadcasted_iota(jnp.int32, (16, 64), 0)
     ga, gf = ga_ref[...].astype(F32), gf_ref[...].astype(F32)
     gains = jnp.where(row == 0, ga, jnp.where(row == 1, gf, 0.0)).astype(BF)
@@ -324,19 +369,20 @@
 
 
 def cut_tokens(h, tokens_t, norm_attn, norm_ffn):
-    whole = lambda *shape: pl.BlockSpec(shape, lambda i: (0, 0))
+    hbm = pl.BlockSpec(memory_space=pltpu.HBM)
+    vmem = pl.BlockSpec(memory_space=pltpu.VMEM)
     return pl.pallas_call(
         cut_kernel,
-        grid=(1,),
-        in_specs=[
-            pl.BlockSpec(memory_space=pltpu.SMEM),
-            whole(64, TOK),
-            whole(1, 64),
-            whole(1, 64),
+        in_specs=[pl.BlockSpec(memory_space=pltpu.SMEM), hbm, hbm, hbm],
+        out_specs=(vmem, vmem),
+        out_shape=(jax.ShapeDtypeStruct((HALF + 16, 64), BF),) * 2,
+        scratch_shapes=[
+            pltpu.VMEM((64, TOK), BF),
+            pltpu.VMEM((1, 64), BF),
+            pltpu.VMEM((1, 64), BF),
+            pltpu.SemaphoreType.DMA((3,)),
         ],
-        out_specs=(whole(HALF + 16, 64), whole(HALF + 16, 64)),
-        out_shape=(jax.ShapeDtypeStruct((HALF + 16, 64), BF),) * 2,
-        compiler_params=params(),
+        compiler_params=params(58),
         name="cut_tokens",
     )(h, tokens_t, norm_attn.reshape(1, 64), norm_ffn.reshape(1, 64))
 
@@ -362,51 +408,78 @@
     )(h, keep, got)
 
 
-def gained_rows(x_ref, g_ref, xs):
-    for j in range(CHIPS):
-        gain = g_ref[j, 1:2].astype(F32)
-        xs[:, j * LANE : (j + 1) * LANE] = (x_ref[j].astype(F32) * gain).astype(BF)
+def load_half(x_ref, xv, sems):
+    copies = [
+        pltpu.make_async_copy(x_ref.at[pl.ds(4 * i, 4)], xv.at[pl.ds(4 * i, 4)], sems.at[i])
+        for i in range(CHIPS // 4)
+    ]
+    for copy in copies:
+        copy.start()
+    return copies
+
+
+def gained_rows(copies, xv, g_ref, xs):
+    for i, copy in enumerate(copies):
+        copy.wait()
+        for j in range(4 * i, 4 * i + 4):
+            gain = g_ref[j, 1:2].astype(F32)
+            xs[:, j * LANE : (j + 1) * LANE] = (xv[j].astype(F32) * gain).astype(BF)
+
+
+HBM = pl.BlockSpec(memory_space=pltpu.HBM)
 
 
 def gate_up_main_kernel(h_ref, x_ref, g_ref, wg_ref, wu_ref, *rest):
-    out_ref, xs = rest[-2:]
-    step = pl.program_id(0)
-
-    @pl.when(step == 0)
-    def _():
-        gained_rows(x_ref, g_ref, xs)
-
-    wide = wg_ref.shape[0]
-    at = pl.multiple_of(step * wide, wide)
-    out_ref[:, pl.ds(at, wide)] = nt(xs[...], wg_ref[...]).astype(BF)
-    out_ref[:, pl.ds(MAIN + at, wide)] = nt(xs[...], wu_ref[...]).astype(BF)
+    out_ref, copy_ref, xv, xs, result, in_sems, out_sems = rest[-7:]
+    gained_rows(load_half(x_ref, xv, in_sems), xv, g_ref, xs)
+    rows = pl.ds(pl.multiple_of(h_ref[0] * HALF, HALF), HALF)
+    copies = [pltpu.make_async_copy(xv, copy_ref, out_sems.at[2])]
+    copies[0].start()
+    for n, w_ref in enumerate((wg_ref, wu_ref)):
+        result[n] = nt(xs[...], w_ref[...]).astype(BF)
+        copies.append(
+            pltpu.make_async_copy(
+                result.at[n], out_ref.at[rows, pl.ds(n * MAIN, MAIN)], out_sems.at[n]
+            )
+        )
+        copies[-1].start()
+    for copy in copies:
+        copy.wait()
 
 
 def gate_up_main(h, x, gains, wg_t, wu_t, held=None):
-    steps = 1
-    wide = MAIN // steps
+    w_spec = pl.BlockSpec((MAIN, 2048), lambda i, h: (0, 0))
     in_specs = [
-        pl.BlockSpec((CHIPS, HALF, LANE), lambda i, h: (0, 0, 0)),
+        HBM,
         pl.BlockSpec((CHIPS, 16, LANE), lambda i, h: (0, HALF // 16, 0)),
-        pl.BlockSpec((wide, 2048), lambda i, h: (i, 0)),
-        pl.BlockSpec((wide, 2048), lambda i, h: (i, 0)),
+        w_spec,
+        w_spec,
     ]
     operands = [h, x, gains, wg_t, wu_t]
     aliases = {}
     if held is not None:
-        in_specs.append(pl.BlockSpec(memory_space=pl.ANY))
+        in_specs.append(HBM)
         operands.append(held)
         aliases = {5: 0}
     return pl.pallas_call(
         gate_up_main_kernel,
         grid_spec=pltpu.PrefetchScalarGridSpec(
             num_scalar_prefetch=1,
-            grid=(steps,),
+            grid=(1,),
             in_specs=in_specs,
-            out_specs=pl.BlockSpec((HALF, 2 * MAIN), lambda i, h: (h[0], 0)),
-            scratch_shapes=[pltpu.VMEM((HALF, 2048), BF)],
-        ),
-        out_shape=jax.ShapeDtypeStruct((TOK, 2 * MAIN), BF),
+            out_specs=(HBM, HBM),
+            scratch_shapes=[
+                pltpu.VMEM((CHIPS, HALF, LANE), BF),
+                pltpu.VMEM((HALF, 2048), BF),
+                pltpu.VMEM((2, HALF, MAIN), BF),
+                pltpu.SemaphoreType.DMA((CHIPS // 4,)),
+                pltpu.SemaphoreType.DMA((3,)),
+            ],
+        ),
+        out_shape=(
+            jax.ShapeDtypeStruct((TOK, 2 * MAIN), BF),
+            jax.ShapeDtypeStruct((CHIPS, HALF, LANE), BF),
+        ),
         input_output_aliases=aliases,
         compiler_params=params(24),
         cost_estimate=pl.CostEstimate(
@@ -418,44 +491,61 @@
     )(*operands)
 
 
-def gate_up_side_kernel(h_ref, own_ref, other_ref, g_ref, wg_ref, wu_ref, _, out_ref, xs):
+def gate_up_side_kernel(
+    h_ref, own_ref, other_ref, g_ref, wg_ref, wu_ref, _, out_ref, xv, xs, wv, own_sems, other_sems, w_sems
+):
+    loads = [load_half(own_ref, xv.at[0], own_sems), load_half(other_ref, xv.at[1], other_sems)]
+    w_loads = [
+        pltpu.make_async_copy(w_ref.at[pl.ds(MAIN, REST)], wv.at[n], w_sems.at[n])
+        for n, w_ref in enumerate((wg_ref, wu_ref))
+    ]
+    for copy in w_loads:
+        copy.start()
     lane = lax.broadcasted_iota(jnp.int32, (HALF, SIDE // 2 - REST), 1)
-    for x_ref, half in ((own_ref, h_ref[0]), (other_ref, 1 - h_ref[0])):
-        gained_rows(x_ref, g_ref, xs)
+    for at, half in ((0, h_ref[0]), (1, 1 - h_ref[0])):
+        gained_rows(loads[at], xv.at[at], g_ref, xs)
         squares = None
         for j in range(CHIPS):
-            wide = x_ref[j].astype(F32)
+            wide = xv[at, j].astype(F32)
             squares = wide * wide if squares is None else squares + wide * wide
         high, low = split_two(jnp.sum(squares, axis=1, keepdims=True))
         extra = jnp.where(lane == 0, high, jnp.where(lane == 1, low, 0.0))
         rows = pl.ds(pl.multiple_of(half * HALF, HALF), HALF)
-        gate = jnp.concatenate([nt(xs[...], wg_ref[...]), extra], axis=1)
+        if at == 0:
+            for copy in w_loads:
+                copy.wait()
+        gate = jnp.concatenate([nt(xs[...], wv[0]), extra], axis=1)
         out_ref[rows, : SIDE // 2] = gate.astype(BF)
-        up = jnp.concatenate([nt(xs[...], wu_ref[...]), jnp.zeros_like(extra)], axis=1)
+        up = jnp.concatenate([nt(xs[...], wv[1]), jnp.zeros_like(extra)], axis=1)
         out_ref[rows, SIDE // 2 :] = up.astype(BF)
 
 
 def gate_up_side(h, own, other, gains, wg_t, wu_t, main):
-    x_spec = pl.BlockSpec((CHIPS, HALF, LANE), lambda i, h: (0, 0, 0))
-    w_spec = pl.BlockSpec((pl.Element(REST), pl.Element(2048)), lambda i, h: (MAIN, 0))
     return pl.pallas_call(
         gate_up_side_kernel,
         grid_spec=pltpu.PrefetchScalarGridSpec(
             num_scalar_prefetch=1,
             grid=(1,),
             in_specs=[
-                x_spec,
-                x_spec,
+                HBM,
+                HBM,
                 pl.BlockSpec((CHIPS, 16, LANE), lambda i, h: (0, HALF // 16, 0)),
-                w_spec,
-                w_spec,
-                pl.BlockSpec(memory_space=pl.ANY),
+                HBM,
+                HBM,
+                HBM,
             ],
             out_specs=pl.BlockSpec((TOK, SIDE), lambda i, h: (0, 0)),
-            scratch_shapes=[pltpu.VMEM((HALF, 2048), BF)],
+            scratch_shapes=[
+                pltpu.VMEM((2, CHIPS, HALF, LANE), BF),
+                pltpu.VMEM((HALF, 2048), BF),
+                pltpu.VMEM((2, REST, 2048), BF),
+                pltpu.SemaphoreType.DMA((CHIPS // 4,)),
+                pltpu.SemaphoreType.DMA((CHIPS // 4,)),
+                pltpu.SemaphoreType.DMA((2,)),
+            ],
         ),
         out_shape=jax.ShapeDtypeStruct((TOK, SIDE), BF),
-        compiler_params=params(24),
+        compiler_params=params(58),
         cost_estimate=pl.CostEstimate(
             flops=4 * TOK * 2048 * REST, bytes_accessed=6 * 1024 * 1024, transcendentals=0
         ),
@@ -463,7 +553,12 @@
     )(h, own, other, gains, wg_t, wu_t, main)
 
 
-def hidden_kernel(main_ref, side_ref, out_ref):
+def hidden_kernel(main_hbm, side_hbm, out_ref, main_ref, side_ref, sems):
+    main_load = pltpu.make_async_copy(main_hbm, main_ref, sems.at[0])
+    side_load = pltpu.make_async_copy(side_hbm, side_ref, sems.at[1])
+    side_load.start()
+    main_load.start()
+    side_load.wait()
     side = side_ref[0].astype(F32)
     for j in range(1, ROWS):
         side = side + side_ref[j].astype(F32)
@@ -474,8 +569,9 @@
         gate, up = gate * inv, up * inv
         return (gate / (1.0 + jnp.exp(-gate)) * up).astype(BF)
 
+    second = gated(side[:, :REST], side[:, SIDE // 2 : SIDE // 2 + REST])
+    main_load.wait()
     first = gated(main_ref[:, :MAIN].astype(F32), main_ref[:, MAIN:].astype(F32))
-    second = gated(side[:, :REST], side[:, SIDE // 2 : SIDE // 2 + REST])
     out_ref[:, :MAIN] = first
     out_ref[:, MAIN:] = second
 
@@ -483,20 +579,20 @@
 def hidden_row(main, side):
     return pl.pallas_call(
         hidden_kernel,
+        in_specs=[HBM, HBM],
         out_shape=jax.ShapeDtypeStruct((SEQ, FFL), BF),
-        compiler_params=params(),
+        scratch_shapes=[
+            pltpu.VMEM((SEQ, 2 * MAIN), BF),
+            pltpu.VMEM((ROWS, SEQ, SIDE), BF),
+            pltpu.SemaphoreType.DMA((2,)),
+        ],
+        compiler_params=params(58),
         name="hidden_row",
     )(main, side)
 
 
 def from_ahead(x, k):
     return lax.ppermute(x, "gx", [(i, (i - k) % ROWS) for i in range(ROWS)])
-
-
-def order_kernel(at_ref, *refs):
-    out_ref = refs[-1]
-    for k, ref in enumerate(refs[:-1]):
-        out_ref[lax.rem(at_ref[0] + k, ROWS)] = ref[...]
 
 
 def all_rows(x):
@@ -506,16 +602,7 @@
     ahead[2] = from_ahead(ahead[1], 1)
     ahead[6] = from_ahead(ahead[7], 7)
     ahead[4] = from_ahead(ahead[3], 1)
-    vmem = pl.BlockSpec(memory_space=pltpu.VMEM)
-    at = jnp.reshape(lax.axis_index("gx"), (1,)).astype(jnp.int32)
-    return pl.pallas_call(
-        order_kernel,
-        in_specs=[pl.BlockSpec(memory_space=pltpu.SMEM)] + [vmem] * ROWS,
-        out_specs=vmem,
-        out_shape=jax.ShapeDtypeStruct((ROWS,) + x.shape, x.dtype),
-        compiler_params=params(),
-        name="order_rows",
-    )(at, *[ahead[k] for k in range(ROWS)])
+    return [ahead[k] for k in range(ROWS)]
 
 
 def rope_table():
@@ -556,18 +643,22 @@
     q, kv = qkv_sum(over_rows(parts))
     kv = lax.all_to_all(kv, "gy", 0, 0, axis_index_groups=KV_GROUPS, tiled=True)
     attended = over_rows(attend(lengths, q, kv, segments)).reshape(TOK, 256)
-    residual, copies = residual_copies(base, project_out(c, attended, w_out))
+    residual, copies = residual_copies(
+        base, project_out(proj_half, c, 1 - c, attended, w_out)
+    )
 
     own = over_chips(copies)
     other = swap(own)
     weights = (w_gate.T, w_up.T)
-    held = gate_up_main(c, own, first, *weights)
-    main = gate_up_main(1 - c, other, first, *weights, held)
+    held, own = gate_up_main(c, own, first, *weights)
+    main, other = gate_up_main(1 - c, other, first, *weights, held)
     side = gate_up_side(c, own, other, first, *weights, main)
     main = lax.psum_scatter(main, "gx", scatter_dimension=0, tiled=True)
     side = over_rows(side.reshape(ROWS, SEQ, SIDE))
-    hidden = all_rows(hidden_row(main, side)).reshape(TOK, FFL)
-    keep, give = final_sum(c, residual, project_out(c, hidden, w_down))
+    hidden = all_rows(hidden_row(main, side))
+    at = jnp.reshape(lax.axis_index("gx"), (1,)).astype(jnp.int32)
+    mine, theirs = jnp.concatenate([c, at]), jnp.concatenate([1 - c, at])
+    keep, give = final_sum(c, residual, project_out(proj_rows_half, mine, theirs, hidden, w_down))
     return place_halves(c, keep, swap(give))
 
 

time: 292 us -> 299 us (1.024)
  Pallas kernels: 23.2 us -> 37.6 us
  local copies, waits for them, and re-layouts: 15.3 us -> 5.98 us
  starting transfers between devices: 36.3 us -> 30.9 us
  waiting for transfers between devices: 19.6 us -> 24.8 us
    pallas_call x3 -> x4, Pallas kernels: 2.59 us -> 12.2 us  [the longest x2 8.39 us: proj_rows_half(): pl.pallas_call(proj_rows_kernel, grid_spec=pltpu.PrefetchScalarGridSpec(n...]
    unnamed x44 -> x36, local copies, waits for them, and re-layouts: 15.3 us -> 5.98 us
    ppermute x7, starting transfers between devices: 17.5 us -> 11.4 us  [from_ahead(): return lax.ppermute(x, 'gx', [(i, (i - k) % ROWS) for i in range(ROWS)])]
    ppermute x7, waiting for transfers between devices: 8.41 us -> 14.1 us  [from_ahead(): return lax.ppermute(x, 'gx', [(i, (i - k) % ROWS) for i in range(ROWS)])]
    pallas_call x2, Pallas kernels: 5.33 us -> 10.2 us  [gate_up_main(): pl.pallas_call(gate_up_main_kernel, grid_spec=pltpu.PrefetchScalarGridSpe...]
    pallas_call x4 -> x2, Pallas kernels: 6.15 us -> 1.7 us  [proj_half(): pl.pallas_call(proj_kernel, grid_spec=pltpu.PrefetchScalarGridSpec(num_sc...]
    pallas_call x1, Pallas kernels: 2.46 us -> 6.87 us  [gate_up_side(): pl.pallas_call(gate_up_side_kernel, grid_spec=pltpu.PrefetchScalarGridSpe...]
  transfers between devices with their start and end apart: 15 -> 15, of which waited for: 11 -> 9; matrix products, arithmetic and copies ran while one was open for 0% -> 0% of each run, Pallas kernels for 3% -> 6%
where the time goes in v5:
time: 299 us; the launch traced here: 298 us
  blocking collectives  184 us (62%)
  Pallas kernels  37.6 us (13%)
  starting transfers between devices  30.9 us (10%)
  waiting for transfers between devices  24.8 us (8%)
  between operations  14.3 us (5%)
  local copies, waits for them, and re-layouts  5.98 us (2%)
    all_to_all x4, blocking collectives, over_chips(): lax.all_to_all(x, 'gy', 0, 0, axis_index_groups=CHIP_GROUPS, tiled=True)  107 us
    all_to_all x3, blocking collectives, over_rows(): return lax.all_to_all(x, 'gx', 0, 0, tiled=True)  76.9 us
    ppermute x6, starting transfers between devices, swap(): return lax.ppermute(x, 'gy', [(i, i ^ 1) for i in range(32)])  14.5 us
    ppermute x7, waiting for transfers between devices, from_ahead(): return lax.ppermute(x, 'gx', [(i, (i - k) % ROWS) for i in range(ROWS)])  14.1 us
    ppermute x7, starting transfers between devices, from_ahead(): return lax.ppermute(x, 'gx', [(i, (i - k) % ROWS) for i in range(ROWS)])  11.4 us
    pallas_call x2, Pallas kernels, gate_up_main(): pl.pallas_call(gate_up_main_kernel, grid_spec=pltpu.PrefetchScalarGridSpe...  10.2 us
    pallas_call x2, Pallas kernels, proj_rows_half(): pl.pallas_call(proj_rows_kernel, grid_spec=pltpu.PrefetchScalarGridSpec(n...  8.39 us
    pallas_call x1, Pallas kernels, gate_up_side(): pl.pallas_call(gate_up_side_kernel, grid_spec=pltpu.PrefetchScalarGridSpe...  6.87 us
  transfers between devices with their start and end apart: 15, of which 9 were waited for; matrix products, arithmetic and copies ran while one was open for 0% of the time, Pallas kernels for 6%

profile of v5, /device:TPU:1, one launch (start us, length us, event | category | flops | bytes accessed | tf_op | source)
XLA Modules:
  0.0 298.3 jit_solution(12686667619661708303)
XLA Ops:
  8.2 3.3 %collective-permute-start = (bf16[400,64]{1,0:T(8,128)(2,1)}, bf16[400,64]{1,0:T(8,128)(2,1)S(1)}, u32[]{:S(2)}, u32[]{:S(2)}) collective-permute-start(bf16[400,64]{1,0:T(8,128)(2,1)} %get-tuple-element.18), channel_id=1, source_target_pairs={{0,1},{1,0},{2,3},{3,2},{4,5},{5,4},{6,7},{7,6},{8,9},{9,8},{10,11... | collective-permute-start | bytes 153608 | tf_op jit(solution)/shard_map/ppermute | solution.py:38
  14.0 27.6 %all_to_all.40.x_ref.g_ref = bf16[16,400,128]{2,1,0:T(8,128)(2,1)S(1)} all-to-all(bf16[16,400,128]{2,1,0:T(8,128)(2,1)S(1)} %join_copies.1.base_ref), channel_id=1, replica_groups={{0,2,4,6,8,10,12,14,16,18,20,22,24,26,28,30},{1,3,5,7,9,11,13,15,17,19,..., dimensions={0} | all-to-all | bytes 3276800 | tf_op jit(solution)/shard_map/all_to_all | solution.py:42
  48.4 24.8 %all_to_all.41.p_ref = bf16[8,128,256]{2,1,0:T(8,128)(2,1)S(1)} all-to-all(bf16[8,128,256]{2,1,0:T(8,128)(2,1)S(1)} %qkv_half.3), channel_id=1, replica_groups=mesh['gx'=8,'gy'=32] {'gx'}, dimensions={0} | all-to-all | bytes 1048576 | tf_op jit(solution)/shard_map/all_to_all | solution.py:46
  74.5 5.1 %all-to-all-start.2 = ((f32[8,32,96]{2,1,0:T(8,128)}), f32[8,32,96]{2,1,0:T(8,128)S(1)}, u32[]{:S(2)}, u32[]{:S(2)}) async-start(f32[8,32,96]{2,1,0:T(8,128)} %get-tuple-element.20), calls=%async_computation.2 | async-start | bytes 262144 | tf_op jit(solution)/shard_map/all_to_all | solution.py:644
  80.2 4.6 %all-to-all-done.2.kv_ref = f32[8,32,96]{2,1,0:T(8,128)S(1)} async-done(((f32[8,32,96]{2,1,0:T(8,128)}), f32[8,32,96]{2,1,0:T(8,128)S(1)}, u32[]{:S(2)}, u32[]{:S(2)}) %all-to-all-start.2) | async-done | bytes 98336 | tf_op jit(solution)/shard_map/all_to_all | solution.py:644
  86.4 15.9 %all_to_all.42 = bf16[8,96,256]{2,1,0:T(8,128)(2,1)S(1)} all-to-all(bf16[8,96,256]{2,1,0:T(8,128)(2,1)S(1)} %attend.1), channel_id=1, replica_groups=mesh['gx'=8,'gy'=32] {'gx'}, dimensions={0} | all-to-all | bytes 786432 | tf_op jit(solution)/shard_map/all_to_all | solution.py:46
  103.2 2.2 collective-permute-start.2
  106.3 2.2 collective-permute-done.2
  108.9 24.9 %all_to_all.43.p_ref = bf16[16,384,128]{2,1,0:T(8,128)(2,1)S(1)} all-to-all(bf16[16,384,128]{2,1,0:T(8,128)(2,1)S(1)} %add_convert_fusion.1), channel_id=1, replica_groups={{0,2,4,6,8,10,12,14,16,18,20,22,24,26,28,30},{1,3,5,7,9,11,13,15,17,19,..., dimensions={0} | all-to-all | bytes 3145728 | tf_op jit(solution)/shard_map/all_to_all | solution.py:42
  134.1 24.8 %all_to_all.44.x_ref = bf16[16,384,128]{2,1,0:T(8,128)(2,1)S(1)} all-to-all(bf16[16,384,128]{2,1,0:T(8,128)(2,1)S(1)} %get-tuple-element.22), channel_id=1, replica_groups={{0,2,4,6,8,10,12,14,16,18,20,22,24,26,28,30},{1,3,5,7,9,11,13,15,17,19,..., dimensions={0} | all-to-all | bytes 3145728 | tf_op jit(solution)/shard_map/all_to_all | solution.py:42
  158.9 2.3 collective-permute-start.3
  161.2 5.1 %gate_up_main.2 = (bf16[768,1280]{1,0:T(8,128)(2,1)S(1)}, bf16[16,384,128]{2,1,0:T(8,128)(2,1)S(1)}) custom-call(s32[1]{0:T(128)} %bitcast.h_ref, bf16[16,384,128]{2,1,0:T(8,128)(2,1)S(1)} %all_to_all.44.x_ref, bf16[16,400,128]{2,1,0:T(8,128)(2,1)S(1)} %all_to_all.40.x_ref.g_ref, bf16[832,2048]{1,0:T(8,128)(2,1)S(1)} %bitcast.14, bf16[832,2048]{1,0:T(8,128)(2,1)S(1)} %bitcast.17), custom_call_target="tpu_custom_call" | custom-call | flops 2013265920 | bytes 8388608 | tf_op jit(solution)/shard_map/gate_up_main/pallas_call | solution.py:464
  166.4 5.1 %gate_up_main.3 = (bf16[768,1280]{1,0:T(8,128)(2,1)S(1)}, bf16[16,384,128]{2,1,0:T(8,128)(2,1)S(1)}) custom-call(s32[1]{0:T(128)S(6)} %sub.2.h_ref, bf16[16,384,128]{2,1,0:T(8,128)(2,1)S(1)} %collective-permute-done.3.x_ref, bf16[16,400,128]{2,1,0:T(8,128)(2,1)S(1)} %all_to_all.40.x_ref.g_ref, ...), custom_call_target="tpu_custom_call", output_to_operand_aliasing={{0}: (5, {})} | custom-call | flops 2013265920 | bytes 8388608 | tf_op jit(solution)/shard_map/gate_up_main/pallas_call | solution.py:464
  174.0 6.9 %gate_up_side.1 = bf16[768,512]{1,0:T(8,128)(2,1)} custom-call(s32[1]{0:T(128)} %bitcast.h_ref, bf16[16,384,128]{2,1,0:T(8,128)(2,1)} %copy-done.7, bf16[16,384,128]{2,1,0:T(8,128)(2,1)} %copy-done.8, bf16[16,400,128]{2,1,0:T(8,128)(2,1)} %copy-done, bf16[832,2048]{1,0:T(8,128)(2,1)} %bitcast.13, bf16[832,2048]{1,0:T(8,128)(2,1)} %bitcast.16, ...), custom_call_target="tpu_custom_call" | custom-call | flops 1207959552 | bytes 6291456 | tf_op jit(solution)/shard_map/gate_up_side/pallas_call | solution.py:524
  180.9 36.2 %all_to_all.45.side_hbm = bf16[8,96,512]{2,1,0:T(8,128)(2,1)} all-to-all(bf16[8,96,512]{2,1,0:T(8,128)(2,1)} %bitcast.26), channel_id=1, replica_groups=mesh['gx'=8,'gy'=32] {'gx'}, dimensions={0} | all-to-all | bytes 1572864 | tf_op jit(solution)/shard_map/all_to_all | solution.py:46
  220.3 2.2 collective-permute-start.4
  222.5 2.4 collective-permute-start.6
  228.5 4.3 %collective-permute-done.6.refs_3_ = bf16[96,832]{1,0:T(8,128)(2,1)} collective-permute-done((bf16[96,832]{1,0:T(8,128)(2,1)}, bf16[96,832]{1,0:T(8,128)(2,1)}, u32[]{:S(2)}, u32[]{:S(2)}) %collective-permute-start.6) | collective-permute-done | bytes 159776 | tf_op jit(solution)/shard_map/ppermute | solution.py:595
  232.7 2.7 collective-permute-start.7
  235.4 8.4 %collective-permute-done.10.refs_6_ = bf16[96,832]{1,0:T(8,128)(2,1)} collective-permute-done((bf16[96,832]{1,0:T(8,128)(2,1)}, bf16[96,832]{1,0:T(8,128)(2,1)}, u32[]{:S(2)}, u32[]{:S(2)}) %collective-permute-start.10) | collective-permute-done | bytes 159776 | tf_op jit(solution)/shard_map/ppermute | solution.py:595
  246.2 4.2 %proj_rows_half.3 = bf16[16,384,128]{2,1,0:T(8,128)(2,1)S(1)} custom-call(s32[2]{0:T(128)S(1)} %pad_add_fusion.1.h_ref, bf16[96,832]{1,0:T(8,128)(2,1)S(1)} %copy-done.9, bf16[96,832]{1,0:T(8,128)(2,1)} %collective-permute-done.4.refs_1_, bf16[96,832]{1,0:T(8,128)(2,1)} %collective-permute-done.5.refs_2_, bf16[96,832]{1,0:T(8,128)(2,1)} %collective-permute-done.6.refs_3_, ...), custom_call_target="tpu_custom_call" | custom-call | flops 1308622848 | bytes 4194304 | tf_op jit(solution)/shard_map/proj_rows_half/pallas_call | solution.py:266
  250.4 3.4 %collective-permute-start.11 = (bf16[16,384,128]{2,1,0:T(8,128)(2,1)S(1)}, bf16[16,384,128]{2,1,0:T(8,128)(2,1)S(1)}, u32[]{:S(2)}, u32[]{:S(2)}) collective-permute-start(bf16[16,384,128]{2,1,0:T(8,128)(2,1)S(1)} %proj_rows_half.3), channel_id=1, source_target_pairs={{0,1},{1,0},{2,3},{3,2},{4,5},{5,4},{6,7},{7,6},{8,9},{9,8},{10,11... | collective-permute-start | bytes 4718600 | tf_op jit(solution)/shard_map/ppermute | solution.py:38
  253.8 4.2 %proj_rows_half.2 = f32[16,384,128]{2,1,0:T(8,128)S(1)} custom-call(s32[2]{0:T(128)S(1)} %pad_add_fusion.h_ref, bf16[96,832]{1,0:T(8,128)(2,1)S(1)} %copy-done.10, bf16[96,832]{1,0:T(8,128)(2,1)} %collective-permute-done.4.refs_1_, bf16[96,832]{1,0:T(8,128)(2,1)} %collective-permute-done.5.refs_2_, bf16[96,832]{1,0:T(8,128)(2,1)} %collective-permute-done.6.refs_3_, ...), custom_call_target="tpu_custom_call" | custom-call | flops 1308622848 | bytes 4194304 | tf_op jit(solution)/shard_map/proj_rows_half/pallas_call | solution.py:266
  258.4 29.5 %all_to_all.46.p_ref = bf16[16,384,128]{2,1,0:T(8,128)(2,1)S(1)} all-to-all(bf16[16,384,128]{2,1,0:T(8,128)(2,1)S(1)} %add_convert_fusion), channel_id=1, replica_groups={{0,2,4,6,8,10,12,14,16,18,20,22,24,26,28,30},{1,3,5,7,9,11,13,15,17,19,..., dimensions={0} | all-to-all | bytes 3145728 | tf_op jit(solution)/shard_map/all_to_all | solution.py:42
  (71 shorter events, 31.8 us)
Async XLA Ops:
  8.2 4.5 %collective-permute-start = (bf16[400,64]{1,0:T(8,128)(2,1)}, bf16[400,64]{1,0:T(8,128)(2,1)S(1)}, u32[]{:S(2)}, u32[]{:S(2)}) collective-permute-start(bf16[400,64]{1,0:T(8,128)(2,1)} %get-tuple-element.18), channel_id=1, source_target_pairs={{0,1},{1,0},{2,3},{3,2},{4,5},{5,4},{6,7},{7,6},{8,9},{9,8},{10,11... | collective-permute-start | bytes 153608 | tf_op jit(solution)/shard_map/ppermute | solution.py:38
  13.9 29.4 %copy-start.6 = (bf16[2048,256]{1,0:T(8,128)(2,1)S(1)}, bf16[2048,256]{1,0:T(8,128)(2,1)}, u32[]{:S(2)}) copy-start(bf16[2048,256]{1,0:T(8,128)(2,1)} %wq_ref.3) | copy-start | bytes 3145732
  14.0 29.4 %copy-start.11 = (bf16[2048,16]{0,1:T(8,128)(2,1)S(1)}, bf16[2048,16]{0,1:T(8,128)(2,1)}, u32[]{:S(2)}) copy-start(bf16[2048,16]{0,1:T(8,128)(2,1)} %param.16) | copy-start | bytes 196612
  14.0 29.4 %copy-start.12 = (bf16[2048,16]{0,1:T(8,128)(2,1)S(1)}, bf16[2048,16]{0,1:T(8,128)(2,1)}, u32[]{:S(2)}) copy-start(bf16[2048,16]{0,1:T(8,128)(2,1)} %param.17) | copy-start | bytes 196612
  41.6 124.8 %copy-start = (bf16[16,400,128]{2,1,0:T(8,128)(2,1)}, bf16[16,400,128]{2,1,0:T(8,128)(2,1)S(1)}, u32[]{:S(2)}) copy-start(bf16[16,400,128]{2,1,0:T(8,128)(2,1)S(1)} %all_to_all.40.x_ref.g_ref) | copy-start | bytes 4915204
  41.6 4.9 %collective-permute-start.1 = (bf16[16,400,128]{2,1,0:T(8,128)(2,1)S(1)}, bf16[16,400,128]{2,1,0:T(8,128)(2,1)S(1)}, u32[]{:S(2)}, u32[]{:S(2)}) collective-permute-start(bf16[16,400,128]{2,1,0:T(8,128)(2,1)S(1)} %all_to_all.40.x_ref.g_ref), channel_id=1, source_target_pairs={{0,1},{1,0},{2,3},{3,2},{4,5},{5,4},{6,7},{7,6},{8,9},{9,8},{10,11... | collective-permute-start | bytes 4915208 | tf_op jit(solution)/shard_map/ppermute | solution.py:38
  48.4 36.5 %copy-start.13 = (f32[2,128,128]{2,1,0:T(8,128)S(1)}, f32[2,128,128]{2,1,0:T(8,128)}, u32[]{:S(2)}) copy-start(f32[2,128,128]{2,1,0:T(8,128)} %constant.26.clone.table_ref) | copy-start | bytes 393220
  48.4 36.5 %copy-start.17 = (s32[96]{0:T(128)S(1)}, s32[96]{0:T(128)}, u32[]{:S(2)}) copy-start(s32[96]{0:T(128)} %param.24) | copy-start | bytes 1156
  74.5 10.4 %all-to-all-start.2 = ((f32[8,32,96]{2,1,0:T(8,128)}), f32[8,32,96]{2,1,0:T(8,128)S(1)}, u32[]{:S(2)}, u32[]{:S(2)}) async-start(f32[8,32,96]{2,1,0:T(8,128)} %get-tuple-element.20), calls=%async_computation.2 | async-start | bytes 262144 | tf_op jit(solution)/shard_map/all_to_all | solution.py:644
  79.6 138.1 %reduce-scatter.2.cloned.1.call-start = ((), (), s32[]{:S(2)}) async-start(), calls=%async_computation.9 | async-start | bytes 2211840 | tf_op jit(solution)/shard_map/reduce_scatter | solution.py:656
  103.2 5.2 %collective-permute-start.2 = (bf16[16,384,128]{2,1,0:T(8,128)(2,1)S(1)}, bf16[16,384,128]{2,1,0:T(8,128)(2,1)S(1)}, u32[]{:S(2)}, u32[]{:S(2)}) collective-permute-start(bf16[16,384,128]{2,1,0:T(8,128)(2,1)S(1)} %proj_half.3), channel_id=1, source_target_pairs={{0,1},{1,0},{2,3},{3,2},{4,5},{5,4},{6,7},{7,6},{8,9},{9,8},{10,11... | collective-permute-start | bytes 4718600 | tf_op jit(solution)/shard_map/ppermute | solution.py:38
  108.9 52.4 %copy-start.2 = (bf16[2048,832]{0,1:T(8,128)(2,1)S(1)}, bf16[2048,832]{0,1:T(8,128)(2,1)}, u32[]{:S(2)}) copy-start(bf16[2048,832]{0,1:T(8,128)(2,1)} %param.21) | copy-start | bytes 10223620
  133.8 27.5 %copy-start.1 = (bf16[2048,832]{0,1:T(8,128)(2,1)S(1)}, bf16[2048,832]{0,1:T(8,128)(2,1)}, u32[]{:S(2)}) copy-start(bf16[2048,832]{0,1:T(8,128)(2,1)} %param.20) | copy-start | bytes 10223620
  158.9 7.5 %collective-permute-start.3 = (bf16[16,384,128]{2,1,0:T(8,128)(2,1)S(1)}, bf16[16,384,128]{2,1,0:T(8,128)(2,1)S(1)}, u32[]{:S(2)}, u32[]{:S(2)}) collective-permute-start(bf16[16,384,128]{2,1,0:T(8,128)(2,1)S(1)} %all_to_all.44.x_ref), channel_id=1, source_target_pairs={{0,1},{1,0},{2,3},{3,2},{4,5},{5,4},{6,7},{7,6},{8,9},{9,8},{10,11... | collective-permute-start | bytes 4718600 | tf_op jit(solution)/shard_map/ppermute | solution.py:38
  174.0 71.2 %copy-start.4 = (bf16[832,2048]{1,0:T(8,128)(2,1)S(1)}, bf16[832,2048]{1,0:T(8,128)(2,1)}, u32[]{:S(2)}) copy-start(bf16[832,2048]{1,0:T(8,128)(2,1)} %refs_8_.3) | copy-start | bytes 10223620
  219.8 6.0 %collective-permute-start.9 = (bf16[96,832]{1,0:T(8,128)(2,1)}, bf16[96,832]{1,0:T(8,128)(2,1)}, u32[]{:S(2)}, u32[]{:S(2)}) collective-permute-start(bf16[96,832]{1,0:T(8,128)(2,1)} %hidden_row.1.refs_0_), channel_id=1, source_target_pairs={{0,32},{32,64},{64,96},{96,128},{128,160},{160,192},{192,224},{224... | collective-permute-start | bytes 479240 | tf_op jit(solution)/shard_map/ppermute | solution.py:595
  220.3 7.2 %collective-permute-start.4 = (bf16[96,832]{1,0:T(8,128)(2,1)}, bf16[96,832]{1,0:T(8,128)(2,1)}, u32[]{:S(2)}, u32[]{:S(2)}) collective-permute-start(bf16[96,832]{1,0:T(8,128)(2,1)} %hidden_row.1.refs_0_), channel_id=1, source_target_pairs={{0,224},{32,0},{64,32},{96,64},{128,96},{160,128},{192,160},{224,1... | collective-permute-start | bytes 479240 | tf_op jit(solution)/shard_map/ppermute | solution.py:595
  222.5 10.2 %collective-permute-start.6 = (bf16[96,832]{1,0:T(8,128)(2,1)}, bf16[96,832]{1,0:T(8,128)(2,1)}, u32[]{:S(2)}, u32[]{:S(2)}) collective-permute-start(bf16[96,832]{1,0:T(8,128)(2,1)} %hidden_row.1.refs_0_), channel_id=1, source_target_pairs={{0,160},{32,192},{64,224},{96,0},{128,32},{160,64},{192,96},{224,1... | collective-permute-start | bytes 479240 | tf_op jit(solution)/shard_map/ppermute | solution.py:595
  224.9 10.5 %collective-permute-start.8 = (bf16[96,832]{1,0:T(8,128)(2,1)}, bf16[96,832]{1,0:T(8,128)(2,1)}, u32[]{:S(2)}, u32[]{:S(2)}) collective-permute-start(bf16[96,832]{1,0:T(8,128)(2,1)} %hidden_row.1.refs_0_), channel_id=1, source_target_pairs={{0,96},{32,128},{64,160},{96,192},{128,224},{160,0},{192,32},{224,... | collective-permute-start | bytes 479240 | tf_op jit(solution)/shard_map/ppermute | solution.py:595
  225.8 18.1 %collective-permute-start.10 = (bf16[96,832]{1,0:T(8,128)(2,1)}, bf16[96,832]{1,0:T(8,128)(2,1)}, u32[]{:S(2)}, u32[]{:S(2)}) collective-permute-start(bf16[96,832]{1,0:T(8,128)(2,1)} %collective-permute-done.9.refs_7_), channel_id=1, source_target_pairs={{0,32},{32,64},{64,96},{96,128},{128,160},{160,192},{192,224},{224... | collective-permute-start | bytes 479240 | tf_op jit(solution)/shard_map/ppermute | solution.py:595
  227.5 16.3 %collective-permute-start.5 = (bf16[96,832]{1,0:T(8,128)(2,1)}, bf16[96,832]{1,0:T(8,128)(2,1)}, u32[]{:S(2)}, u32[]{:S(2)}) collective-permute-start(bf16[96,832]{1,0:T(8,128)(2,1)} %collective-permute-done.4.refs_1_), channel_id=1, source_target_pairs={{0,224},{32,0},{64,32},{96,64},{128,96},{160,128},{192,160},{224,1... | collective-permute-start | bytes 479240 | tf_op jit(solution)/shard_map/ppermute | solution.py:595
  232.7 12.5 %collective-permute-start.7 = (bf16[96,832]{1,0:T(8,128)(2,1)}, bf16[96,832]{1,0:T(8,128)(2,1)}, u32[]{:S(2)}, u32[]{:S(2)}) collective-permute-start(bf16[96,832]{1,0:T(8,128)(2,1)} %collective-permute-done.6.refs_3_), channel_id=1, source_target_pairs={{0,224},{32,0},{64,32},{96,64},{128,96},{160,128},{192,160},{224,1... | collective-permute-start | bytes 479240 | tf_op jit(solution)/shard_map/ppermute | solution.py:595
  250.4 7.6 %collective-permute-start.11 = (bf16[16,384,128]{2,1,0:T(8,128)(2,1)S(1)}, bf16[16,384,128]{2,1,0:T(8,128)(2,1)S(1)}, u32[]{:S(2)}, u32[]{:S(2)}) collective-permute-start(bf16[16,384,128]{2,1,0:T(8,128)(2,1)S(1)} %proj_rows_half.3), channel_id=1, source_target_pairs={{0,1},{1,0},{2,3},{3,2},{4,5},{5,4},{6,7},{7,6},{8,9},{9,8},{10,11... | collective-permute-start | bytes 4718600 | tf_op jit(solution)/shard_map/ppermute | solution.py:38
  288.2 2.5 collective-permute-start.12
  (9 other events, 36.3 us)
Sparse Core Ops, SparseCore 0:
  174.1 43.4 reduce-scatter.1

commit v6 on v4

--- a/solution.py
+++ b/solution.py
@@ -79,8 +79,9 @@
 
 
 def qkv_kernel(h_ref, x_ref, g_ref, wq_ref, wk_ref, wv_ref, *rest):
-    out_ref, acc_q, acc_kv, acc_sq = rest[-4:]
+    out_ref, gains_ref, acc_q, acc_kv, acc_sq = rest[-5:]
     k = pl.program_id(0)
+    gains_ref[...] = g_ref[...]
 
     @pl.when(k == 0)
     def _():
@@ -130,14 +131,20 @@
             num_scalar_prefetch=1,
             grid=(KSTEP,),
             in_specs=in_specs,
-            out_specs=pl.BlockSpec((HALF // SEQ, 128, 256), lambda k, h: (h[0], 0, 0)),
+            out_specs=(
+                pl.BlockSpec((HALF // SEQ, 128, 256), lambda k, h: (h[0], 0, 0)),
+                pl.BlockSpec((chips, 16, LANE), lambda k, h: (k, 0, 0)),
+            ),
             scratch_shapes=[
                 pltpu.VMEM((HALF, 256), F32),
                 pltpu.VMEM((32, HALF), F32),
                 pltpu.VMEM((HALF, LANE), F32),
             ],
         ),
-        out_shape=jax.ShapeDtypeStruct((ROWS, 128, 256), BF),
+        out_shape=(
+            jax.ShapeDtypeStruct((ROWS, 128, 256), BF),
+            jax.ShapeDtypeStruct((CHIPS, 16, LANE), BF),
+        ),
         input_output_aliases=aliases,
         compiler_params=params(),
         cost_estimate=pl.CostEstimate(
@@ -242,10 +249,10 @@
     )(h, x, w)
 
 
-def project_out(c, x, w):
-    given = proj_half(1 - c, x, w, BF)
+def project_out(mine, theirs, x, w):
+    given = proj_half(theirs, x, w, BF)
     got = swap(given)
-    kept = proj_half(c, x, w, F32)
+    kept = proj_half(mine, x, w, F32)
     return over_chips((kept + got.astype(F32)).astype(BF))
 
 
@@ -311,7 +318,7 @@
     )(h, keep, got).T
 
 
-def cut_kernel(h_ref, t_ref, ga_ref, gf_ref, keep_ref, give_ref):
+def cut_kernel(h_ref, other_ref, at_ref, t_ref, ga_ref, gf_ref, keep_ref, give_ref):
     row = lax.broadcasted_iota(jnp.int32, (16, 64), 0)
     ga, gf = ga_ref[...].astype(F32), gf_ref[...].astype(F32)
     gains = jnp.where(row == 0, ga, jnp.where(row == 1, gf, 0.0)).astype(BF)
@@ -323,12 +330,14 @@
     give_ref[:HALF] = jnp.where(h_ref[0] == 0, second, first)
 
 
-def cut_tokens(h, tokens_t, norm_attn, norm_ffn):
+def cut_tokens(h, other, at, tokens_t, norm_attn, norm_ffn):
     whole = lambda *shape: pl.BlockSpec(shape, lambda i: (0, 0))
     return pl.pallas_call(
         cut_kernel,
         grid=(1,),
         in_specs=[
+            pl.BlockSpec(memory_space=pltpu.SMEM),
+            pl.BlockSpec(memory_space=pltpu.SMEM),
             pl.BlockSpec(memory_space=pltpu.SMEM),
             whole(64, TOK),
             whole(1, 64),
@@ -338,7 +347,7 @@
         out_shape=(jax.ShapeDtypeStruct((HALF + 16, 64), BF),) * 2,
         compiler_params=params(),
         name="cut_tokens",
-    )(h, tokens_t, norm_attn.reshape(1, 64), norm_ffn.reshape(1, 64))
+    )(h, other, at, tokens_t, norm_attn.reshape(1, 64), norm_ffn.reshape(1, 64))
 
 
 def join_kernel(h_ref, keep_ref, got_ref, copies_ref):
@@ -369,8 +378,9 @@
 
 
 def gate_up_main_kernel(h_ref, x_ref, g_ref, wg_ref, wu_ref, *rest):
-    out_ref, xs = rest[-2:]
+    out_ref, made_ref, xs = rest[-3:]
     step = pl.program_id(0)
+    made_ref[0] = step
 
     @pl.when(step == 0)
     def _():
@@ -387,7 +397,7 @@
     wide = MAIN // steps
     in_specs = [
         pl.BlockSpec((CHIPS, HALF, LANE), lambda i, h: (0, 0, 0)),
-        pl.BlockSpec((CHIPS, 16, LANE), lambda i, h: (0, HALF // 16, 0)),
+        pl.BlockSpec((CHIPS, 16, LANE), lambda i, h: (0, 0, 0)),
         pl.BlockSpec((wide, 2048), lambda i, h: (i, 0)),
         pl.BlockSpec((wide, 2048), lambda i, h: (i, 0)),
     ]
@@ -403,10 +413,16 @@
             num_scalar_prefetch=1,
             grid=(steps,),
             in_specs=in_specs,
-            out_specs=pl.BlockSpec((HALF, 2 * MAIN), lambda i, h: (h[0], 0)),
+            out_specs=(
+                pl.BlockSpec((HALF, 2 * MAIN), lambda i, h: (h[0], 0)),
+                pl.BlockSpec(memory_space=pltpu.SMEM),
+            ),
             scratch_shapes=[pltpu.VMEM((HALF, 2048), BF)],
         ),
-        out_shape=jax.ShapeDtypeStruct((TOK, 2 * MAIN), BF),
+        out_shape=(
+            jax.ShapeDtypeStruct((TOK, 2 * MAIN), BF),
+            jax.ShapeDtypeStruct((1,), jnp.int32),
+        ),
         input_output_aliases=aliases,
         compiler_params=params(24),
         cost_estimate=pl.CostEstimate(
@@ -435,7 +451,7 @@
         out_ref[rows, SIDE // 2 :] = up.astype(BF)
 
 
-def gate_up_side(h, own, other, gains, wg_t, wu_t, main):
+def gate_up_side(h, own, other, gains, wg_t, wu_t, made):
     x_spec = pl.BlockSpec((CHIPS, HALF, LANE), lambda i, h: (0, 0, 0))
     w_spec = pl.BlockSpec((pl.Element(REST), pl.Element(2048)), lambda i, h: (MAIN, 0))
     return pl.pallas_call(
@@ -446,21 +462,21 @@
             in_specs=[
                 x_spec,
                 x_spec,
-                pl.BlockSpec((CHIPS, 16, LANE), lambda i, h: (0, HALF // 16, 0)),
+                pl.BlockSpec((CHIPS, 16, LANE), lambda i, h: (0, 0, 0)),
                 w_spec,
                 w_spec,
-                pl.BlockSpec(memory_space=pl.ANY),
+                pl.BlockSpec(memory_space=pltpu.SMEM),
             ],
             out_specs=pl.BlockSpec((TOK, SIDE), lambda i, h: (0, 0)),
             scratch_shapes=[pltpu.VMEM((HALF, 2048), BF)],
         ),
         out_shape=jax.ShapeDtypeStruct((TOK, SIDE), BF),
-        compiler_params=params(24),
+        compiler_params=params(58),
         cost_estimate=pl.CostEstimate(
             flops=4 * TOK * 2048 * REST, bytes_accessed=6 * 1024 * 1024, transcendentals=0
         ),
         name="gate_up_side",
-    )(h, own, other, gains, wg_t, wu_t, main)
+    )(h, own, other, gains, wg_t, wu_t, made)
 
 
 def hidden_kernel(main_ref, side_ref, out_ref):
@@ -499,7 +515,7 @@
         out_ref[lax.rem(at_ref[0] + k, ROWS)] = ref[...]
 
 
-def all_rows(x):
+def all_rows(at, x):
     ahead = {0: x}
     for k in (1, 7, 3, 5):
         ahead[k] = from_ahead(x, k)
@@ -507,7 +523,6 @@
     ahead[6] = from_ahead(ahead[7], 7)
     ahead[4] = from_ahead(ahead[3], 1)
     vmem = pl.BlockSpec(memory_space=pltpu.VMEM)
-    at = jnp.reshape(lax.axis_index("gx"), (1,)).astype(jnp.int32)
     return pl.pallas_call(
         order_kernel,
         in_specs=[pl.BlockSpec(memory_space=pltpu.SMEM)] + [vmem] * ROWS,
@@ -544,31 +559,31 @@
     lengths,
     segments,
 ):
-    core = lax.axis_index("gy") % 2
-    c = jnp.reshape(core, (1,)).astype(jnp.int32)
-
-    keep, give = cut_tokens(c, tokens.T, norm_attn, norm_ffn)
-    base = join_copies(c, keep, swap(give))
+    core, at = lax.axis_index("gy") % 2, jnp.reshape(lax.axis_index("gx"), (1,))
+    mine, theirs = jnp.reshape(core, (1,)), jnp.reshape(1 - core, (1,))
+
+    keep, give = cut_tokens(mine, theirs, at, tokens.T, norm_attn, norm_ffn)
+    base = join_copies(mine, keep, swap(give))
     first = over_chips(base)
     other = swap(first)
-    held = qkv_half(c, first, first, w_query, w_key.T, w_value.T)
-    parts = qkv_half(1 - c, other, first, w_query, w_key.T, w_value.T, held)
+    held, gains = qkv_half(mine, first, first, w_query, w_key.T, w_value.T)
+    parts, _ = qkv_half(theirs, other, first, w_query, w_key.T, w_value.T, held)
     q, kv = qkv_sum(over_rows(parts))
     kv = lax.all_to_all(kv, "gy", 0, 0, axis_index_groups=KV_GROUPS, tiled=True)
     attended = over_rows(attend(lengths, q, kv, segments)).reshape(TOK, 256)
-    residual, copies = residual_copies(base, project_out(c, attended, w_out))
+    residual, copies = residual_copies(base, project_out(mine, theirs, attended, w_out))
 
     own = over_chips(copies)
     other = swap(own)
     weights = (w_gate.T, w_up.T)
-    held = gate_up_main(c, own, first, *weights)
-    main = gate_up_main(1 - c, other, first, *weights, held)
-    side = gate_up_side(c, own, other, first, *weights, main)
+    held, _ = gate_up_main(mine, own, gains, *weights)
+    main, made = gate_up_main(theirs, other, gains, *weights, held)
+    side = gate_up_side(mine, own, other, gains, *weights, made)
     main = lax.psum_scatter(main, "gx", scatter_dimension=0, tiled=True)
     side = over_rows(side.reshape(ROWS, SEQ, SIDE))
-    hidden = all_rows(hidden_row(main, side)).reshape(TOK, FFL)
-    keep, give = final_sum(c, residual, project_out(c, hidden, w_down))
-    return place_halves(c, keep, swap(give))
+    hidden = all_rows(at, hidden_row(main, side)).reshape(TOK, FFL)
+    keep, give = final_sum(mine, residual, project_out(mine, theirs, hidden, w_down))
+    return place_halves(mine, keep, swap(give))
 
 
 def solution(mesh):

time: 292 us -> 286 us (0.979)
  local copies, waits for them, and re-layouts: 15.3 us -> 3.21 us
  Pallas kernels: 23.2 us -> 27.8 us
  waiting for transfers between devices: 19.6 us -> 23.8 us
    unnamed x44 -> x36, local copies, waits for them, and re-layouts: 15.3 us -> 3.21 us
    pallas_call x1, Pallas kernels: 2.46 us -> 6.34 us  [gate_up_side(): pl.pallas_call(gate_up_side_kernel, grid_spec=pltpu.PrefetchScalarGridSpe...]
    reduce_scatter x1, waiting for transfers between devices: 0.01 us -> 3.73 us  [per_device(): main = lax.psum_scatter(main, 'gx', scatter_dimension=0, tiled=True)]
  transfers between devices with their start and end apart: 15 -> 15, of which waited for: 11 -> 11; matrix products, arithmetic and copies ran while one was open for 0% -> 0% of each run, Pallas kernels for 3% -> 5%
where the time goes in v6:
time: 286 us; the launch traced here: 285 us
  blocking collectives  180 us (63%)
  starting transfers between devices  35.5 us (12%)
  Pallas kernels  27.8 us (10%)
  waiting for transfers between devices  23.8 us (8%)
  between operations  14.3 us (5%)
  local copies, waits for them, and re-layouts  3.21 us (1%)
    all_to_all x4, blocking collectives, over_chips(): lax.all_to_all(x, 'gy', 0, 0, axis_index_groups=CHIP_GROUPS, tiled=True)  106 us
    all_to_all x3, blocking collectives, over_rows(): return lax.all_to_all(x, 'gx', 0, 0, tiled=True)  74.4 us
    ppermute x7, starting transfers between devices, from_ahead(): return lax.ppermute(x, 'gx', [(i, (i - k) % ROWS) for i in range(ROWS)])  15.9 us
    ppermute x6, starting transfers between devices, swap(): return lax.ppermute(x, 'gy', [(i, i ^ 1) for i in range(32)])  14.6 us
    ppermute x7, waiting for transfers between devices, from_ahead(): return lax.ppermute(x, 'gx', [(i, (i - k) % ROWS) for i in range(ROWS)])  9.31 us
    pallas_call x2, Pallas kernels, gate_up_main(): pl.pallas_call(gate_up_main_kernel, grid_spec=pltpu.PrefetchScalarGridSpe...  7.21 us
    pallas_call x1, Pallas kernels, gate_up_side(): pl.pallas_call(gate_up_side_kernel, grid_spec=pltpu.PrefetchScalarGridSpe...  6.34 us
    pallas_call x4, Pallas kernels, proj_half(): pl.pallas_call(proj_kernel, grid_spec=pltpu.PrefetchScalarGridSpec(num_sc...  6.15 us
  transfers between devices with their start and end apart: 15, of which 11 were waited for; matrix products, arithmetic and copies ran while one was open for 0% of the time, Pallas kernels for 5%

profile of v6, /device:TPU:1, one launch (start us, length us, event | category | flops | bytes accessed | tf_op | source)
XLA Modules:
  0.0 285.5 jit_solution(13163230773986322322)
XLA Ops:
  8.8 3.3 %collective-permute-start = (bf16[400,64]{1,0:T(8,128)(2,1)S(1)}, bf16[400,64]{1,0:T(8,128)(2,1)S(1)}, u32[]{:S(2)}, u32[]{:S(2)}) collective-permute-start(bf16[400,64]{1,0:T(8,128)(2,1)S(1)} %get-tuple-element.20), channel_id=1, source_target_pairs={{0,1},{1,0},{2,3},{3,2},{4,5},{5,4},{6,7},{7,6},{8,9},{9,8},{10,11... | collective-permute-start | bytes 153608 | tf_op jit(solution)/shard_map/ppermute | solution.py:38
  13.5 27.8 %all_to_all.40.x_ref.g_ref = bf16[16,400,128]{2,1,0:T(8,128)(2,1)S(1)} all-to-all(bf16[16,400,128]{2,1,0:T(8,128)(2,1)S(1)} %join_copies.1.base_ref), channel_id=1, replica_groups={{0,2,4,6,8,10,12,14,16,18,20,22,24,26,28,30},{1,3,5,7,9,11,13,15,17,19,..., dimensions={0} | all-to-all | bytes 3276800 | tf_op jit(solution)/shard_map/all_to_all | solution.py:42
  46.2 2.7 qkv_half.3
  48.9 24.8 %all_to_all.41.p_ref = bf16[8,128,256]{2,1,0:T(8,128)(2,1)S(1)} all-to-all(bf16[8,128,256]{2,1,0:T(8,128)(2,1)S(1)} %get-tuple-element.22), channel_id=1, replica_groups=mesh['gx'=8,'gy'=32] {'gx'}, dimensions={0} | all-to-all | bytes 1048576 | tf_op jit(solution)/shard_map/all_to_all | solution.py:46
  74.4 5.0 %all-to-all-start.2 = ((f32[8,32,96]{2,1,0:T(8,128)}), f32[8,32,96]{2,1,0:T(8,128)S(1)}, u32[]{:S(2)}, u32[]{:S(2)}) async-start(f32[8,32,96]{2,1,0:T(8,128)} %get-tuple-element.24), calls=%async_computation.2 | async-start | bytes 262144 | tf_op jit(solution)/shard_map/all_to_all | solution.py:572
  80.0 4.6 %all-to-all-done.2.kv_ref = f32[8,32,96]{2,1,0:T(8,128)S(1)} async-done(((f32[8,32,96]{2,1,0:T(8,128)}), f32[8,32,96]{2,1,0:T(8,128)S(1)}, u32[]{:S(2)}, u32[]{:S(2)}) %all-to-all-start.2) | async-done | bytes 98336 | tf_op jit(solution)/shard_map/all_to_all | solution.py:572
  85.3 15.9 %all_to_all.42 = bf16[8,96,256]{2,1,0:T(8,128)(2,1)S(1)} all-to-all(bf16[8,96,256]{2,1,0:T(8,128)(2,1)S(1)} %attend.1), channel_id=1, replica_groups=mesh['gx'=8,'gy'=32] {'gx'}, dimensions={0} | all-to-all | bytes 786432 | tf_op jit(solution)/shard_map/all_to_all | solution.py:46
  107.7 24.9 %all_to_all.43.p_ref = bf16[16,384,128]{2,1,0:T(8,128)(2,1)S(1)} all-to-all(bf16[16,384,128]{2,1,0:T(8,128)(2,1)S(1)} %add_convert_fusion.1), channel_id=1, replica_groups={{0,2,4,6,8,10,12,14,16,18,20,22,24,26,28,30},{1,3,5,7,9,11,13,15,17,19,..., dimensions={0} | all-to-all | bytes 3145728 | tf_op jit(solution)/shard_map/all_to_all | solution.py:42
  132.9 24.8 %all_to_all.44.x_ref.own_ref = bf16[16,384,128]{2,1,0:T(8,128)(2,1)S(1)} all-to-all(bf16[16,384,128]{2,1,0:T(8,128)(2,1)S(1)} %get-tuple-element.26), channel_id=1, replica_groups={{0,2,4,6,8,10,12,14,16,18,20,22,24,26,28,30},{1,3,5,7,9,11,13,15,17,19,..., dimensions={0} | all-to-all | bytes 3145728 | tf_op jit(solution)/shard_map/all_to_all | solution.py:42
  157.7 2.3 collective-permute-start.3
  160.1 3.6 %gate_up_main.2 = (bf16[768,1280]{1,0:T(8,128)(2,1)}, s32[1]{0:T(128)}) custom-call(s32[1]{0:T(128)} %bitcast.h_ref, bf16[16,384,128]{2,1,0:T(8,128)(2,1)S(1)} %all_to_all.44.x_ref.own_ref, bf16[16,16,128]{2,1,0:T(8,128)(2,1)S(1)} %get-tuple-element.27.g_ref, bf16[832,2048]{1,0:T(8,128)(2,1)S(1)} %bitcast.16, bf16[832,2048]{1,0:T(8,128)(2,1)S(1)} %bitcast.19), custom_call_target="tpu_custom_call" | custom-call | flops 2013265920 | bytes 8388608 | tf_op jit(solution)/shard_map/gate_up_main/pallas_call | solution.py:410
  163.7 3.6 %gate_up_main.3 = (bf16[768,1280]{1,0:T(8,128)(2,1)}, s32[1]{0:T(128)}) custom-call(s32[1]{0:T(128)} %bitcast.1.other_ref.h_ref, bf16[16,384,128]{2,1,0:T(8,128)(2,1)S(1)} %collective-permute-done.3.x_ref.other_ref, bf16[16,16,128]{2,1,0:T(8,128)(2,1)S(1)} %get-tuple-element.27.g_ref, ...), custom_call_target="tpu_custom_call", output_to_operand_aliasing={{0}: (5, {})} | custom-call | flops 2013265920 | bytes 8388608 | tf_op jit(solution)/shard_map/gate_up_main/pallas_call | solution.py:410
  167.4 6.3 %gate_up_side.1 = bf16[768,512]{1,0:T(8,128)(2,1)} custom-call(s32[1]{0:T(128)} %bitcast.h_ref, bf16[16,384,128]{2,1,0:T(8,128)(2,1)} %copy-done.4, bf16[16,384,128]{2,1,0:T(8,128)(2,1)} %copy-done.6, bf16[16,16,128]{2,1,0:T(8,128)(2,1)} %copy-done.9, bf16[832,2048]{1,0:T(8,128)(2,1)} %bitcast.15, bf16[832,2048]{1,0:T(8,128)(2,1)} %bitcast.18, ...), custom_call_target="tpu_custom_call" | custom-call | flops 1207959552 | bytes 6291456 | tf_op jit(solution)/shard_map/gate_up_side/pallas_call | solution.py:457
  173.7 33.7 %all_to_all.45.side_ref = bf16[8,96,512]{2,1,0:T(8,128)(2,1)S(1)} all-to-all(bf16[8,96,512]{2,1,0:T(8,128)(2,1)} %bitcast.33), channel_id=1, replica_groups=mesh['gx'=8,'gy'=32] {'gx'}, dimensions={0} | all-to-all | bytes 1572864 | tf_op jit(solution)/shard_map/all_to_all | solution.py:46
  207.4 3.7 %reduce-scatter.2.cloned.1.call-done.main_ref = bf16[96,1280]{1,0:T(8,128)(2,1)} async-done(((bf16[768,1280]{1,0:T(8,128)(2,1)}), bf16[96,1280]{1,0:T(8,128)(2,1)}) %reduce-scatter.2.cloned.1.call-update) | async-done | bytes 245776 | tf_op jit(solution)/shard_map/reduce_scatter | solution.py:582
  213.6 2.5 collective-permute-start.6
  220.5 7.9 %collective-permute-start.7 = (bf16[96,832]{1,0:T(8,128)(2,1)S(1)}, bf16[96,832]{1,0:T(8,128)(2,1)S(1)}, u32[]{:S(2)}, u32[]{:S(2)}) collective-permute-start(bf16[96,832]{1,0:T(8,128)(2,1)S(1)} %collective-permute-done.6.refs_3_), channel_id=1, source_target_pairs={{0,224},{32,0},{64,32},{96,64},{128,96},{160,128},{192,160},{224,1... | collective-permute-start | bytes 479240 | tf_op jit(solution)/shard_map/ppermute | solution.py:509
  228.4 3.3 %collective-permute-done.4.refs_1_ = bf16[96,832]{1,0:T(8,128)(2,1)S(1)} collective-permute-done((bf16[96,832]{1,0:T(8,128)(2,1)S(1)}, bf16[96,832]{1,0:T(8,128)(2,1)S(1)}, u32[]{:S(2)}, u32[]{:S(2)}) %collective-permute-start.4) | collective-permute-done | bytes 159776 | tf_op jit(solution)/shard_map/ppermute | solution.py:509
  231.9 2.9 %collective-permute-done.10.refs_6_ = bf16[96,832]{1,0:T(8,128)(2,1)S(1)} collective-permute-done((bf16[96,832]{1,0:T(8,128)(2,1)S(1)}, bf16[96,832]{1,0:T(8,128)(2,1)S(1)}, u32[]{:S(2)}, u32[]{:S(2)}) %collective-permute-start.10) | collective-permute-done | bytes 159776 | tf_op jit(solution)/shard_map/ppermute | solution.py:509
  234.8 2.8 collective-permute-done.5.refs_2_
  237.7 2.2 proj_half.7
  240.0 3.1 %collective-permute-start.11 = (bf16[16,384,128]{2,1,0:T(8,128)(2,1)S(1)}, bf16[16,384,128]{2,1,0:T(8,128)(2,1)S(1)}, u32[]{:S(2)}, u32[]{:S(2)}) collective-permute-start(bf16[16,384,128]{2,1,0:T(8,128)(2,1)S(1)} %proj_half.7), channel_id=1, source_target_pairs={{0,1},{1,0},{2,3},{3,2},{4,5},{5,4},{6,7},{7,6},{8,9},{9,8},{10,11... | collective-permute-start | bytes 4718600 | tf_op jit(solution)/shard_map/ppermute | solution.py:38
  243.1 2.2 proj_half.6
  246.5 28.2 %all_to_all.46.p_ref = bf16[16,384,128]{2,1,0:T(8,128)(2,1)S(1)} all-to-all(bf16[16,384,128]{2,1,0:T(8,128)(2,1)S(1)} %add_convert_fusion), channel_id=1, replica_groups={{0,2,4,6,8,10,12,14,16,18,20,22,24,26,28,30},{1,3,5,7,9,11,13,15,17,19,..., dimensions={0} | all-to-all | bytes 3145728 | tf_op jit(solution)/shard_map/all_to_all | solution.py:42
  (70 shorter events, 28.7 us)
Async XLA Ops:
  8.8 4.3 %collective-permute-start = (bf16[400,64]{1,0:T(8,128)(2,1)S(1)}, bf16[400,64]{1,0:T(8,128)(2,1)S(1)}, u32[]{:S(2)}, u32[]{:S(2)}) collective-permute-start(bf16[400,64]{1,0:T(8,128)(2,1)S(1)} %get-tuple-element.20), channel_id=1, source_target_pairs={{0,1},{1,0},{2,3},{3,2},{4,5},{5,4},{6,7},{7,6},{8,9},{9,8},{10,11... | collective-permute-start | bytes 153608 | tf_op jit(solution)/shard_map/ppermute | solution.py:38
  13.4 27.8 %copy-start.2 = (bf16[16,400,128]{2,1,0:T(8,128)(2,1)}, bf16[16,400,128]{2,1,0:T(8,128)(2,1)S(1)}, u32[]{:S(2)}) copy-start(bf16[16,400,128]{2,1,0:T(8,128)(2,1)S(1)} %join_copies.1.base_ref) | copy-start | bytes 4915204
  13.4 29.6 %copy-start.7 = (bf16[2048,256]{1,0:T(8,128)(2,1)S(1)}, bf16[2048,256]{1,0:T(8,128)(2,1)}, u32[]{:S(2)}) copy-start(bf16[2048,256]{1,0:T(8,128)(2,1)} %wq_ref.3) | copy-start | bytes 3145732
  13.5 29.6 %copy-start.10 = (bf16[2048,16]{0,1:T(8,128)(2,1)S(1)}, bf16[2048,16]{0,1:T(8,128)(2,1)}, u32[]{:S(2)}) copy-start(bf16[2048,16]{0,1:T(8,128)(2,1)} %param.16) | copy-start | bytes 196612
  13.5 29.6 %copy-start.11 = (bf16[2048,16]{0,1:T(8,128)(2,1)S(1)}, bf16[2048,16]{0,1:T(8,128)(2,1)}, u32[]{:S(2)}) copy-start(bf16[2048,16]{0,1:T(8,128)(2,1)} %param.17) | copy-start | bytes 196612
  41.2 4.9 %collective-permute-start.1 = (bf16[16,400,128]{2,1,0:T(8,128)(2,1)S(1)}, bf16[16,400,128]{2,1,0:T(8,128)(2,1)S(1)}, u32[]{:S(2)}, u32[]{:S(2)}) collective-permute-start(bf16[16,400,128]{2,1,0:T(8,128)(2,1)S(1)} %all_to_all.40.x_ref.g_ref), channel_id=1, source_target_pairs={{0,1},{1,0},{2,3},{3,2},{4,5},{5,4},{6,7},{7,6},{8,9},{9,8},{10,11... | collective-permute-start | bytes 4915208 | tf_op jit(solution)/shard_map/ppermute | solution.py:38
  44.9 118.8 %copy-start.9 = (bf16[16,16,128]{2,1,0:T(8,128)(2,1)}, bf16[16,16,128]{2,1,0:T(8,128)(2,1)S(1)}, u32[]{:S(2)}) copy-start(bf16[16,16,128]{2,1,0:T(8,128)(2,1)S(1)} %get-tuple-element.27.g_ref) | copy-start | bytes 196612
  48.9 35.8 %copy-start.13 = (f32[2,128,128]{2,1,0:T(8,128)S(1)}, f32[2,128,128]{2,1,0:T(8,128)}, u32[]{:S(2)}) copy-start(f32[2,128,128]{2,1,0:T(8,128)} %constant.25.clone.table_ref) | copy-start | bytes 393220
  48.9 35.8 %copy-start.17 = (s32[96]{0:T(128)S(1)}, s32[96]{0:T(128)}, u32[]{:S(2)}) copy-start(s32[96]{0:T(128)} %param.24) | copy-start | bytes 1156
  48.9 52.4 %copy-start.8 = (bf16[256,2048]{1,0:T(8,128)(2,1)S(1)}, bf16[256,2048]{1,0:T(8,128)(2,1)}, u32[]{:S(2)}) copy-start(bf16[256,2048]{1,0:T(8,128)(2,1)} %w_ref.5) | copy-start | bytes 3145732
  74.4 10.3 %all-to-all-start.2 = ((f32[8,32,96]{2,1,0:T(8,128)}), f32[8,32,96]{2,1,0:T(8,128)S(1)}, u32[]{:S(2)}, u32[]{:S(2)}) async-start(f32[8,32,96]{2,1,0:T(8,128)} %get-tuple-element.24), calls=%async_computation.2 | async-start | bytes 262144 | tf_op jit(solution)/shard_map/all_to_all | solution.py:572
  79.4 131.7 %reduce-scatter.2.cloned.1.call-start = ((), (), s32[]{:S(2)}) async-start(), calls=%async_computation.9 | async-start | bytes 2211840 | tf_op jit(solution)/shard_map/reduce_scatter | solution.py:582
  102.1 5.2 %collective-permute-start.2 = (bf16[16,384,128]{2,1,0:T(8,128)(2,1)S(1)}, bf16[16,384,128]{2,1,0:T(8,128)(2,1)S(1)}, u32[]{:S(2)}, u32[]{:S(2)}) collective-permute-start(bf16[16,384,128]{2,1,0:T(8,128)(2,1)S(1)} %proj_half.5), channel_id=1, source_target_pairs={{0,1},{1,0},{2,3},{3,2},{4,5},{5,4},{6,7},{7,6},{8,9},{9,8},{10,11... | collective-permute-start | bytes 4718600 | tf_op jit(solution)/shard_map/ppermute | solution.py:38
  107.7 52.4 %copy-start.1 = (bf16[2048,832]{0,1:T(8,128)(2,1)S(1)}, bf16[2048,832]{0,1:T(8,128)(2,1)}, u32[]{:S(2)}) copy-start(bf16[2048,832]{0,1:T(8,128)(2,1)} %param.21) | copy-start | bytes 10223620
  157.7 6.0 %collective-permute-start.3 = (bf16[16,384,128]{2,1,0:T(8,128)(2,1)S(1)}, bf16[16,384,128]{2,1,0:T(8,128)(2,1)S(1)}, u32[]{:S(2)}, u32[]{:S(2)}) collective-permute-start(bf16[16,384,128]{2,1,0:T(8,128)(2,1)S(1)} %all_to_all.44.x_ref.own_ref), channel_id=1, source_target_pairs={{0,1},{1,0},{2,3},{3,2},{4,5},{5,4},{6,7},{7,6},{8,9},{9,8},{10,11... | collective-permute-start | bytes 4718600 | tf_op jit(solution)/shard_map/ppermute | solution.py:38
  212.4 6.0 %collective-permute-start.9 = (bf16[96,832]{1,0:T(8,128)(2,1)S(1)}, bf16[96,832]{1,0:T(8,128)(2,1)S(1)}, u32[]{:S(2)}, u32[]{:S(2)}) collective-permute-start(bf16[96,832]{1,0:T(8,128)(2,1)S(1)} %hidden_row.1.refs_0_), channel_id=1, source_target_pairs={{0,32},{32,64},{64,96},{96,128},{128,160},{160,192},{192,224},{224... | collective-permute-start | bytes 479240 | tf_op jit(solution)/shard_map/ppermute | solution.py:509
  213.6 6.9 %collective-permute-start.6 = (bf16[96,832]{1,0:T(8,128)(2,1)S(1)}, bf16[96,832]{1,0:T(8,128)(2,1)S(1)}, u32[]{:S(2)}, u32[]{:S(2)}) collective-permute-start(bf16[96,832]{1,0:T(8,128)(2,1)S(1)} %hidden_row.1.refs_0_), channel_id=1, source_target_pairs={{0,160},{32,192},{64,224},{96,0},{128,32},{160,64},{192,96},{224,1... | collective-permute-start | bytes 479240 | tf_op jit(solution)/shard_map/ppermute | solution.py:509
  216.1 15.6 %collective-permute-start.4 = (bf16[96,832]{1,0:T(8,128)(2,1)S(1)}, bf16[96,832]{1,0:T(8,128)(2,1)S(1)}, u32[]{:S(2)}, u32[]{:S(2)}) collective-permute-start(bf16[96,832]{1,0:T(8,128)(2,1)S(1)} %hidden_row.1.refs_0_), channel_id=1, source_target_pairs={{0,224},{32,0},{64,32},{96,64},{128,96},{160,128},{192,160},{224,1... | collective-permute-start | bytes 479240 | tf_op jit(solution)/shard_map/ppermute | solution.py:509
  217.6 14.3 %collective-permute-start.8 = (bf16[96,832]{1,0:T(8,128)(2,1)S(1)}, bf16[96,832]{1,0:T(8,128)(2,1)S(1)}, u32[]{:S(2)}, u32[]{:S(2)}) collective-permute-start(bf16[96,832]{1,0:T(8,128)(2,1)S(1)} %hidden_row.1.refs_0_), channel_id=1, source_target_pairs={{0,96},{32,128},{64,160},{96,192},{128,224},{160,0},{192,32},{224,... | collective-permute-start | bytes 479240 | tf_op jit(solution)/shard_map/ppermute | solution.py:509
  218.4 16.4 %collective-permute-start.10 = (bf16[96,832]{1,0:T(8,128)(2,1)S(1)}, bf16[96,832]{1,0:T(8,128)(2,1)S(1)}, u32[]{:S(2)}, u32[]{:S(2)}) collective-permute-start(bf16[96,832]{1,0:T(8,128)(2,1)S(1)} %collective-permute-done.9.refs_7_), channel_id=1, source_target_pairs={{0,32},{32,64},{64,96},{96,128},{128,160},{160,192},{192,224},{224... | collective-permute-start | bytes 479240 | tf_op jit(solution)/shard_map/ppermute | solution.py:509
  220.5 14.4 %collective-permute-start.7 = (bf16[96,832]{1,0:T(8,128)(2,1)S(1)}, bf16[96,832]{1,0:T(8,128)(2,1)S(1)}, u32[]{:S(2)}, u32[]{:S(2)}) collective-permute-start(bf16[96,832]{1,0:T(8,128)(2,1)S(1)} %collective-permute-done.6.refs_3_), channel_id=1, source_target_pairs={{0,224},{32,0},{64,32},{96,64},{128,96},{160,128},{192,160},{224,1... | collective-permute-start | bytes 479240 | tf_op jit(solution)/shard_map/ppermute | solution.py:509
  231.7 5.9 %collective-permute-start.5 = (bf16[96,832]{1,0:T(8,128)(2,1)S(1)}, bf16[96,832]{1,0:T(8,128)(2,1)S(1)}, u32[]{:S(2)}, u32[]{:S(2)}) collective-permute-start(bf16[96,832]{1,0:T(8,128)(2,1)S(1)} %collective-permute-done.4.refs_1_), channel_id=1, source_target_pairs={{0,224},{32,0},{64,32},{96,64},{128,96},{160,128},{192,160},{224,1... | collective-permute-start | bytes 479240 | tf_op jit(solution)/shard_map/ppermute | solution.py:509
  240.0 6.2 %collective-permute-start.11 = (bf16[16,384,128]{2,1,0:T(8,128)(2,1)S(1)}, bf16[16,384,128]{2,1,0:T(8,128)(2,1)S(1)}, u32[]{:S(2)}, u32[]{:S(2)}) collective-permute-start(bf16[16,384,128]{2,1,0:T(8,128)(2,1)S(1)} %proj_half.7), channel_id=1, source_target_pairs={{0,1},{1,0},{2,3},{3,2},{4,5},{5,4},{6,7},{7,6},{8,9},{9,8},{10,11... | collective-permute-start | bytes 4718600 | tf_op jit(solution)/shard_map/ppermute | solution.py:38
  275.1 2.8 collective-permute-start.12
  (9 other events, 91.2 us)
Sparse Core Ops, SparseCore 0:
  167.5 43.5 reduce-scatter.1

commit v7 on v6

--- a/solution.py
+++ b/solution.py
@@ -27,9 +27,9 @@
 ROWS = 8
 KSTEP = 4
 FFL = 832
-MAIN = 640
+MAIN = 768
 REST = FFL - MAIN
-SIDE = 512
+SIDE = 256
 CHIP_GROUPS = [[2 * i + c for i in range(CHIPS)] for c in range(2)]
 KV_GROUPS = [list(range(8 * i, 8 * i + 8)) for i in range(4)]
 
@@ -97,16 +97,16 @@
     @pl.when(k == pl.num_programs(0) - 1)
     def _():
         high, low = split_two(jnp.sum(jnp.transpose(acc_sq[...]), axis=0, keepdims=True))
-        at = lax.broadcasted_iota(jnp.int32, (16, SEQ), 0)
-        gap = jnp.zeros((16, LANE - SEQ), F32)
+        def squeezed(row):
+            cuts = [row[:, j * 32 : (j + 1) * 32] for j in range(SEQ // 32)]
+            return jnp.concatenate(cuts + [jnp.zeros((16 - SEQ // 32, 32), F32)], axis=0)
+
         for r in range(HALF // SEQ):
             here = slice(r * SEQ, (r + 1) * SEQ)
+            kv = acc_kv[:, here]
             out_ref[r, :SEQ] = acc_q[here].astype(BF)
-            kv = acc_kv[:, here]
-            sums = jnp.where(at == 0, high[:, here], jnp.where(at == 1, low[:, here], 0.0))
-            top = jnp.concatenate([kv[:16], gap, kv[16:], gap], axis=1)
-            bottom = jnp.concatenate([sums, gap, sums, gap], axis=1)
-            out_ref[r, SEQ:] = jnp.concatenate([top, bottom], axis=0).astype(BF)
+            below = [kv[:16], squeezed(high[:, here]), kv[16:], squeezed(low[:, here])]
+            out_ref[r, SEQ:] = jnp.concatenate(below, axis=1).astype(BF)
 
 
 def qkv_half(h, x, gains, wq, wk_t, wv_t, held=None):
@@ -132,7 +132,7 @@
             grid=(KSTEP,),
             in_specs=in_specs,
             out_specs=(
-                pl.BlockSpec((HALF // SEQ, 128, 256), lambda k, h: (h[0], 0, 0)),
+                pl.BlockSpec((HALF // SEQ, SEQ + 16, 256), lambda k, h: (h[0], 0, 0)),
                 pl.BlockSpec((chips, 16, LANE), lambda k, h: (k, 0, 0)),
             ),
             scratch_shapes=[
@@ -142,7 +142,7 @@
             ],
         ),
         out_shape=(
-            jax.ShapeDtypeStruct((ROWS, 128, 256), BF),
+            jax.ShapeDtypeStruct((ROWS, SEQ + 16, 256), BF),
             jax.ShapeDtypeStruct((CHIPS, 16, LANE), BF),
         ),
         input_output_aliases=aliases,
@@ -158,7 +158,8 @@
     total = p_ref[0].astype(F32)
     for j in range(1, ROWS):
         total = total + p_ref[j].astype(F32)
-    squares = total[112:113, :LANE] + total[113:114, :LANE]
+    extra = total[SEQ:, SEQ:LANE] + total[SEQ:, LANE + SEQ :]
+    squares = jnp.concatenate([extra[j : j + 1] for j in range(3)] + [extra[3:4]], axis=1)
     inv = lax.rsqrt(squares / D + EPS)
     down = jnp.transpose(jnp.broadcast_to(inv, (LANE, LANE)))[:SEQ]
     q_ref[...] = total[:SEQ] * jnp.concatenate([down, down], axis=1)

time: 286 us -> 280 us (0.979)
  blocking collectives: 180 us -> 167 us
  waiting for transfers between devices: 23.8 us -> 31 us
    all_to_all x3, blocking collectives: 74.4 us -> 61.3 us  [over_rows(): return lax.all_to_all(x, 'gx', 0, 0, tiled=True)]
    reduce_scatter x1, waiting for transfers between devices: 3.73 us -> 11.5 us  [per_device(): main = lax.psum_scatter(main, 'gx', scatter_dimension=0, tiled=True)]
where the time goes in v7:
time: 280 us
  blocking collectives  167 us (60%)
  starting transfers between devices  35.2 us (13%)
  waiting for transfers between devices  31 us (11%)
  Pallas kernels  27.7 us (10%)
  between operations  14.3 us (5%)
  local copies, waits for them, and re-layouts  4.21 us (2%)
    all_to_all x4, blocking collectives, over_chips(): lax.all_to_all(x, 'gy', 0, 0, axis_index_groups=CHIP_GROUPS, tiled=True)  105 us
    all_to_all x3, blocking collectives, over_rows(): return lax.all_to_all(x, 'gx', 0, 0, tiled=True)  61.3 us
    ppermute x7, starting transfers between devices, from_ahead(): return lax.ppermute(x, 'gx', [(i, (i - k) % ROWS) for i in range(ROWS)])  15.6 us
    ppermute x6, starting transfers between devices, swap(): return lax.ppermute(x, 'gy', [(i, i ^ 1) for i in range(32)])  14.6 us
    reduce_scatter x1, waiting for transfers between devices, per_device(): main = lax.psum_scatter(main, 'gx', scatter_dimension=0, tiled=True)  11.5 us
    ppermute x7, waiting for transfers between devices, from_ahead(): return lax.ppermute(x, 'gx', [(i, (i - k) % ROWS) for i in range(ROWS)])  8.87 us
    pallas_call x2, Pallas kernels, gate_up_main(): pl.pallas_call(gate_up_main_kernel, grid_spec=pltpu.PrefetchScalarGridSpe...  7.43 us
    pallas_call x4, Pallas kernels, proj_half(): pl.pallas_call(proj_kernel, grid_spec=pltpu.PrefetchScalarGridSpec(num_sc...  6.24 us
  transfers between devices with their start and end apart: 15, of which 11 were waited for; matrix products, arithmetic and copies ran while one was open for 0% of the time, Pallas kernels for 5%

profile of v7, /device:TPU:1, one launch (start us, length us, event | category | flops | bytes accessed | tf_op | source)
XLA Modules:
  0.0 279.7 jit_solution(17828034372947850749)
XLA Ops:
  8.8 3.3 %collective-permute-start = (bf16[400,64]{1,0:T(8,128)(2,1)S(1)}, bf16[400,64]{1,0:T(8,128)(2,1)S(1)}, u32[]{:S(2)}, u32[]{:S(2)}) collective-permute-start(bf16[400,64]{1,0:T(8,128)(2,1)S(1)} %get-tuple-element.20), channel_id=1, source_target_pairs={{0,1},{1,0},{2,3},{3,2},{4,5},{5,4},{6,7},{7,6},{8,9},{9,8},{10,11... | collective-permute-start | bytes 153608 | tf_op jit(solution)/shard_map/ppermute | solution.py:38
  13.5 27.6 %all_to_all.40.x_ref.g_ref = bf16[16,400,128]{2,1,0:T(8,128)(2,1)S(1)} all-to-all(bf16[16,400,128]{2,1,0:T(8,128)(2,1)S(1)} %join_copies.1.base_ref), channel_id=1, replica_groups={{0,2,4,6,8,10,12,14,16,18,20,22,24,26,28,30},{1,3,5,7,9,11,13,15,17,19,..., dimensions={0} | all-to-all | bytes 3276800 | tf_op jit(solution)/shard_map/all_to_all | solution.py:42
  46.0 2.8 qkv_half.3
  48.8 23.3 %all_to_all.41.p_ref = bf16[8,112,256]{2,1,0:T(8,128)(2,1)S(1)} all-to-all(bf16[8,112,256]{2,1,0:T(8,128)(2,1)S(1)} %get-tuple-element.22), channel_id=1, replica_groups=mesh['gx'=8,'gy'=32] {'gx'}, dimensions={0} | all-to-all | bytes 917504 | tf_op jit(solution)/shard_map/all_to_all | solution.py:46
  72.9 5.1 %all-to-all-start.2 = ((f32[8,32,96]{2,1,0:T(8,128)}), f32[8,32,96]{2,1,0:T(8,128)S(1)}, u32[]{:S(2)}, u32[]{:S(2)}) async-start(f32[8,32,96]{2,1,0:T(8,128)} %get-tuple-element.24), calls=%async_computation.2 | async-start | bytes 262144 | tf_op jit(solution)/shard_map/all_to_all | solution.py:573
  78.6 4.6 %all-to-all-done.2.kv_ref = f32[8,32,96]{2,1,0:T(8,128)S(1)} async-done(((f32[8,32,96]{2,1,0:T(8,128)}), f32[8,32,96]{2,1,0:T(8,128)S(1)}, u32[]{:S(2)}, u32[]{:S(2)}) %all-to-all-start.2) | async-done | bytes 98336 | tf_op jit(solution)/shard_map/all_to_all | solution.py:573
  83.9 15.9 %all_to_all.42 = bf16[8,96,256]{2,1,0:T(8,128)(2,1)S(1)} all-to-all(bf16[8,96,256]{2,1,0:T(8,128)(2,1)S(1)} %attend.1), channel_id=1, replica_groups=mesh['gx'=8,'gy'=32] {'gx'}, dimensions={0} | all-to-all | bytes 786432 | tf_op jit(solution)/shard_map/all_to_all | solution.py:46
  103.7 2.2 collective-permute-done.2
  106.3 24.9 %all_to_all.43.p_ref = bf16[16,384,128]{2,1,0:T(8,128)(2,1)S(1)} all-to-all(bf16[16,384,128]{2,1,0:T(8,128)(2,1)S(1)} %add_convert_fusion.1), channel_id=1, replica_groups={{0,2,4,6,8,10,12,14,16,18,20,22,24,26,28,30},{1,3,5,7,9,11,13,15,17,19,..., dimensions={0} | all-to-all | bytes 3145728 | tf_op jit(solution)/shard_map/all_to_all | solution.py:42
  131.5 24.8 %all_to_all.44.x_ref.own_ref = bf16[16,384,128]{2,1,0:T(8,128)(2,1)S(1)} all-to-all(bf16[16,384,128]{2,1,0:T(8,128)(2,1)S(1)} %get-tuple-element.26), channel_id=1, replica_groups={{0,2,4,6,8,10,12,14,16,18,20,22,24,26,28,30},{1,3,5,7,9,11,13,15,17,19,..., dimensions={0} | all-to-all | bytes 3145728 | tf_op jit(solution)/shard_map/all_to_all | solution.py:42
  156.3 2.3 collective-permute-start.3
  158.7 3.7 %gate_up_main.2 = (bf16[768,1536]{1,0:T(8,128)(2,1)}, s32[1]{0:T(128)}) custom-call(s32[1]{0:T(128)} %bitcast.h_ref, bf16[16,384,128]{2,1,0:T(8,128)(2,1)S(1)} %all_to_all.44.x_ref.own_ref, bf16[16,16,128]{2,1,0:T(8,128)(2,1)S(1)} %get-tuple-element.27.g_ref, bf16[832,2048]{1,0:T(8,128)(2,1)S(1)} %bitcast.16, bf16[832,2048]{1,0:T(8,128)(2,1)S(1)} %bitcast.19), custom_call_target="tpu_custom_call" | custom-call | flops 2415919104 | bytes 8388608 | tf_op jit(solution)/shard_map/gate_up_main/pallas_call | solution.py:411
  162.4 3.7 %gate_up_main.3 = (bf16[768,1536]{1,0:T(8,128)(2,1)}, s32[1]{0:T(128)}) custom-call(s32[1]{0:T(128)} %bitcast.1.other_ref.h_ref, bf16[16,384,128]{2,1,0:T(8,128)(2,1)S(1)} %collective-permute-done.3.x_ref.other_ref, bf16[16,16,128]{2,1,0:T(8,128)(2,1)S(1)} %get-tuple-element.27.g_ref, ...), custom_call_target="tpu_custom_call", output_to_operand_aliasing={{0}: (5, {})} | custom-call | flops 2415919104 | bytes 8388608 | tf_op jit(solution)/shard_map/gate_up_main/pallas_call | solution.py:411
  166.2 5.8 %gate_up_side.1 = bf16[768,256]{1,0:T(8,128)(2,1)} custom-call(s32[1]{0:T(128)} %bitcast.h_ref, bf16[16,384,128]{2,1,0:T(8,128)(2,1)} %copy-done.3, bf16[16,384,128]{2,1,0:T(8,128)(2,1)} %copy-done.4, bf16[16,16,128]{2,1,0:T(8,128)(2,1)} %copy-done.11, bf16[832,2048]{1,0:T(8,128)(2,1)} %bitcast.15, bf16[832,2048]{1,0:T(8,128)(2,1)} %bitcast.18, ...), custom_call_target="tpu_custom_call" | custom-call | flops 402653184 | bytes 6291456 | tf_op jit(solution)/shard_map/gate_up_side/pallas_call | solution.py:458
  171.9 22.1 %all_to_all.45.side_ref = bf16[8,96,256]{2,1,0:T(8,128)(2,1)} all-to-all(bf16[8,96,256]{2,1,0:T(8,128)(2,1)} %bitcast.33), channel_id=1, replica_groups=mesh['gx'=8,'gy'=32] {'gx'}, dimensions={0} | all-to-all | bytes 786432 | tf_op jit(solution)/shard_map/all_to_all | solution.py:46
  194.0 11.5 %reduce-scatter.2.cloned.1.call-done.main_ref = bf16[96,1536]{1,0:T(8,128)(2,1)} async-done(((bf16[768,1536]{1,0:T(8,128)(2,1)}), bf16[96,1536]{1,0:T(8,128)(2,1)}) %reduce-scatter.2.cloned.1.call-update) | async-done | bytes 294928 | tf_op jit(solution)/shard_map/reduce_scatter | solution.py:583
  208.4 2.3 collective-permute-start.6
  214.9 7.5 %collective-permute-start.7 = (bf16[96,832]{1,0:T(8,128)(2,1)S(1)}, bf16[96,832]{1,0:T(8,128)(2,1)S(1)}, u32[]{:S(2)}, u32[]{:S(2)}) collective-permute-start(bf16[96,832]{1,0:T(8,128)(2,1)S(1)} %collective-permute-done.6.refs_3_), channel_id=1, source_target_pairs={{0,224},{32,0},{64,32},{96,64},{128,96},{160,128},{192,160},{224,1... | collective-permute-start | bytes 479240 | tf_op jit(solution)/shard_map/ppermute | solution.py:510
  225.1 4.7 %collective-permute-done.10.refs_6_ = bf16[96,832]{1,0:T(8,128)(2,1)S(1)} collective-permute-done((bf16[96,832]{1,0:T(8,128)(2,1)S(1)}, bf16[96,832]{1,0:T(8,128)(2,1)S(1)}, u32[]{:S(2)}, u32[]{:S(2)}) %collective-permute-start.10) | collective-permute-done | bytes 159776 | tf_op jit(solution)/shard_map/ppermute | solution.py:510
  229.8 2.4 collective-permute-done.5.refs_2_
  232.3 2.3 proj_half.7
  234.6 3.1 %collective-permute-start.11 = (bf16[16,384,128]{2,1,0:T(8,128)(2,1)S(1)}, bf16[16,384,128]{2,1,0:T(8,128)(2,1)S(1)}, u32[]{:S(2)}, u32[]{:S(2)}) collective-permute-start(bf16[16,384,128]{2,1,0:T(8,128)(2,1)S(1)} %proj_half.7), channel_id=1, source_target_pairs={{0,1},{1,0},{2,3},{3,2},{4,5},{5,4},{6,7},{7,6},{8,9},{9,8},{10,11... | collective-permute-start | bytes 4718600 | tf_op jit(solution)/shard_map/ppermute | solution.py:38
  237.7 2.2 proj_half.6
  241.1 27.8 %all_to_all.46.p_ref = bf16[16,384,128]{2,1,0:T(8,128)(2,1)S(1)} all-to-all(bf16[16,384,128]{2,1,0:T(8,128)(2,1)S(1)} %add_convert_fusion), channel_id=1, replica_groups={{0,2,4,6,8,10,12,14,16,18,20,22,24,26,28,30},{1,3,5,7,9,11,13,15,17,19,..., dimensions={0} | all-to-all | bytes 3145728 | tf_op jit(solution)/shard_map/all_to_all | solution.py:42
  (68 shorter events, 29.4 us)
Async XLA Ops:
  8.8 4.3 %collective-permute-start = (bf16[400,64]{1,0:T(8,128)(2,1)S(1)}, bf16[400,64]{1,0:T(8,128)(2,1)S(1)}, u32[]{:S(2)}, u32[]{:S(2)}) collective-permute-start(bf16[400,64]{1,0:T(8,128)(2,1)S(1)} %get-tuple-element.20), channel_id=1, source_target_pairs={{0,1},{1,0},{2,3},{3,2},{4,5},{5,4},{6,7},{7,6},{8,9},{9,8},{10,11... | collective-permute-start | bytes 153608 | tf_op jit(solution)/shard_map/ppermute | solution.py:38
  13.4 29.4 %copy-start.5 = (bf16[2048,256]{1,0:T(8,128)(2,1)S(1)}, bf16[2048,256]{1,0:T(8,128)(2,1)}, u32[]{:S(2)}) copy-start(bf16[2048,256]{1,0:T(8,128)(2,1)} %wq_ref.3) | copy-start | bytes 3145732
  13.5 29.4 %copy-start.9 = (bf16[2048,16]{0,1:T(8,128)(2,1)S(1)}, bf16[2048,16]{0,1:T(8,128)(2,1)}, u32[]{:S(2)}) copy-start(bf16[2048,16]{0,1:T(8,128)(2,1)} %param.16) | copy-start | bytes 196612
  13.5 29.4 %copy-start.10 = (bf16[2048,16]{0,1:T(8,128)(2,1)S(1)}, bf16[2048,16]{0,1:T(8,128)(2,1)}, u32[]{:S(2)}) copy-start(bf16[2048,16]{0,1:T(8,128)(2,1)} %param.17) | copy-start | bytes 196612
  41.1 4.9 %collective-permute-start.1 = (bf16[16,400,128]{2,1,0:T(8,128)(2,1)S(1)}, bf16[16,400,128]{2,1,0:T(8,128)(2,1)S(1)}, u32[]{:S(2)}, u32[]{:S(2)}) collective-permute-start(bf16[16,400,128]{2,1,0:T(8,128)(2,1)S(1)} %all_to_all.40.x_ref.g_ref), channel_id=1, source_target_pairs={{0,1},{1,0},{2,3},{3,2},{4,5},{5,4},{6,7},{7,6},{8,9},{9,8},{10,11... | collective-permute-start | bytes 4915208 | tf_op jit(solution)/shard_map/ppermute | solution.py:38
  44.9 117.5 %copy-start.11 = (bf16[16,16,128]{2,1,0:T(8,128)(2,1)}, bf16[16,16,128]{2,1,0:T(8,128)(2,1)S(1)}, u32[]{:S(2)}) copy-start(bf16[16,16,128]{2,1,0:T(8,128)(2,1)S(1)} %get-tuple-element.27.g_ref) | copy-start | bytes 196612
  48.8 34.5 %copy-start.12 = (f32[2,128,128]{2,1,0:T(8,128)S(1)}, f32[2,128,128]{2,1,0:T(8,128)}, u32[]{:S(2)}) copy-start(f32[2,128,128]{2,1,0:T(8,128)} %constant.25.clone.table_ref) | copy-start | bytes 393220
  48.8 34.5 %copy-start.16 = (s32[96]{0:T(128)S(1)}, s32[96]{0:T(128)}, u32[]{:S(2)}) copy-start(s32[96]{0:T(128)} %param.24) | copy-start | bytes 1156
  48.8 51.0 %copy-start.6 = (bf16[256,2048]{1,0:T(8,128)(2,1)S(1)}, bf16[256,2048]{1,0:T(8,128)(2,1)}, u32[]{:S(2)}) copy-start(bf16[256,2048]{1,0:T(8,128)(2,1)} %w_ref.5) | copy-start | bytes 3145732
  72.9 10.4 %all-to-all-start.2 = ((f32[8,32,96]{2,1,0:T(8,128)}), f32[8,32,96]{2,1,0:T(8,128)S(1)}, u32[]{:S(2)}, u32[]{:S(2)}) async-start(f32[8,32,96]{2,1,0:T(8,128)} %get-tuple-element.24), calls=%async_computation.2 | async-start | bytes 262144 | tf_op jit(solution)/shard_map/all_to_all | solution.py:573
  78.0 127.5 %reduce-scatter.2.cloned.1.call-start = ((), (), s32[]{:S(2)}) async-start(), calls=%async_computation.9 | async-start | bytes 2654208 | tf_op jit(solution)/shard_map/reduce_scatter | solution.py:583
  100.7 5.2 %collective-permute-start.2 = (bf16[16,384,128]{2,1,0:T(8,128)(2,1)S(1)}, bf16[16,384,128]{2,1,0:T(8,128)(2,1)S(1)}, u32[]{:S(2)}, u32[]{:S(2)}) collective-permute-start(bf16[16,384,128]{2,1,0:T(8,128)(2,1)S(1)} %proj_half.5), channel_id=1, source_target_pairs={{0,1},{1,0},{2,3},{3,2},{4,5},{5,4},{6,7},{7,6},{8,9},{9,8},{10,11... | collective-permute-start | bytes 4718600 | tf_op jit(solution)/shard_map/ppermute | solution.py:38
  106.3 52.4 %copy-start.2 = (bf16[2048,832]{0,1:T(8,128)(2,1)S(1)}, bf16[2048,832]{0,1:T(8,128)(2,1)}, u32[]{:S(2)}) copy-start(bf16[2048,832]{0,1:T(8,128)(2,1)} %param.21) | copy-start | bytes 10223620
  156.3 6.1 %collective-permute-start.3 = (bf16[16,384,128]{2,1,0:T(8,128)(2,1)S(1)}, bf16[16,384,128]{2,1,0:T(8,128)(2,1)S(1)}, u32[]{:S(2)}, u32[]{:S(2)}) collective-permute-start(bf16[16,384,128]{2,1,0:T(8,128)(2,1)S(1)} %all_to_all.44.x_ref.own_ref), channel_id=1, source_target_pairs={{0,1},{1,0},{2,3},{3,2},{4,5},{5,4},{6,7},{7,6},{8,9},{9,8},{10,11... | collective-permute-start | bytes 4718600 | tf_op jit(solution)/shard_map/ppermute | solution.py:38
  194.0 38.3 %copy-start = (bf16[832,2048]{1,0:T(8,128)(2,1)S(1)}, bf16[832,2048]{1,0:T(8,128)(2,1)}, u32[]{:S(2)}) copy-start(bf16[832,2048]{1,0:T(8,128)(2,1)} %w_ref.7) | copy-start | bytes 10223620
  207.7 6.0 %collective-permute-start.9 = (bf16[96,832]{1,0:T(8,128)(2,1)S(1)}, bf16[96,832]{1,0:T(8,128)(2,1)S(1)}, u32[]{:S(2)}, u32[]{:S(2)}) collective-permute-start(bf16[96,832]{1,0:T(8,128)(2,1)S(1)} %hidden_row.1.refs_0_), channel_id=1, source_target_pairs={{0,32},{32,64},{64,96},{96,128},{128,160},{160,192},{192,224},{224... | collective-permute-start | bytes 479240 | tf_op jit(solution)/shard_map/ppermute | solution.py:510
  208.4 6.5 %collective-permute-start.6 = (bf16[96,832]{1,0:T(8,128)(2,1)S(1)}, bf16[96,832]{1,0:T(8,128)(2,1)S(1)}, u32[]{:S(2)}, u32[]{:S(2)}) collective-permute-start(bf16[96,832]{1,0:T(8,128)(2,1)S(1)} %hidden_row.1.refs_0_), channel_id=1, source_target_pairs={{0,160},{32,192},{64,224},{96,0},{128,32},{160,64},{192,96},{224,1... | collective-permute-start | bytes 479240 | tf_op jit(solution)/shard_map/ppermute | solution.py:510
  210.7 13.1 %collective-permute-start.4 = (bf16[96,832]{1,0:T(8,128)(2,1)S(1)}, bf16[96,832]{1,0:T(8,128)(2,1)S(1)}, u32[]{:S(2)}, u32[]{:S(2)}) collective-permute-start(bf16[96,832]{1,0:T(8,128)(2,1)S(1)} %hidden_row.1.refs_0_), channel_id=1, source_target_pairs={{0,224},{32,0},{64,32},{96,64},{128,96},{160,128},{192,160},{224,1... | collective-permute-start | bytes 479240 | tf_op jit(solution)/shard_map/ppermute | solution.py:510
  212.1 13.0 %collective-permute-start.8 = (bf16[96,832]{1,0:T(8,128)(2,1)S(1)}, bf16[96,832]{1,0:T(8,128)(2,1)S(1)}, u32[]{:S(2)}, u32[]{:S(2)}) collective-permute-start(bf16[96,832]{1,0:T(8,128)(2,1)S(1)} %hidden_row.1.refs_0_), channel_id=1, source_target_pairs={{0,96},{32,128},{64,160},{96,192},{128,224},{160,0},{192,32},{224,... | collective-permute-start | bytes 479240 | tf_op jit(solution)/shard_map/ppermute | solution.py:510
  213.8 16.0 %collective-permute-start.10 = (bf16[96,832]{1,0:T(8,128)(2,1)S(1)}, bf16[96,832]{1,0:T(8,128)(2,1)S(1)}, u32[]{:S(2)}, u32[]{:S(2)}) collective-permute-start(bf16[96,832]{1,0:T(8,128)(2,1)S(1)} %collective-permute-done.9.refs_7_), channel_id=1, source_target_pairs={{0,32},{32,64},{64,96},{96,128},{128,160},{160,192},{192,224},{224... | collective-permute-start | bytes 479240 | tf_op jit(solution)/shard_map/ppermute | solution.py:510
  214.9 14.9 %collective-permute-start.7 = (bf16[96,832]{1,0:T(8,128)(2,1)S(1)}, bf16[96,832]{1,0:T(8,128)(2,1)S(1)}, u32[]{:S(2)}, u32[]{:S(2)}) collective-permute-start(bf16[96,832]{1,0:T(8,128)(2,1)S(1)} %collective-permute-done.6.refs_3_), channel_id=1, source_target_pairs={{0,224},{32,0},{64,32},{96,64},{128,96},{160,128},{192,160},{224,1... | collective-permute-start | bytes 479240 | tf_op jit(solution)/shard_map/ppermute | solution.py:510
  223.8 8.4 %collective-permute-start.5 = (bf16[96,832]{1,0:T(8,128)(2,1)S(1)}, bf16[96,832]{1,0:T(8,128)(2,1)S(1)}, u32[]{:S(2)}, u32[]{:S(2)}) collective-permute-start(bf16[96,832]{1,0:T(8,128)(2,1)S(1)} %collective-permute-done.4.refs_1_), channel_id=1, source_target_pairs={{0,224},{32,0},{64,32},{96,64},{128,96},{160,128},{192,160},{224,1... | collective-permute-start | bytes 479240 | tf_op jit(solution)/shard_map/ppermute | solution.py:510
  234.6 6.1 %collective-permute-start.11 = (bf16[16,384,128]{2,1,0:T(8,128)(2,1)S(1)}, bf16[16,384,128]{2,1,0:T(8,128)(2,1)S(1)}, u32[]{:S(2)}, u32[]{:S(2)}) collective-permute-start(bf16[16,384,128]{2,1,0:T(8,128)(2,1)S(1)} %proj_half.7), channel_id=1, source_target_pairs={{0,1},{1,0},{2,3},{3,2},{4,5},{5,4},{6,7},{7,6},{8,9},{9,8},{10,11... | collective-permute-start | bytes 4718600 | tf_op jit(solution)/shard_map/ppermute | solution.py:38
  269.3 2.8 collective-permute-start.12
  (8 other events, 41.4 us)
Sparse Core Ops, SparseCore 0:
  166.3 39.1 reduce-scatter.1

commit v8 on v7

--- a/solution.py
+++ b/solution.py
@@ -40,6 +40,54 @@
 
 def over_chips(x):
     return lax.all_to_all(x, "gy", 0, 0, axis_index_groups=CHIP_GROUPS, tiled=True)
+
+
+def over_ring(x, k, stage):
+    pairs = []
+    for i in range(32):
+        y, across, core = i // 8, i // 2 % 4, i % 2
+        if (core == 0) == (stage == 0):
+            across = (across + k) % 4
+        else:
+            y = (y + k) % 4
+        pairs.append((y * 8 + across * 2 + core, i))
+    return lax.ppermute(x, "gy", pairs)
+
+
+def stack_kernel(*refs):
+    for j, ref in enumerate(refs[:-1]):
+        refs[-1][j] = ref[...]
+
+
+def order_chips_kernel(g_ref, *refs):
+    out_ref = refs[-1]
+    core = lax.rem(g_ref[0], 2)
+    across, y = lax.rem(lax.div(g_ref[0], 2), 4), lax.div(g_ref[0], 8)
+    for a in range(4):
+        for b in range(4):
+            here_y = lax.rem(y + jnp.where(core == 0, a, b), 4)
+            here_x = lax.rem(across + jnp.where(core == 0, b, a), 4)
+            out_ref[here_y * 4 + here_x] = refs[a][b]
+
+
+def from_chips(g, x):
+    vmem = pl.BlockSpec(memory_space=pltpu.VMEM)
+    line = pl.pallas_call(
+        stack_kernel,
+        in_specs=[vmem] * 4,
+        out_specs=vmem,
+        out_shape=jax.ShapeDtypeStruct((4,) + x.shape, x.dtype),
+        compiler_params=params(),
+        name="stack_line",
+    )(x, *[over_ring(x, k, 0) for k in (1, 2, 3)])
+    return pl.pallas_call(
+        order_chips_kernel,
+        in_specs=[pl.BlockSpec(memory_space=pltpu.SMEM)] + [vmem] * 4,
+        out_specs=vmem,
+        out_shape=jax.ShapeDtypeStruct((CHIPS,) + x.shape, x.dtype),
+        compiler_params=params(),
+        name="order_chips",
+    )(g, line, *[over_ring(line, k, 1) for k in (1, 2, 3)])
 
 
 def over_rows(x):
@@ -257,25 +305,19 @@
     return over_chips((kept + got.astype(F32)).astype(BF))
 
 
-def residual_kernel(base_ref, p_ref, out_ref, copies_ref):
+def residual_kernel(base_ref, p_ref, out_ref):
     total = p_ref[0].astype(F32)
     for j in range(1, CHIPS):
         total = total + p_ref[j].astype(F32)
-    result = (base_ref[0, :HALF].astype(F32) + total).astype(BF)
-    out_ref[...] = result
-    for j in range(CHIPS):
-        copies_ref[j] = result
-
-
-def residual_copies(base, parts):
+    out_ref[...] = (base_ref[:HALF].astype(F32) + total).astype(BF)
+
+
+def residual_sum(base, parts):
     return pl.pallas_call(
         residual_kernel,
-        out_shape=(
-            jax.ShapeDtypeStruct((HALF, LANE), BF),
-            jax.ShapeDtypeStruct((CHIPS, HALF, LANE), BF),
-        ),
-        compiler_params=params(),
-        name="residual_copies",
+        out_shape=jax.ShapeDtypeStruct((HALF, LANE), BF),
+        compiler_params=params(),
+        name="residual_sum",
     )(base, parts)
 
 
@@ -319,7 +361,7 @@
     )(h, keep, got).T
 
 
-def cut_kernel(h_ref, other_ref, at_ref, t_ref, ga_ref, gf_ref, keep_ref, give_ref):
+def cut_kernel(h_ref, other_ref, at_ref, place_ref, t_ref, ga_ref, gf_ref, keep_ref, give_ref):
     row = lax.broadcasted_iota(jnp.int32, (16, 64), 0)
     ga, gf = ga_ref[...].astype(F32), gf_ref[...].astype(F32)
     gains = jnp.where(row == 0, ga, jnp.where(row == 1, gf, 0.0)).astype(BF)
@@ -331,12 +373,13 @@
     give_ref[:HALF] = jnp.where(h_ref[0] == 0, second, first)
 
 
-def cut_tokens(h, other, at, tokens_t, norm_attn, norm_ffn):
+def cut_tokens(h, other, at, place, tokens_t, norm_attn, norm_ffn):
     whole = lambda *shape: pl.BlockSpec(shape, lambda i: (0, 0))
     return pl.pallas_call(
         cut_kernel,
         grid=(1,),
         in_specs=[
+            pl.BlockSpec(memory_space=pltpu.SMEM),
             pl.BlockSpec(memory_space=pltpu.SMEM),
             pl.BlockSpec(memory_space=pltpu.SMEM),
             pl.BlockSpec(memory_space=pltpu.SMEM),
@@ -348,27 +391,25 @@
         out_shape=(jax.ShapeDtypeStruct((HALF + 16, 64), BF),) * 2,
         compiler_params=params(),
         name="cut_tokens",
-    )(h, other, at, tokens_t, norm_attn.reshape(1, 64), norm_ffn.reshape(1, 64))
-
-
-def join_kernel(h_ref, keep_ref, got_ref, copies_ref):
+    )(h, other, at, place, tokens_t, norm_attn.reshape(1, 64), norm_ffn.reshape(1, 64))
+
+
+def join_kernel(h_ref, keep_ref, got_ref, out_ref):
     keep, got = keep_ref[...], got_ref[...]
     mine_first = jnp.concatenate([keep, got], axis=1)
     mine_last = jnp.concatenate([got, keep], axis=1)
-    base = jnp.where(h_ref[0] == 0, mine_first, mine_last)
-    for j in range(CHIPS):
-        copies_ref[j] = base
-
-
-def join_copies(h, keep, got):
+    out_ref[...] = jnp.where(h_ref[0] == 0, mine_first, mine_last)
+
+
+def join_cores(h, keep, got):
     vmem = pl.BlockSpec(memory_space=pltpu.VMEM)
     return pl.pallas_call(
         join_kernel,
         in_specs=[pl.BlockSpec(memory_space=pltpu.SMEM), vmem, vmem],
         out_specs=vmem,
-        out_shape=jax.ShapeDtypeStruct((CHIPS, HALF + 16, LANE), BF),
-        compiler_params=params(),
-        name="join_copies",
+        out_shape=jax.ShapeDtypeStruct((HALF + 16, LANE), BF),
+        compiler_params=params(),
+        name="join_cores",
     )(h, keep, got)
 
 
@@ -562,19 +603,20 @@
 ):
     core, at = lax.axis_index("gy") % 2, jnp.reshape(lax.axis_index("gx"), (1,))
     mine, theirs = jnp.reshape(core, (1,)), jnp.reshape(1 - core, (1,))
-
-    keep, give = cut_tokens(mine, theirs, at, tokens.T, norm_attn, norm_ffn)
-    base = join_copies(mine, keep, swap(give))
-    first = over_chips(base)
+    place = jnp.reshape(lax.axis_index("gy"), (1,))
+
+    keep, give = cut_tokens(mine, theirs, at, place, tokens.T, norm_attn, norm_ffn)
+    base = join_cores(mine, keep, swap(give))
+    first = from_chips(place, base)
     other = swap(first)
     held, gains = qkv_half(mine, first, first, w_query, w_key.T, w_value.T)
     parts, _ = qkv_half(theirs, other, first, w_query, w_key.T, w_value.T, held)
     q, kv = qkv_sum(over_rows(parts))
     kv = lax.all_to_all(kv, "gy", 0, 0, axis_index_groups=KV_GROUPS, tiled=True)
     attended = over_rows(attend(lengths, q, kv, segments)).reshape(TOK, 256)
-    residual, copies = residual_copies(base, project_out(mine, theirs, attended, w_out))
-
-    own = over_chips(copies)
+    residual = residual_sum(base, project_out(mine, theirs, attended, w_out))
+
+    own = from_chips(place, residual)
     other = swap(own)
     weights = (w_gate.T, w_up.T)
     held, _ = gate_up_main(mine, own, gains, *weights)

time: 280 us -> 276 us (0.986)
  blocking collectives: 167 us -> 118 us
  waiting for transfers between devices: 31 us -> 60.4 us
  starting transfers between devices: 35.2 us -> 50.6 us
    all_to_all x4 -> x2, blocking collectives: 105 us -> 55.3 us  [over_chips(): lax.all_to_all(x, 'gy', 0, 0, axis_index_groups=CHIP_GROUPS, tiled=True)]
    ppermute x0 -> x12, waiting for transfers between devices: none -> 26.2 us  [over_ring(): return lax.ppermute(x, 'gy', pairs)]
    ppermute x0 -> x12, starting transfers between devices: none -> 13.9 us  [over_ring(): return lax.ppermute(x, 'gy', pairs)]
    ppermute x6, starting transfers between devices: 14.6 us -> 18 us  [swap(): return lax.ppermute(x, 'gy', [(i, i ^ 1) for i in range(32)])]
  transfers between devices with their start and end apart: 15 -> 27, of which waited for: 11 -> 20; matrix products, arithmetic and copies ran while one was open for 0% -> 0% of each run, Pallas kernels for 5% -> 5%
where the time goes in v8:
time: 276 us
  blocking collectives  118 us (43%)
  waiting for transfers between devices  60.4 us (22%)
  starting transfers between devices  50.6 us (18%)
  Pallas kernels  27.7 us (10%)
  between operations  14.3 us (5%)
  local copies, waits for them, and re-layouts  4.21 us (2%)
    all_to_all x3, blocking collectives, over_rows(): return lax.all_to_all(x, 'gx', 0, 0, tiled=True)  62.3 us
    all_to_all x2, blocking collectives, over_chips(): lax.all_to_all(x, 'gy', 0, 0, axis_index_groups=CHIP_GROUPS, tiled=True)  55.3 us
    ppermute x12, waiting for transfers between devices, over_ring(): return lax.ppermute(x, 'gy', pairs)  26.2 us
    ppermute x6, starting transfers between devices, swap(): return lax.ppermute(x, 'gy', [(i, i ^ 1) for i in range(32)])  18 us
    ppermute x12, starting transfers between devices, over_ring(): return lax.ppermute(x, 'gy', pairs)  13.9 us
    ppermute x7, starting transfers between devices, from_ahead(): return lax.ppermute(x, 'gx', [(i, (i - k) % ROWS) for i in range(ROWS)])  12.9 us
    reduce_scatter x1, waiting for transfers between devices, per_device(): main = lax.psum_scatter(main, 'gx', scatter_dimension=0, tiled=True)  12.3 us
    ppermute x7, waiting for transfers between devices, from_ahead(): return lax.ppermute(x, 'gx', [(i, (i - k) % ROWS) for i in range(ROWS)])  11.3 us
  transfers between devices with their start and end apart: 27, of which 20 were waited for; matrix products, arithmetic and copies ran while one was open for 0% of the time, Pallas kernels for 5%

profile of v8, /device:TPU:1, one launch (start us, length us, event | category | flops | bytes accessed | tf_op | source)
XLA Modules:
  0.0 275.6 jit_solution(18181665557738685126)
XLA Ops:
  8.8 3.3 %collective-permute-start = (bf16[400,64]{1,0:T(8,128)(2,1)S(1)}, bf16[400,64]{1,0:T(8,128)(2,1)S(1)}, u32[]{:S(2)}, u32[]{:S(2)}) collective-permute-start(bf16[400,64]{1,0:T(8,128)(2,1)S(1)} %get-tuple-element.18), channel_id=1, source_target_pairs={{0,1},{1,0},{2,3},{3,2},{4,5},{5,4},{6,7},{7,6},{8,9},{9,8},{10,11... | collective-permute-start | bytes 153608 | tf_op jit(solution)/shard_map/ppermute | solution.py:38
  16.6 2.9 %collective-permute-done.3.refs_3_ = bf16[400,128]{1,0:T(8,128)(2,1)S(1)} collective-permute-done((bf16[400,128]{1,0:T(8,128)(2,1)S(1)}, bf16[400,128]{1,0:T(8,128)(2,1)S(1)}, u32[]{:S(2)}, u32[]{:S(2)}) %collective-permute-start.3) | collective-permute-done | bytes 102432 | tf_op jit(solution)/shard_map/ppermute | solution.py:54
  24.3 4.2 %collective-permute-done.6.refs_3_ = bf16[4,400,128]{2,1,0:T(8,128)(2,1)S(1)} collective-permute-done((bf16[4,400,128]{2,1,0:T(8,128)(2,1)S(1)}, bf16[4,400,128]{2,1,0:T(8,128)(2,1)S(1)}, u32[]{:S(2)}, u32[]{:S(2)}) %collective-permute-start.6) | collective-permute-done | bytes 409632 | tf_op jit(solution)/shard_map/ppermute | solution.py:54
  28.5 4.7 %collective-permute-done.5.refs_2_ = bf16[4,400,128]{2,1,0:T(8,128)(2,1)S(1)} collective-permute-done((bf16[4,400,128]{2,1,0:T(8,128)(2,1)S(1)}, bf16[4,400,128]{2,1,0:T(8,128)(2,1)S(1)}, u32[]{:S(2)}, u32[]{:S(2)}) %collective-permute-start.5) | collective-permute-done | bytes 409632 | tf_op jit(solution)/shard_map/ppermute | solution.py:54
  33.6 2.7 collective-permute-start.7
  39.5 2.8 %qkv_half.3 = (bf16[8,112,256]{2,1,0:T(8,128)(2,1)S(1)}, bf16[16,16,128]{2,1,0:T(8,128)(2,1)}) custom-call(s32[1]{0:T(128)} %bitcast.1.other_ref.h_ref, bf16[16,400,128]{2,1,0:T(8,128)(2,1)S(1)} %collective-permute-done.7.x_ref, bf16[16,400,128]{2,1,0:T(8,128)(2,1)S(1)} %order_chips.2.x_ref.g_ref, ...), custom_call_target="tpu_custom_call", output_to_operand_aliasing={{0}: (6, {})} | custom-call | flops 603979776 | bytes 4194304 | tf_op jit(solution)/shard_map/qkv_half/pallas_call | solution.py:176
  42.3 23.0 %all_to_all.30.p_ref = bf16[8,112,256]{2,1,0:T(8,128)(2,1)S(1)} all-to-all(bf16[8,112,256]{2,1,0:T(8,128)(2,1)S(1)} %get-tuple-element.20), channel_id=1, replica_groups=mesh['gx'=8,'gy'=32] {'gx'}, dimensions={0} | all-to-all | bytes 917504 | tf_op jit(solution)/shard_map/all_to_all | solution.py:94
  66.0 5.7 %all-to-all-start.1 = ((f32[8,32,96]{2,1,0:T(8,128)}), f32[8,32,96]{2,1,0:T(8,128)S(1)}, u32[]{:S(2)}, u32[]{:S(2)}) async-start(f32[8,32,96]{2,1,0:T(8,128)} %get-tuple-element.22), calls=%async_computation.1 | async-start | bytes 262144 | tf_op jit(solution)/shard_map/all_to_all | solution.py:615
  72.4 4.6 %all-to-all-done.1.kv_ref = f32[8,32,96]{2,1,0:T(8,128)S(1)} async-done(((f32[8,32,96]{2,1,0:T(8,128)}), f32[8,32,96]{2,1,0:T(8,128)S(1)}, u32[]{:S(2)}, u32[]{:S(2)}) %all-to-all-start.1) | async-done | bytes 98336 | tf_op jit(solution)/shard_map/all_to_all | solution.py:615
  77.6 15.9 %all_to_all.31 = bf16[8,96,256]{2,1,0:T(8,128)(2,1)S(1)} all-to-all(bf16[8,96,256]{2,1,0:T(8,128)(2,1)S(1)} %attend.1), channel_id=1, replica_groups=mesh['gx'=8,'gy'=32] {'gx'}, dimensions={0} | all-to-all | bytes 786432 | tf_op jit(solution)/shard_map/all_to_all | solution.py:94
  100.1 26.6 %all_to_all.32.p_ref = bf16[16,384,128]{2,1,0:T(8,128)(2,1)S(1)} all-to-all(bf16[16,384,128]{2,1,0:T(8,128)(2,1)S(1)} %add_convert_fusion.1), channel_id=1, replica_groups={{0,2,4,6,8,10,12,14,16,18,20,22,24,26,28,30},{1,3,5,7,9,11,13,15,17,19,..., dimensions={0} | all-to-all | bytes 3145728 | tf_op jit(solution)/shard_map/all_to_all | solution.py:42
  129.9 2.8 %collective-permute-done.11.refs_3_ = bf16[384,128]{1,0:T(8,128)(2,1)S(1)} collective-permute-done((bf16[384,128]{1,0:T(8,128)(2,1)S(1)}, bf16[384,128]{1,0:T(8,128)(2,1)S(1)}, u32[]{:S(2)}, u32[]{:S(2)}) %collective-permute-start.11) | collective-permute-done | bytes 98336 | tf_op jit(solution)/shard_map/ppermute | solution.py:54
  137.0 9.2 %collective-permute-done.14.refs_3_ = bf16[4,384,128]{2,1,0:T(8,128)(2,1)S(1)} collective-permute-done((bf16[4,384,128]{2,1,0:T(8,128)(2,1)S(1)}, bf16[4,384,128]{2,1,0:T(8,128)(2,1)S(1)}, u32[]{:S(2)}, u32[]{:S(2)}) %collective-permute-start.14) | collective-permute-done | bytes 393248 | tf_op jit(solution)/shard_map/ppermute | solution.py:54
  147.0 4.1 %collective-permute-start.15 = (bf16[16,384,128]{2,1,0:T(8,128)(2,1)S(1)}, bf16[16,384,128]{2,1,0:T(8,128)(2,1)S(1)}, u32[]{:S(2)}, u32[]{:S(2)}) collective-permute-start(bf16[16,384,128]{2,1,0:T(8,128)(2,1)S(1)} %order_chips.3.x_ref.own_ref), channel_id=1, source_target_pairs={{0,1},{1,0},{2,3},{3,2},{4,5},{5,4},{6,7},{7,6},{8,9},{9,8},{10,11... | collective-permute-start | bytes 4718600 | tf_op jit(solution)/shard_map/ppermute | solution.py:38
  151.1 3.7 %gate_up_main.2 = (bf16[768,1536]{1,0:T(8,128)(2,1)}, s32[1]{0:T(128)}) custom-call(s32[1]{0:T(128)} %bitcast.h_ref, bf16[16,384,128]{2,1,0:T(8,128)(2,1)S(1)} %order_chips.3.x_ref.own_ref, bf16[16,16,128]{2,1,0:T(8,128)(2,1)S(1)} %get-tuple-element.23.g_ref, bf16[832,2048]{1,0:T(8,128)(2,1)S(1)} %bitcast.17, bf16[832,2048]{1,0:T(8,128)(2,1)S(1)} %bitcast.20), custom_call_target="tpu_custom_call" | custom-call | flops 2415919104 | bytes 8388608 | tf_op jit(solution)/shard_map/gate_up_main/pallas_call | solution.py:452
  154.9 3.7 %gate_up_main.3 = (bf16[768,1536]{1,0:T(8,128)(2,1)}, s32[1]{0:T(128)}) custom-call(s32[1]{0:T(128)} %bitcast.1.other_ref.h_ref, bf16[16,384,128]{2,1,0:T(8,128)(2,1)S(1)} %collective-permute-done.15.x_ref.other_ref, bf16[16,16,128]{2,1,0:T(8,128)(2,1)S(1)} %get-tuple-element.23.g_ref, ...), custom_call_target="tpu_custom_call", output_to_operand_aliasing={{0}: (5, {})} | custom-call | flops 2415919104 | bytes 8388608 | tf_op jit(solution)/shard_map/gate_up_main/pallas_call | solution.py:452
  158.6 5.8 %gate_up_side.1 = bf16[768,256]{1,0:T(8,128)(2,1)} custom-call(s32[1]{0:T(128)} %bitcast.h_ref, bf16[16,384,128]{2,1,0:T(8,128)(2,1)} %copy-done.3, bf16[16,384,128]{2,1,0:T(8,128)(2,1)} %copy-done.4, bf16[16,16,128]{2,1,0:T(8,128)(2,1)} %copy-done.11, bf16[832,2048]{1,0:T(8,128)(2,1)} %bitcast.16, bf16[832,2048]{1,0:T(8,128)(2,1)} %bitcast.19, ...), custom_call_target="tpu_custom_call" | custom-call | flops 402653184 | bytes 6291456 | tf_op jit(solution)/shard_map/gate_up_side/pallas_call | solution.py:499
  164.4 23.3 %all_to_all.33.side_ref = bf16[8,96,256]{2,1,0:T(8,128)(2,1)} all-to-all(bf16[8,96,256]{2,1,0:T(8,128)(2,1)} %bitcast.34), channel_id=1, replica_groups=mesh['gx'=8,'gy'=32] {'gx'}, dimensions={0} | all-to-all | bytes 786432 | tf_op jit(solution)/shard_map/all_to_all | solution.py:94
  187.7 12.3 %reduce-scatter.2.cloned.1.call-done.main_ref = bf16[96,1536]{1,0:T(8,128)(2,1)} async-done(((bf16[768,1536]{1,0:T(8,128)(2,1)}), bf16[96,1536]{1,0:T(8,128)(2,1)}) %reduce-scatter.2.cloned.1.call-update) | async-done | bytes 294928 | tf_op jit(solution)/shard_map/reduce_scatter | solution.py:625
  209.4 6.1 %collective-permute-start.19 = (bf16[96,832]{1,0:T(8,128)(2,1)S(1)}, bf16[96,832]{1,0:T(8,128)(2,1)S(1)}, u32[]{:S(2)}, u32[]{:S(2)}) collective-permute-start(bf16[96,832]{1,0:T(8,128)(2,1)S(1)} %collective-permute-done.18.refs_3_), channel_id=1, source_target_pairs={{0,224},{32,0},{64,32},{96,64},{128,96},{160,128},{192,160},{224,1... | collective-permute-start | bytes 479240 | tf_op jit(solution)/shard_map/ppermute | solution.py:551
  215.5 5.0 %collective-permute-done.16.refs_1_ = bf16[96,832]{1,0:T(8,128)(2,1)S(1)} collective-permute-done((bf16[96,832]{1,0:T(8,128)(2,1)S(1)}, bf16[96,832]{1,0:T(8,128)(2,1)S(1)}, u32[]{:S(2)}, u32[]{:S(2)}) %collective-permute-start.16) | collective-permute-done | bytes 159776 | tf_op jit(solution)/shard_map/ppermute | solution.py:551
  220.5 5.4 %collective-permute-done.22.refs_6_ = bf16[96,832]{1,0:T(8,128)(2,1)S(1)} collective-permute-done((bf16[96,832]{1,0:T(8,128)(2,1)S(1)}, bf16[96,832]{1,0:T(8,128)(2,1)S(1)}, u32[]{:S(2)}, u32[]{:S(2)}) %collective-permute-start.22) | collective-permute-done | bytes 159776 | tf_op jit(solution)/shard_map/ppermute | solution.py:551
  228.8 3.9 %collective-permute-start.23 = (bf16[16,384,128]{2,1,0:T(8,128)(2,1)S(1)}, bf16[16,384,128]{2,1,0:T(8,128)(2,1)S(1)}, u32[]{:S(2)}, u32[]{:S(2)}) collective-permute-start(bf16[16,384,128]{2,1,0:T(8,128)(2,1)S(1)} %proj_half.7), channel_id=1, source_target_pairs={{0,1},{1,0},{2,3},{3,2},{4,5},{5,4},{6,7},{7,6},{8,9},{9,8},{10,11... | collective-permute-start | bytes 4718600 | tf_op jit(solution)/shard_map/ppermute | solution.py:38
  236.1 28.8 %all_to_all.34.p_ref = bf16[16,384,128]{2,1,0:T(8,128)(2,1)S(1)} all-to-all(bf16[16,384,128]{2,1,0:T(8,128)(2,1)S(1)} %add_convert_fusion), channel_id=1, replica_groups={{0,2,4,6,8,10,12,14,16,18,20,22,24,26,28,30},{1,3,5,7,9,11,13,15,17,19,..., dimensions={0} | all-to-all | bytes 3145728 | tf_op jit(solution)/shard_map/all_to_all | solution.py:42
  (94 shorter events, 50.9 us)
Async XLA Ops:
  13.3 6.2 %collective-permute-start.3 = (bf16[400,128]{1,0:T(8,128)(2,1)S(1)}, bf16[400,128]{1,0:T(8,128)(2,1)S(1)}, u32[]{:S(2)}, u32[]{:S(2)}) collective-permute-start(bf16[400,128]{1,0:T(8,128)(2,1)S(1)} %join_cores.1.refs_0_.base_ref), channel_id=1, source_target_pairs={{6,0},{25,1},{0,2},{27,3},{2,4},{29,5},{4,6},{31,7},{14,8},{1,9},{... | collective-permute-start | bytes 307208 | tf_op jit(solution)/shard_map/ppermute | solution.py:54
  13.3 6.1 %collective-permute-start.2 = (bf16[400,128]{1,0:T(8,128)(2,1)S(1)}, bf16[400,128]{1,0:T(8,128)(2,1)S(1)}, u32[]{:S(2)}, u32[]{:S(2)}) collective-permute-start(bf16[400,128]{1,0:T(8,128)(2,1)S(1)} %join_cores.1.refs_0_.base_ref), channel_id=1, source_target_pairs={{4,0},{17,1},{6,2},{19,3},{0,4},{21,5},{2,6},{23,7},{12,8},{25,9},... | collective-permute-start | bytes 307208 | tf_op jit(solution)/shard_map/ppermute | solution.py:54
  20.1 8.4 %collective-permute-start.6 = (bf16[4,400,128]{2,1,0:T(8,128)(2,1)S(1)}, bf16[4,400,128]{2,1,0:T(8,128)(2,1)S(1)}, u32[]{:S(2)}, u32[]{:S(2)}) collective-permute-start(bf16[4,400,128]{2,1,0:T(8,128)(2,1)S(1)} %stack_line.2.refs_0_), channel_id=1, source_target_pairs={{24,0},{7,1},{26,2},{1,3},{28,4},{3,5},{30,6},{5,7},{0,8},{15,9},{... | collective-permute-start | bytes 1228808 | tf_op jit(solution)/shard_map/ppermute | solution.py:54
  20.6 12.6 %collective-permute-start.5 = (bf16[4,400,128]{2,1,0:T(8,128)(2,1)S(1)}, bf16[4,400,128]{2,1,0:T(8,128)(2,1)S(1)}, u32[]{:S(2)}, u32[]{:S(2)}) collective-permute-start(bf16[4,400,128]{2,1,0:T(8,128)(2,1)S(1)} %stack_line.2.refs_0_), channel_id=1, source_target_pairs={{16,0},{5,1},{18,2},{7,3},{20,4},{1,5},{22,6},{3,7},{24,8},{13,9},... | collective-permute-start | bytes 1228808 | tf_op jit(solution)/shard_map/ppermute | solution.py:54
  23.1 10.4 %collective-permute-start.4 = (bf16[4,400,128]{2,1,0:T(8,128)(2,1)S(1)}, bf16[4,400,128]{2,1,0:T(8,128)(2,1)S(1)}, u32[]{:S(2)}, u32[]{:S(2)}) collective-permute-start(bf16[4,400,128]{2,1,0:T(8,128)(2,1)S(1)} %stack_line.2.refs_0_), channel_id=1, source_target_pairs={{8,0},{3,1},{10,2},{5,3},{12,4},{7,5},{14,6},{1,7},{16,8},{11,9},{... | collective-permute-start | bytes 1228808 | tf_op jit(solution)/shard_map/ppermute | solution.py:54
  33.6 5.8 %collective-permute-start.7 = (bf16[16,400,128]{2,1,0:T(8,128)(2,1)S(1)}, bf16[16,400,128]{2,1,0:T(8,128)(2,1)S(1)}, u32[]{:S(2)}, u32[]{:S(2)}) collective-permute-start(bf16[16,400,128]{2,1,0:T(8,128)(2,1)S(1)} %order_chips.2.x_ref.g_ref), channel_id=1, source_target_pairs={{0,1},{1,0},{2,3},{3,2},{4,5},{5,4},{6,7},{7,6},{8,9},{9,8},{10,11... | collective-permute-start | bytes 4915208 | tf_op jit(solution)/shard_map/ppermute | solution.py:38
  66.0 11.0 %all-to-all-start.1 = ((f32[8,32,96]{2,1,0:T(8,128)}), f32[8,32,96]{2,1,0:T(8,128)S(1)}, u32[]{:S(2)}, u32[]{:S(2)}) async-start(f32[8,32,96]{2,1,0:T(8,128)} %get-tuple-element.22), calls=%async_computation.1 | async-start | bytes 262144 | tf_op jit(solution)/shard_map/all_to_all | solution.py:615
  71.8 128.2 %reduce-scatter.2.cloned.1.call-start = ((), (), s32[]{:S(2)}) async-start(), calls=%async_computation.7 | async-start | bytes 2654208 | tf_op jit(solution)/shard_map/reduce_scatter | solution.py:625
  94.4 5.2 %collective-permute-start.8 = (bf16[16,384,128]{2,1,0:T(8,128)(2,1)S(1)}, bf16[16,384,128]{2,1,0:T(8,128)(2,1)S(1)}, u32[]{:S(2)}, u32[]{:S(2)}) collective-permute-start(bf16[16,384,128]{2,1,0:T(8,128)(2,1)S(1)} %proj_half.5), channel_id=1, source_target_pairs={{0,1},{1,0},{2,3},{3,2},{4,5},{5,4},{6,7},{7,6},{8,9},{9,8},{10,11... | collective-permute-start | bytes 4718600 | tf_op jit(solution)/shard_map/ppermute | solution.py:38
  126.8 5.8 %collective-permute-start.11 = (bf16[384,128]{1,0:T(8,128)(2,1)S(1)}, bf16[384,128]{1,0:T(8,128)(2,1)S(1)}, u32[]{:S(2)}, u32[]{:S(2)}) collective-permute-start(bf16[384,128]{1,0:T(8,128)(2,1)S(1)} %residual_sum.1.refs_0_.base_ref), channel_id=1, source_target_pairs={{6,0},{25,1},{0,2},{27,3},{2,4},{29,5},{4,6},{31,7},{14,8},{1,9},{... | collective-permute-start | bytes 294920 | tf_op jit(solution)/shard_map/ppermute | solution.py:54
  126.9 5.7 %collective-permute-start.10 = (bf16[384,128]{1,0:T(8,128)(2,1)S(1)}, bf16[384,128]{1,0:T(8,128)(2,1)S(1)}, u32[]{:S(2)}, u32[]{:S(2)}) collective-permute-start(bf16[384,128]{1,0:T(8,128)(2,1)S(1)} %residual_sum.1.refs_0_.base_ref), channel_id=1, source_target_pairs={{4,0},{17,1},{6,2},{19,3},{0,4},{21,5},{2,6},{23,7},{12,8},{25,9},... | collective-permute-start | bytes 294920 | tf_op jit(solution)/shard_map/ppermute | solution.py:54
  128.7 4.8 %collective-permute-start.9 = (bf16[384,128]{1,0:T(8,128)(2,1)S(1)}, bf16[384,128]{1,0:T(8,128)(2,1)S(1)}, u32[]{:S(2)}, u32[]{:S(2)}) collective-permute-start(bf16[384,128]{1,0:T(8,128)(2,1)S(1)} %residual_sum.1.refs_0_.base_ref), channel_id=1, source_target_pairs={{2,0},{9,1},{4,2},{11,3},{6,4},{13,5},{0,6},{15,7},{10,8},{17,9},{... | collective-permute-start | bytes 294920 | tf_op jit(solution)/shard_map/ppermute | solution.py:54
  133.6 12.6 %collective-permute-start.14 = (bf16[4,384,128]{2,1,0:T(8,128)(2,1)S(1)}, bf16[4,384,128]{2,1,0:T(8,128)(2,1)S(1)}, u32[]{:S(2)}, u32[]{:S(2)}) collective-permute-start(bf16[4,384,128]{2,1,0:T(8,128)(2,1)S(1)} %stack_line.3.refs_0_), channel_id=1, source_target_pairs={{24,0},{7,1},{26,2},{1,3},{28,4},{3,5},{30,6},{5,7},{0,8},{15,9},{... | collective-permute-start | bytes 1179656 | tf_op jit(solution)/shard_map/ppermute | solution.py:54
  133.9 12.3 %collective-permute-start.13 = (bf16[4,384,128]{2,1,0:T(8,128)(2,1)S(1)}, bf16[4,384,128]{2,1,0:T(8,128)(2,1)S(1)}, u32[]{:S(2)}, u32[]{:S(2)}) collective-permute-start(bf16[4,384,128]{2,1,0:T(8,128)(2,1)S(1)} %stack_line.3.refs_0_), channel_id=1, source_target_pairs={{16,0},{5,1},{18,2},{7,3},{20,4},{1,5},{22,6},{3,7},{24,8},{13,9},... | collective-permute-start | bytes 1179656 | tf_op jit(solution)/shard_map/ppermute | solution.py:54
  135.1 11.8 %collective-permute-start.12 = (bf16[4,384,128]{2,1,0:T(8,128)(2,1)S(1)}, bf16[4,384,128]{2,1,0:T(8,128)(2,1)S(1)}, u32[]{:S(2)}, u32[]{:S(2)}) collective-permute-start(bf16[4,384,128]{2,1,0:T(8,128)(2,1)S(1)} %stack_line.3.refs_0_), channel_id=1, source_target_pairs={{8,0},{3,1},{10,2},{5,3},{12,4},{7,5},{14,6},{1,7},{16,8},{11,9},{... | collective-permute-start | bytes 1179656 | tf_op jit(solution)/shard_map/ppermute | solution.py:54
  147.0 7.9 %collective-permute-start.15 = (bf16[16,384,128]{2,1,0:T(8,128)(2,1)S(1)}, bf16[16,384,128]{2,1,0:T(8,128)(2,1)S(1)}, u32[]{:S(2)}, u32[]{:S(2)}) collective-permute-start(bf16[16,384,128]{2,1,0:T(8,128)(2,1)S(1)} %order_chips.3.x_ref.own_ref), channel_id=1, source_target_pairs={{0,1},{1,0},{2,3},{3,2},{4,5},{5,4},{6,7},{7,6},{8,9},{9,8},{10,11... | collective-permute-start | bytes 4718600 | tf_op jit(solution)/shard_map/ppermute | solution.py:38
  202.2 6.0 %collective-permute-start.21 = (bf16[96,832]{1,0:T(8,128)(2,1)S(1)}, bf16[96,832]{1,0:T(8,128)(2,1)S(1)}, u32[]{:S(2)}, u32[]{:S(2)}) collective-permute-start(bf16[96,832]{1,0:T(8,128)(2,1)S(1)} %hidden_row.1.refs_0_), channel_id=1, source_target_pairs={{0,32},{32,64},{64,96},{96,128},{128,160},{160,192},{192,224},{224... | collective-permute-start | bytes 479240 | tf_op jit(solution)/shard_map/ppermute | solution.py:551
  202.9 6.5 %collective-permute-start.18 = (bf16[96,832]{1,0:T(8,128)(2,1)S(1)}, bf16[96,832]{1,0:T(8,128)(2,1)S(1)}, u32[]{:S(2)}, u32[]{:S(2)}) collective-permute-start(bf16[96,832]{1,0:T(8,128)(2,1)S(1)} %hidden_row.1.refs_0_), channel_id=1, source_target_pairs={{0,160},{32,192},{64,224},{96,0},{128,32},{160,64},{192,96},{224,1... | collective-permute-start | bytes 479240 | tf_op jit(solution)/shard_map/ppermute | solution.py:551
  205.5 15.0 %collective-permute-start.16 = (bf16[96,832]{1,0:T(8,128)(2,1)S(1)}, bf16[96,832]{1,0:T(8,128)(2,1)S(1)}, u32[]{:S(2)}, u32[]{:S(2)}) collective-permute-start(bf16[96,832]{1,0:T(8,128)(2,1)S(1)} %hidden_row.1.refs_0_), channel_id=1, source_target_pairs={{0,224},{32,0},{64,32},{96,64},{128,96},{160,128},{192,160},{224,1... | collective-permute-start | bytes 479240 | tf_op jit(solution)/shard_map/ppermute | solution.py:551
  206.6 13.9 %collective-permute-start.20 = (bf16[96,832]{1,0:T(8,128)(2,1)S(1)}, bf16[96,832]{1,0:T(8,128)(2,1)S(1)}, u32[]{:S(2)}, u32[]{:S(2)}) collective-permute-start(bf16[96,832]{1,0:T(8,128)(2,1)S(1)} %hidden_row.1.refs_0_), channel_id=1, source_target_pairs={{0,96},{32,128},{64,160},{96,192},{128,224},{160,0},{192,32},{224,... | collective-permute-start | bytes 479240 | tf_op jit(solution)/shard_map/ppermute | solution.py:551
  208.3 17.6 %collective-permute-start.22 = (bf16[96,832]{1,0:T(8,128)(2,1)S(1)}, bf16[96,832]{1,0:T(8,128)(2,1)S(1)}, u32[]{:S(2)}, u32[]{:S(2)}) collective-permute-start(bf16[96,832]{1,0:T(8,128)(2,1)S(1)} %collective-permute-done.21.refs_7_), channel_id=1, source_target_pairs={{0,32},{32,64},{64,96},{96,128},{128,160},{160,192},{192,224},{224... | collective-permute-start | bytes 479240 | tf_op jit(solution)/shard_map/ppermute | solution.py:551
  209.4 16.4 %collective-permute-start.19 = (bf16[96,832]{1,0:T(8,128)(2,1)S(1)}, bf16[96,832]{1,0:T(8,128)(2,1)S(1)}, u32[]{:S(2)}, u32[]{:S(2)}) collective-permute-start(bf16[96,832]{1,0:T(8,128)(2,1)S(1)} %collective-permute-done.18.refs_3_), channel_id=1, source_target_pairs={{0,224},{32,0},{64,32},{96,64},{128,96},{160,128},{192,160},{224,1... | collective-permute-start | bytes 479240 | tf_op jit(solution)/shard_map/ppermute | solution.py:551
  220.5 6.0 %collective-permute-start.17 = (bf16[96,832]{1,0:T(8,128)(2,1)S(1)}, bf16[96,832]{1,0:T(8,128)(2,1)S(1)}, u32[]{:S(2)}, u32[]{:S(2)}) collective-permute-start(bf16[96,832]{1,0:T(8,128)(2,1)S(1)} %collective-permute-done.16.refs_1_), channel_id=1, source_target_pairs={{0,224},{32,0},{64,32},{96,64},{128,96},{160,128},{192,160},{224,1... | collective-permute-start | bytes 479240 | tf_op jit(solution)/shard_map/ppermute | solution.py:551
  228.8 6.9 %collective-permute-start.23 = (bf16[16,384,128]{2,1,0:T(8,128)(2,1)S(1)}, bf16[16,384,128]{2,1,0:T(8,128)(2,1)S(1)}, u32[]{:S(2)}, u32[]{:S(2)}) collective-permute-start(bf16[16,384,128]{2,1,0:T(8,128)(2,1)S(1)} %proj_half.7), channel_id=1, source_target_pairs={{0,1},{1,0},{2,3},{3,2},{4,5},{5,4},{6,7},{7,6},{8,9},{9,8},{10,11... | collective-permute-start | bytes 4718600 | tf_op jit(solution)/shard_map/ppermute | solution.py:38
  (20 other events, 421.1 us)
Sparse Core Ops, SparseCore 0:
  158.8 41.1 reduce-scatter.1

commit v9 on v8

--- a/solution.py
+++ b/solution.py
@@ -59,9 +59,10 @@
         refs[-1][j] = ref[...]
 
 
-def order_chips_kernel(g_ref, *refs):
+def order_chips_kernel(of_other, g_ref, *refs):
     out_ref = refs[-1]
     core = lax.rem(g_ref[0], 2)
+    core = 1 - core if of_other else core
     across, y = lax.rem(lax.div(g_ref[0], 2), 4), lax.div(g_ref[0], 8)
     for a in range(4):
         for b in range(4):
@@ -80,14 +81,19 @@
         compiler_params=params(),
         name="stack_line",
     )(x, *[over_ring(x, k, 0) for k in (1, 2, 3)])
-    return pl.pallas_call(
-        order_chips_kernel,
-        in_specs=[pl.BlockSpec(memory_space=pltpu.SMEM)] + [vmem] * 4,
-        out_specs=vmem,
-        out_shape=jax.ShapeDtypeStruct((CHIPS,) + x.shape, x.dtype),
-        compiler_params=params(),
-        name="order_chips",
-    )(g, line, *[over_ring(line, k, 1) for k in (1, 2, 3)])
+    pieces = [line] + [over_ring(line, k, 1) for k in (1, 2, 3)]
+
+    def ordered(of_other, pieces):
+        return pl.pallas_call(
+            functools.partial(order_chips_kernel, of_other),
+            in_specs=[pl.BlockSpec(memory_space=pltpu.SMEM)] + [vmem] * 4,
+            out_specs=vmem,
+            out_shape=jax.ShapeDtypeStruct((CHIPS,) + x.shape, x.dtype),
+            compiler_params=params(),
+            name="order_chips",
+        )(g, *pieces)
+
+    return ordered(False, pieces), ordered(True, [swap(piece) for piece in pieces])
 
 
 def over_rows(x):
@@ -607,8 +613,7 @@
 
     keep, give = cut_tokens(mine, theirs, at, place, tokens.T, norm_attn, norm_ffn)
     base = join_cores(mine, keep, swap(give))
-    first = from_chips(place, base)
-    other = swap(first)
+    first, other = from_chips(place, base)
     held, gains = qkv_half(mine, first, first, w_query, w_key.T, w_value.T)
     parts, _ = qkv_half(theirs, other, first, w_query, w_key.T, w_value.T, held)
     q, kv = qkv_sum(over_rows(parts))
@@ -616,8 +621,7 @@
     attended = over_rows(attend(lengths, q, kv, segments)).reshape(TOK, 256)
     residual = residual_sum(base, project_out(mine, theirs, attended, w_out))
 
-    own = from_chips(place, residual)
-    other = swap(own)
+    own, other = from_chips(place, residual)
     weights = (w_gate.T, w_up.T)
     held, _ = gate_up_main(mine, own, gains, *weights)
     main, made = gate_up_main(theirs, other, gains, *weights, held)

time: 276 us -> 275 us (level)
  waiting for transfers between devices: 60.4 us -> 51.1 us
  starting transfers between devices: 50.6 us -> 58.8 us
    ppermute x12, waiting for transfers between devices: 26.2 us -> 17.1 us  [over_ring(): return lax.ppermute(x, 'gy', pairs)]
    ppermute x6 -> x12, starting transfers between devices: 18 us -> 26 us  [swap(): return lax.ppermute(x, 'gy', [(i, i ^ 1) for i in range(32)])]
    ppermute x6 -> x12, waiting for transfers between devices: 6.03 us -> 4.92 us  [swap(): return lax.ppermute(x, 'gy', [(i, i ^ 1) for i in range(32)])]
  transfers between devices with their start and end apart: 27 -> 33, of which waited for: 20 -> 17; matrix products, arithmetic and copies ran while one was open for 0% -> 0% of each run, Pallas kernels for 5% -> 5%
where the time goes in v9:
time: 275 us
  blocking collectives  117 us (43%)
  starting transfers between devices  58.8 us (21%)
  waiting for transfers between devices  51.1 us (19%)
  Pallas kernels  28 us (10%)
  between operations  14.4 us (5%)
  local copies, waits for them, and re-layouts  4.21 us (2%)
    all_to_all x3, blocking collectives, over_rows(): return lax.all_to_all(x, 'gx', 0, 0, tiled=True)  62 us
    all_to_all x2, blocking collectives, over_chips(): lax.all_to_all(x, 'gy', 0, 0, axis_index_groups=CHIP_GROUPS, tiled=True)  55.2 us
    ppermute x12, starting transfers between devices, swap(): return lax.ppermute(x, 'gy', [(i, i ^ 1) for i in range(32)])  26 us
    ppermute x12, waiting for transfers between devices, over_ring(): return lax.ppermute(x, 'gy', pairs)  17.1 us
    ppermute x12, starting transfers between devices, over_ring(): return lax.ppermute(x, 'gy', pairs)  13.9 us
    ppermute x7, starting transfers between devices, from_ahead(): return lax.ppermute(x, 'gx', [(i, (i - k) % ROWS) for i in range(ROWS)])  13 us
    reduce_scatter x1, waiting for transfers between devices, per_device(): main = lax.psum_scatter(main, 'gx', scatter_dimension=0, tiled=True)  12.3 us
    ppermute x7, waiting for transfers between devices, from_ahead(): return lax.ppermute(x, 'gx', [(i, (i - k) % ROWS) for i in range(ROWS)])  12.1 us
  transfers between devices with their start and end apart: 33, of which 17 were waited for; matrix products, arithmetic and copies ran while one was open for 0% of the time, Pallas kernels for 5%

profile of v9, /device:TPU:1, one launch (start us, length us, event | category | flops | bytes accessed | tf_op | source)
XLA Modules:
  0.0 274.6 jit_solution(8122045741925358308)
XLA Ops:
  8.8 3.3 %collective-permute-start = (bf16[400,64]{1,0:T(8,128)(2,1)S(1)}, bf16[400,64]{1,0:T(8,128)(2,1)S(1)}, u32[]{:S(2)}, u32[]{:S(2)}) collective-permute-start(bf16[400,64]{1,0:T(8,128)(2,1)S(1)} %get-tuple-element.18), channel_id=1, source_target_pairs={{0,1},{1,0},{2,3},{3,2},{4,5},{5,4},{6,7},{7,6},{8,9},{9,8},{10,11... | collective-permute-start | bytes 153608 | tf_op jit(solution)/shard_map/ppermute | solution.py:38
  16.6 2.9 %collective-permute-done.3.refs_3_ = bf16[400,128]{1,0:T(8,128)(2,1)S(1)} collective-permute-done((bf16[400,128]{1,0:T(8,128)(2,1)S(1)}, bf16[400,128]{1,0:T(8,128)(2,1)S(1)}, u32[]{:S(2)}, u32[]{:S(2)}) %collective-permute-start.3) | collective-permute-done | bytes 102432 | tf_op jit(solution)/shard_map/ppermute | solution.py:54
  33.1 2.6 collective-permute-start.8
  38.5 2.8 %qkv_half.3 = (bf16[8,112,256]{2,1,0:T(8,128)(2,1)S(1)}, bf16[16,16,128]{2,1,0:T(8,128)(2,1)}) custom-call(s32[1]{0:T(128)} %bitcast.1.other_ref.h_ref, bf16[16,400,128]{2,1,0:T(8,128)(2,1)S(1)} %order_chips.4.x_ref, bf16[16,400,128]{2,1,0:T(8,128)(2,1)S(1)} %order_chips.5.x_ref.g_ref, ...), custom_call_target="tpu_custom_call", output_to_operand_aliasing={{0}: (6, {})} | custom-call | flops 603979776 | bytes 4194304 | tf_op jit(solution)/shard_map/qkv_half/pallas_call | solution.py:182
  41.3 22.8 %all_to_all.30.p_ref = bf16[8,112,256]{2,1,0:T(8,128)(2,1)S(1)} all-to-all(bf16[8,112,256]{2,1,0:T(8,128)(2,1)S(1)} %get-tuple-element.20), channel_id=1, replica_groups=mesh['gx'=8,'gy'=32] {'gx'}, dimensions={0} | all-to-all | bytes 917504 | tf_op jit(solution)/shard_map/all_to_all | solution.py:100
  64.9 5.9 %all-to-all-start.1 = ((f32[8,32,96]{2,1,0:T(8,128)}), f32[8,32,96]{2,1,0:T(8,128)S(1)}, u32[]{:S(2)}, u32[]{:S(2)}) async-start(f32[8,32,96]{2,1,0:T(8,128)} %get-tuple-element.22), calls=%async_computation.1 | async-start | bytes 262144 | tf_op jit(solution)/shard_map/all_to_all | solution.py:620
  71.4 4.6 %all-to-all-done.1.kv_ref = f32[8,32,96]{2,1,0:T(8,128)S(1)} async-done(((f32[8,32,96]{2,1,0:T(8,128)}), f32[8,32,96]{2,1,0:T(8,128)S(1)}, u32[]{:S(2)}, u32[]{:S(2)}) %all-to-all-start.1) | async-done | bytes 98336 | tf_op jit(solution)/shard_map/all_to_all | solution.py:620
  76.7 15.9 %all_to_all.31 = bf16[8,96,256]{2,1,0:T(8,128)(2,1)S(1)} all-to-all(bf16[8,96,256]{2,1,0:T(8,128)(2,1)S(1)} %attend.1), channel_id=1, replica_groups=mesh['gx'=8,'gy'=32] {'gx'}, dimensions={0} | all-to-all | bytes 786432 | tf_op jit(solution)/shard_map/all_to_all | solution.py:100
  99.1 26.6 %all_to_all.32.p_ref = bf16[16,384,128]{2,1,0:T(8,128)(2,1)S(1)} all-to-all(bf16[16,384,128]{2,1,0:T(8,128)(2,1)S(1)} %add_convert_fusion.1), channel_id=1, replica_groups={{0,2,4,6,8,10,12,14,16,18,20,22,24,26,28,30},{1,3,5,7,9,11,13,15,17,19,..., dimensions={0} | all-to-all | bytes 3145728 | tf_op jit(solution)/shard_map/all_to_all | solution.py:42
  129.1 2.8 %collective-permute-done.14.refs_3_ = bf16[384,128]{1,0:T(8,128)(2,1)S(1)} collective-permute-done((bf16[384,128]{1,0:T(8,128)(2,1)S(1)}, bf16[384,128]{1,0:T(8,128)(2,1)S(1)}, u32[]{:S(2)}, u32[]{:S(2)}) %collective-permute-start.14) | collective-permute-done | bytes 98336 | tf_op jit(solution)/shard_map/ppermute | solution.py:54
  136.1 3.2 %collective-permute-start.15 = (bf16[4,384,128]{2,1,0:T(8,128)(2,1)S(1)}, bf16[4,384,128]{2,1,0:T(8,128)(2,1)S(1)}, u32[]{:S(2)}, u32[]{:S(2)}) collective-permute-start(bf16[4,384,128]{2,1,0:T(8,128)(2,1)S(1)} %stack_line.3.refs_0_), channel_id=1, source_target_pairs={{0,1},{1,0},{2,3},{3,2},{4,5},{5,4},{6,7},{7,6},{8,9},{9,8},{10,11... | collective-permute-start | bytes 1179656 | tf_op jit(solution)/shard_map/ppermute | solution.py:38
  139.3 6.0 %collective-permute-done.20.refs_3_ = bf16[4,384,128]{2,1,0:T(8,128)(2,1)S(1)} collective-permute-done((bf16[4,384,128]{2,1,0:T(8,128)(2,1)S(1)}, bf16[4,384,128]{2,1,0:T(8,128)(2,1)S(1)}, u32[]{:S(2)}, u32[]{:S(2)}) %collective-permute-start.20) | collective-permute-done | bytes 393248 | tf_op jit(solution)/shard_map/ppermute | solution.py:54
  145.3 3.8 %collective-permute-start.21 = (bf16[4,384,128]{2,1,0:T(8,128)(2,1)S(1)}, bf16[4,384,128]{2,1,0:T(8,128)(2,1)S(1)}, u32[]{:S(2)}, u32[]{:S(2)}) collective-permute-start(bf16[4,384,128]{2,1,0:T(8,128)(2,1)S(1)} %collective-permute-done.20.refs_3_), channel_id=1, source_target_pairs={{0,1},{1,0},{2,3},{3,2},{4,5},{5,4},{6,7},{7,6},{8,9},{9,8},{10,11... | collective-permute-start | bytes 1179656 | tf_op jit(solution)/shard_map/ppermute | solution.py:38
  150.1 3.7 %gate_up_main.2 = (bf16[768,1536]{1,0:T(8,128)(2,1)}, s32[1]{0:T(128)}) custom-call(s32[1]{0:T(128)} %bitcast.h_ref, bf16[16,384,128]{2,1,0:T(8,128)(2,1)S(1)} %order_chips.7.x_ref.own_ref, bf16[16,16,128]{2,1,0:T(8,128)(2,1)S(1)} %get-tuple-element.23.g_ref, bf16[832,2048]{1,0:T(8,128)(2,1)S(1)} %bitcast.17, bf16[832,2048]{1,0:T(8,128)(2,1)S(1)} %bitcast.20), custom_call_target="tpu_custom_call" | custom-call | flops 2415919104 | bytes 8388608 | tf_op jit(solution)/shard_map/gate_up_main/pallas_call | solution.py:458
  154.0 3.7 %gate_up_main.3 = (bf16[768,1536]{1,0:T(8,128)(2,1)}, s32[1]{0:T(128)}) custom-call(s32[1]{0:T(128)} %bitcast.1.other_ref.h_ref, bf16[16,384,128]{2,1,0:T(8,128)(2,1)S(1)} %order_chips.6.x_ref.other_ref, bf16[16,16,128]{2,1,0:T(8,128)(2,1)S(1)} %get-tuple-element.23.g_ref, bf16[832,2048]{1,0:T(8,128)(2,1)S(1)} %bitcast.18, ...), custom_call_target="tpu_custom_call", output_to_operand_aliasing={{0}: (5, {})} | custom-call | flops 2415919104 | bytes 8388608 | tf_op jit(solution)/shard_map/gate_up_main/pallas_call | solution.py:458
  157.8 5.8 %gate_up_side.1 = bf16[768,256]{1,0:T(8,128)(2,1)} custom-call(s32[1]{0:T(128)} %bitcast.h_ref, bf16[16,384,128]{2,1,0:T(8,128)(2,1)} %copy-done.4, bf16[16,384,128]{2,1,0:T(8,128)(2,1)} %copy-done, bf16[16,16,128]{2,1,0:T(8,128)(2,1)} %copy-done.11, bf16[832,2048]{1,0:T(8,128)(2,1)} %bitcast.16, bf16[832,2048]{1,0:T(8,128)(2,1)} %bitcast.19, ...), custom_call_target="tpu_custom_call" | custom-call | flops 402653184 | bytes 6291456 | tf_op jit(solution)/shard_map/gate_up_side/pallas_call | solution.py:505
  163.5 23.3 %all_to_all.33.side_ref = bf16[8,96,256]{2,1,0:T(8,128)(2,1)} all-to-all(bf16[8,96,256]{2,1,0:T(8,128)(2,1)} %bitcast.34), channel_id=1, replica_groups=mesh['gx'=8,'gy'=32] {'gx'}, dimensions={0} | all-to-all | bytes 786432 | tf_op jit(solution)/shard_map/all_to_all | solution.py:100
  186.8 12.3 %reduce-scatter.2.cloned.1.call-done.main_ref = bf16[96,1536]{1,0:T(8,128)(2,1)} async-done(((bf16[768,1536]{1,0:T(8,128)(2,1)}), bf16[96,1536]{1,0:T(8,128)(2,1)}) %reduce-scatter.2.cloned.1.call-update) | async-done | bytes 294928 | tf_op jit(solution)/shard_map/reduce_scatter | solution.py:629
  202.1 2.6 collective-permute-start.24
  208.6 6.1 %collective-permute-start.25 = (bf16[96,832]{1,0:T(8,128)(2,1)S(1)}, bf16[96,832]{1,0:T(8,128)(2,1)S(1)}, u32[]{:S(2)}, u32[]{:S(2)}) collective-permute-start(bf16[96,832]{1,0:T(8,128)(2,1)S(1)} %collective-permute-done.24.refs_3_), channel_id=1, source_target_pairs={{0,224},{32,0},{64,32},{96,64},{128,96},{160,128},{192,160},{224,1... | collective-permute-start | bytes 479240 | tf_op jit(solution)/shard_map/ppermute | solution.py:557
  214.7 4.4 %collective-permute-done.22.refs_1_ = bf16[96,832]{1,0:T(8,128)(2,1)S(1)} collective-permute-done((bf16[96,832]{1,0:T(8,128)(2,1)S(1)}, bf16[96,832]{1,0:T(8,128)(2,1)S(1)}, u32[]{:S(2)}, u32[]{:S(2)}) %collective-permute-start.22) | collective-permute-done | bytes 159776 | tf_op jit(solution)/shard_map/ppermute | solution.py:557
  219.2 5.8 %collective-permute-done.28.refs_6_ = bf16[96,832]{1,0:T(8,128)(2,1)S(1)} collective-permute-done((bf16[96,832]{1,0:T(8,128)(2,1)S(1)}, bf16[96,832]{1,0:T(8,128)(2,1)S(1)}, u32[]{:S(2)}, u32[]{:S(2)}) %collective-permute-start.28) | collective-permute-done | bytes 159776 | tf_op jit(solution)/shard_map/ppermute | solution.py:557
  228.9 2.9 %collective-permute-start.29 = (bf16[16,384,128]{2,1,0:T(8,128)(2,1)S(1)}, bf16[16,384,128]{2,1,0:T(8,128)(2,1)S(1)}, u32[]{:S(2)}, u32[]{:S(2)}) collective-permute-start(bf16[16,384,128]{2,1,0:T(8,128)(2,1)S(1)} %proj_half.7), channel_id=1, source_target_pairs={{0,1},{1,0},{2,3},{3,2},{4,5},{5,4},{6,7},{7,6},{8,9},{9,8},{10,11... | collective-permute-start | bytes 4718600 | tf_op jit(solution)/shard_map/ppermute | solution.py:38
  235.2 28.7 %all_to_all.34.p_ref = bf16[16,384,128]{2,1,0:T(8,128)(2,1)S(1)} all-to-all(bf16[16,384,128]{2,1,0:T(8,128)(2,1)S(1)} %add_convert_fusion), channel_id=1, replica_groups={{0,2,4,6,8,10,12,14,16,18,20,22,24,26,28,30},{1,3,5,7,9,11,13,15,17,19,..., dimensions={0} | all-to-all | bytes 3145728 | tf_op jit(solution)/shard_map/all_to_all | solution.py:42
  (108 shorter events, 57.6 us)
Async XLA Ops:
  13.3 6.2 %collective-permute-start.3 = (bf16[400,128]{1,0:T(8,128)(2,1)S(1)}, bf16[400,128]{1,0:T(8,128)(2,1)S(1)}, u32[]{:S(2)}, u32[]{:S(2)}) collective-permute-start(bf16[400,128]{1,0:T(8,128)(2,1)S(1)} %join_cores.1.refs_0_.base_ref), channel_id=1, source_target_pairs={{6,0},{25,1},{0,2},{27,3},{2,4},{29,5},{4,6},{31,7},{14,8},{1,9},{... | collective-permute-start | bytes 307208 | tf_op jit(solution)/shard_map/ppermute | solution.py:54
  13.3 6.1 %collective-permute-start.2 = (bf16[400,128]{1,0:T(8,128)(2,1)S(1)}, bf16[400,128]{1,0:T(8,128)(2,1)S(1)}, u32[]{:S(2)}, u32[]{:S(2)}) collective-permute-start(bf16[400,128]{1,0:T(8,128)(2,1)S(1)} %join_cores.1.refs_0_.base_ref), channel_id=1, source_target_pairs={{4,0},{17,1},{6,2},{19,3},{0,4},{21,5},{2,6},{23,7},{12,8},{25,9},... | collective-permute-start | bytes 307208 | tf_op jit(solution)/shard_map/ppermute | solution.py:54
  20.1 8.4 %collective-permute-start.9 = (bf16[4,400,128]{2,1,0:T(8,128)(2,1)S(1)}, bf16[4,400,128]{2,1,0:T(8,128)(2,1)S(1)}, u32[]{:S(2)}, u32[]{:S(2)}) collective-permute-start(bf16[4,400,128]{2,1,0:T(8,128)(2,1)S(1)} %stack_line.2.refs_0_), channel_id=1, source_target_pairs={{24,0},{7,1},{26,2},{1,3},{28,4},{3,5},{30,6},{5,7},{0,8},{15,9},{... | collective-permute-start | bytes 1228808 | tf_op jit(solution)/shard_map/ppermute | solution.py:54
  20.6 12.6 %collective-permute-start.7 = (bf16[4,400,128]{2,1,0:T(8,128)(2,1)S(1)}, bf16[4,400,128]{2,1,0:T(8,128)(2,1)S(1)}, u32[]{:S(2)}, u32[]{:S(2)}) collective-permute-start(bf16[4,400,128]{2,1,0:T(8,128)(2,1)S(1)} %stack_line.2.refs_0_), channel_id=1, source_target_pairs={{16,0},{5,1},{18,2},{7,3},{20,4},{1,5},{22,6},{3,7},{24,8},{13,9},... | collective-permute-start | bytes 1228808 | tf_op jit(solution)/shard_map/ppermute | solution.py:54
  23.1 12.7 %collective-permute-start.5 = (bf16[4,400,128]{2,1,0:T(8,128)(2,1)S(1)}, bf16[4,400,128]{2,1,0:T(8,128)(2,1)S(1)}, u32[]{:S(2)}, u32[]{:S(2)}) collective-permute-start(bf16[4,400,128]{2,1,0:T(8,128)(2,1)S(1)} %stack_line.2.refs_0_), channel_id=1, source_target_pairs={{8,0},{3,1},{10,2},{5,3},{12,4},{7,5},{14,6},{1,7},{16,8},{11,9},{... | collective-permute-start | bytes 1228808 | tf_op jit(solution)/shard_map/ppermute | solution.py:54
  24.3 14.0 %collective-permute-start.4 = (bf16[4,400,128]{2,1,0:T(8,128)(2,1)S(1)}, bf16[4,400,128]{2,1,0:T(8,128)(2,1)S(1)}, u32[]{:S(2)}, u32[]{:S(2)}) collective-permute-start(bf16[4,400,128]{2,1,0:T(8,128)(2,1)S(1)} %stack_line.2.refs_0_), channel_id=1, source_target_pairs={{0,1},{1,0},{2,3},{3,2},{4,5},{5,4},{6,7},{7,6},{8,9},{9,8},{10,11... | collective-permute-start | bytes 1228808 | tf_op jit(solution)/shard_map/ppermute | solution.py:38
  28.5 9.8 %collective-permute-start.10 = (bf16[4,400,128]{2,1,0:T(8,128)(2,1)S(1)}, bf16[4,400,128]{2,1,0:T(8,128)(2,1)S(1)}, u32[]{:S(2)}, u32[]{:S(2)}) collective-permute-start(bf16[4,400,128]{2,1,0:T(8,128)(2,1)S(1)} %collective-permute-done.9.refs_3_), channel_id=1, source_target_pairs={{0,1},{1,0},{2,3},{3,2},{4,5},{5,4},{6,7},{7,6},{8,9},{9,8},{10,11... | collective-permute-start | bytes 1228808 | tf_op jit(solution)/shard_map/ppermute | solution.py:38
  64.9 11.2 %all-to-all-start.1 = ((f32[8,32,96]{2,1,0:T(8,128)}), f32[8,32,96]{2,1,0:T(8,128)S(1)}, u32[]{:S(2)}, u32[]{:S(2)}) async-start(f32[8,32,96]{2,1,0:T(8,128)} %get-tuple-element.22), calls=%async_computation.1 | async-start | bytes 262144 | tf_op jit(solution)/shard_map/all_to_all | solution.py:620
  70.8 128.4 %reduce-scatter.2.cloned.1.call-start = ((), (), s32[]{:S(2)}) async-start(), calls=%async_computation.7 | async-start | bytes 2654208 | tf_op jit(solution)/shard_map/reduce_scatter | solution.py:629
  125.9 6.0 %collective-permute-start.14 = (bf16[384,128]{1,0:T(8,128)(2,1)S(1)}, bf16[384,128]{1,0:T(8,128)(2,1)S(1)}, u32[]{:S(2)}, u32[]{:S(2)}) collective-permute-start(bf16[384,128]{1,0:T(8,128)(2,1)S(1)} %residual_sum.1.refs_0_.base_ref), channel_id=1, source_target_pairs={{6,0},{25,1},{0,2},{27,3},{2,4},{29,5},{4,6},{31,7},{14,8},{1,9},{... | collective-permute-start | bytes 294920 | tf_op jit(solution)/shard_map/ppermute | solution.py:54
  126.2 5.7 %collective-permute-start.13 = (bf16[384,128]{1,0:T(8,128)(2,1)S(1)}, bf16[384,128]{1,0:T(8,128)(2,1)S(1)}, u32[]{:S(2)}, u32[]{:S(2)}) collective-permute-start(bf16[384,128]{1,0:T(8,128)(2,1)S(1)} %residual_sum.1.refs_0_.base_ref), channel_id=1, source_target_pairs={{4,0},{17,1},{6,2},{19,3},{0,4},{21,5},{2,6},{23,7},{12,8},{25,9},... | collective-permute-start | bytes 294920 | tf_op jit(solution)/shard_map/ppermute | solution.py:54
  132.8 12.4 %collective-permute-start.20 = (bf16[4,384,128]{2,1,0:T(8,128)(2,1)S(1)}, bf16[4,384,128]{2,1,0:T(8,128)(2,1)S(1)}, u32[]{:S(2)}, u32[]{:S(2)}) collective-permute-start(bf16[4,384,128]{2,1,0:T(8,128)(2,1)S(1)} %stack_line.3.refs_0_), channel_id=1, source_target_pairs={{24,0},{7,1},{26,2},{1,3},{28,4},{3,5},{30,6},{5,7},{0,8},{15,9},{... | collective-permute-start | bytes 1179656 | tf_op jit(solution)/shard_map/ppermute | solution.py:54
  132.9 16.1 %collective-permute-start.18 = (bf16[4,384,128]{2,1,0:T(8,128)(2,1)S(1)}, bf16[4,384,128]{2,1,0:T(8,128)(2,1)S(1)}, u32[]{:S(2)}, u32[]{:S(2)}) collective-permute-start(bf16[4,384,128]{2,1,0:T(8,128)(2,1)S(1)} %stack_line.3.refs_0_), channel_id=1, source_target_pairs={{16,0},{5,1},{18,2},{7,3},{20,4},{1,5},{22,6},{3,7},{24,8},{13,9},... | collective-permute-start | bytes 1179656 | tf_op jit(solution)/shard_map/ppermute | solution.py:54
  134.1 14.9 %collective-permute-start.16 = (bf16[4,384,128]{2,1,0:T(8,128)(2,1)S(1)}, bf16[4,384,128]{2,1,0:T(8,128)(2,1)S(1)}, u32[]{:S(2)}, u32[]{:S(2)}) collective-permute-start(bf16[4,384,128]{2,1,0:T(8,128)(2,1)S(1)} %stack_line.3.refs_0_), channel_id=1, source_target_pairs={{8,0},{3,1},{10,2},{5,3},{12,4},{7,5},{14,6},{1,7},{16,8},{11,9},{... | collective-permute-start | bytes 1179656 | tf_op jit(solution)/shard_map/ppermute | solution.py:54
  136.1 17.7 %collective-permute-start.15 = (bf16[4,384,128]{2,1,0:T(8,128)(2,1)S(1)}, bf16[4,384,128]{2,1,0:T(8,128)(2,1)S(1)}, u32[]{:S(2)}, u32[]{:S(2)}) collective-permute-start(bf16[4,384,128]{2,1,0:T(8,128)(2,1)S(1)} %stack_line.3.refs_0_), channel_id=1, source_target_pairs={{0,1},{1,0},{2,3},{3,2},{4,5},{5,4},{6,7},{7,6},{8,9},{9,8},{10,11... | collective-permute-start | bytes 1179656 | tf_op jit(solution)/shard_map/ppermute | solution.py:38
  145.3 8.6 %collective-permute-start.21 = (bf16[4,384,128]{2,1,0:T(8,128)(2,1)S(1)}, bf16[4,384,128]{2,1,0:T(8,128)(2,1)S(1)}, u32[]{:S(2)}, u32[]{:S(2)}) collective-permute-start(bf16[4,384,128]{2,1,0:T(8,128)(2,1)S(1)} %collective-permute-done.20.refs_3_), channel_id=1, source_target_pairs={{0,1},{1,0},{2,3},{3,2},{4,5},{5,4},{6,7},{7,6},{8,9},{9,8},{10,11... | collective-permute-start | bytes 1179656 | tf_op jit(solution)/shard_map/ppermute | solution.py:38
  201.4 6.0 %collective-permute-start.27 = (bf16[96,832]{1,0:T(8,128)(2,1)S(1)}, bf16[96,832]{1,0:T(8,128)(2,1)S(1)}, u32[]{:S(2)}, u32[]{:S(2)}) collective-permute-start(bf16[96,832]{1,0:T(8,128)(2,1)S(1)} %hidden_row.1.refs_0_), channel_id=1, source_target_pairs={{0,32},{32,64},{64,96},{96,128},{128,160},{160,192},{192,224},{224... | collective-permute-start | bytes 479240 | tf_op jit(solution)/shard_map/ppermute | solution.py:557
  202.1 6.5 %collective-permute-start.24 = (bf16[96,832]{1,0:T(8,128)(2,1)S(1)}, bf16[96,832]{1,0:T(8,128)(2,1)S(1)}, u32[]{:S(2)}, u32[]{:S(2)}) collective-permute-start(bf16[96,832]{1,0:T(8,128)(2,1)S(1)} %hidden_row.1.refs_0_), channel_id=1, source_target_pairs={{0,160},{32,192},{64,224},{96,0},{128,32},{160,64},{192,96},{224,1... | collective-permute-start | bytes 479240 | tf_op jit(solution)/shard_map/ppermute | solution.py:557
  204.7 14.4 %collective-permute-start.22 = (bf16[96,832]{1,0:T(8,128)(2,1)S(1)}, bf16[96,832]{1,0:T(8,128)(2,1)S(1)}, u32[]{:S(2)}, u32[]{:S(2)}) collective-permute-start(bf16[96,832]{1,0:T(8,128)(2,1)S(1)} %hidden_row.1.refs_0_), channel_id=1, source_target_pairs={{0,224},{32,0},{64,32},{96,64},{128,96},{160,128},{192,160},{224,1... | collective-permute-start | bytes 479240 | tf_op jit(solution)/shard_map/ppermute | solution.py:557
  205.7 13.5 %collective-permute-start.26 = (bf16[96,832]{1,0:T(8,128)(2,1)S(1)}, bf16[96,832]{1,0:T(8,128)(2,1)S(1)}, u32[]{:S(2)}, u32[]{:S(2)}) collective-permute-start(bf16[96,832]{1,0:T(8,128)(2,1)S(1)} %hidden_row.1.refs_0_), channel_id=1, source_target_pairs={{0,96},{32,128},{64,160},{96,192},{128,224},{160,0},{192,32},{224,... | collective-permute-start | bytes 479240 | tf_op jit(solution)/shard_map/ppermute | solution.py:557
  207.4 17.5 %collective-permute-start.28 = (bf16[96,832]{1,0:T(8,128)(2,1)S(1)}, bf16[96,832]{1,0:T(8,128)(2,1)S(1)}, u32[]{:S(2)}, u32[]{:S(2)}) collective-permute-start(bf16[96,832]{1,0:T(8,128)(2,1)S(1)} %collective-permute-done.27.refs_7_), channel_id=1, source_target_pairs={{0,32},{32,64},{64,96},{96,128},{128,160},{160,192},{192,224},{224... | collective-permute-start | bytes 479240 | tf_op jit(solution)/shard_map/ppermute | solution.py:557
  208.6 16.4 %collective-permute-start.25 = (bf16[96,832]{1,0:T(8,128)(2,1)S(1)}, bf16[96,832]{1,0:T(8,128)(2,1)S(1)}, u32[]{:S(2)}, u32[]{:S(2)}) collective-permute-start(bf16[96,832]{1,0:T(8,128)(2,1)S(1)} %collective-permute-done.24.refs_3_), channel_id=1, source_target_pairs={{0,224},{32,0},{64,32},{96,64},{128,96},{160,128},{192,160},{224,1... | collective-permute-start | bytes 479240 | tf_op jit(solution)/shard_map/ppermute | solution.py:557
  219.2 7.3 %collective-permute-start.23 = (bf16[96,832]{1,0:T(8,128)(2,1)S(1)}, bf16[96,832]{1,0:T(8,128)(2,1)S(1)}, u32[]{:S(2)}, u32[]{:S(2)}) collective-permute-start(bf16[96,832]{1,0:T(8,128)(2,1)S(1)} %collective-permute-done.22.refs_1_), channel_id=1, source_target_pairs={{0,224},{32,0},{64,32},{96,64},{128,96},{160,128},{192,160},{224,1... | collective-permute-start | bytes 479240 | tf_op jit(solution)/shard_map/ppermute | solution.py:557
  228.9 6.0 %collective-permute-start.29 = (bf16[16,384,128]{2,1,0:T(8,128)(2,1)S(1)}, bf16[16,384,128]{2,1,0:T(8,128)(2,1)S(1)}, u32[]{:S(2)}, u32[]{:S(2)}) collective-permute-start(bf16[16,384,128]{2,1,0:T(8,128)(2,1)S(1)} %proj_half.7), channel_id=1, source_target_pairs={{0,1},{1,0},{2,3},{3,2},{4,5},{5,4},{6,7},{7,6},{8,9},{9,8},{10,11... | collective-permute-start | bytes 4718600 | tf_op jit(solution)/shard_map/ppermute | solution.py:38
  (26 other events, 443.9 us)
Sparse Core Ops, SparseCore 0:
  157.9 41.2 reduce-scatter.1
